TPU v7x, 32 devices: a whole 2x2x4 slice. The times are simulated.
32 devices in a mesh: dp: 32 (over z, y, x, core).
Axes of the slice: x: 2, y: 2, z: 4, core: 2. Of those that a mesh axis runs over, the one named last changes fastest.
Arguments:
- tokens: bfloat16 [16384, 1024], P('dp'), may hold values from -6 to 6
- segments: int32 [16384], P('dp'), may hold values from 0 to 64, as said below
- norm_gain: bfloat16 [1024], P('dp'), may hold values from 0.25 to 1.75
- q_weight: bfloat16 [1024, 2048], P('dp'), may hold values from -0.1875 to 0.1875
- k_weight: bfloat16 [1024, 1024], P('dp'), may hold values from -0.1875 to 0.1875
- v_weight: bfloat16 [1024, 1024], P('dp'), may hold values from -0.1875 to 0.1875
- o_weight: bfloat16 [1024, 2048], P('dp'), may hold values from -1 to 1
- q_gain: bfloat16 [128], P('dp'), may hold values from 0.25 to 1.75
- k_gain: bfloat16 [128], P('dp'), may hold values from 0.25 to 1.75
- mlp_gain: bfloat16 [1024], P('dp'), may hold values from 0.25 to 1.75
- gate_weight: bfloat16 [1024, 3072], P('dp'), may hold values from -0.1875 to 0.1875
- up_weight: bfloat16 [1024, 3072], P('dp'), may hold values from -0.1875 to 0.1875
- down_weight: bfloat16 [1024, 3072], P('dp'), may hold values from -0.109375 to 0.109375
- cotangent: bfloat16 [16384, 1024], P('dp'), may hold values from -6 to 6
Outputs:
- mixed_out: bfloat16 [16384, 1024], P('dp')
- tokens_grad: bfloat16 [16384, 1024], P('dp')
- norm_gain_grad: float32 [1024], P('dp')
- q_weight_grad: float32 [1024, 2048], P('dp')
- k_weight_grad: float32 [1024, 1024], P('dp')
- v_weight_grad: float32 [1024, 1024], P('dp')
- o_weight_grad: float32 [1024, 2048], P('dp')
- q_gain_grad: float32 [128], P('dp')
- k_gain_grad: float32 [128], P('dp')
- mlp_gain_grad: float32 [1024], P('dp')
- gate_weight_grad: float32 [1024, 3072], P('dp')
- up_weight_grad: float32 [1024, 3072], P('dp')
- down_weight_grad: float32 [1024, 3072], P('dp')
Inputs may be any that keep to these rules, and one draw needn't show every extreme that they name: `segments`: document numbers never fall along the row and rise by one at each new document; every document lies within two consecutive blocks of 512 tokens of the row and starts in the second half of the first of them if it reaches into the next; no document is longer than 512 tokens, and one is exactly that long.
All inputs are finite; a program needn't handle non-finite values.
Results may differ from a plain program's by a relative error of at most 0.015.
Values may be sent and summed in bfloat16 or wider, within the bound.
No kernel may reach another device: no remote copies, remote signals or barrier semaphores. Data moves between devices by JAX's collectives and lax.ppermute only.
A program may use at most 192 MiB of HBM per device.

v0:
```python
import math

import jax
import jax.numpy as jnp
from jax import lax
from jax.sharding import PartitionSpec as P

epsilon = 1e-06
rope_base = 1000000.0


def passed_along(array, axis, by):
    count = lax.axis_size(axis)
    pairs = [(i, i + by) for i in range(count) if 0 <= i + by < count]
    return lax.ppermute(array, axis, pairs)


def inverse_rms(values):
    return lax.rsqrt(jnp.mean(values * values, axis=-1, keepdims=True) + epsilon)


def rotate(values, cosines, sines):
    half_size = values.shape[-1] // 2
    first_half = values[..., :half_size]
    second = values[..., half_size:]
    return jnp.concatenate(
        [first_half * cosines - second * sines, second * cosines + first_half * sines], axis=-1
    )


def norm_back(gradient, normed, scales):
    return scales * (gradient - normed * jnp.mean(gradient * normed, axis=-1, keepdims=True))


def head_forward(projected, gain_values, cosines, sines):
    scales = inverse_rms(projected)
    normed = projected * scales
    return (normed, scales, rotate(normed * gain_values, cosines, sines))


def head_backward(gradient, normed, scales, gain_values, cosines, sines):
    unrotated = rotate(gradient, cosines, -sines)
    gain_grad = jnp.sum(unrotated * normed, axis=(0, 1))
    return (norm_back(unrotated * gain_values, normed, scales), gain_grad)


def contract_rows(left_side, right_side):
    return lax.dot_general(
        left_side, right_side, (((0,), (0,)), ((), ())), preferred_element_type=jnp.float32
    )


def contract_cols(left_side, right_side):
    return lax.dot_general(
        left_side, right_side, (((1,), (1,)), ((), ())), preferred_element_type=jnp.float32
    )


def per_device(
    tokens,
    segments,
    norm_gain,
    q_weight,
    k_weight,
    v_weight,
    o_weight,
    q_gain,
    k_gain,
    mlp_gain,
    gate_weight,
    up_weight,
    down_weight,
    cotangent,
):
    row_count = tokens.shape[0]
    half_rows = row_count // 2
    device = lax.axis_index("dp")
    attn_full = (
        lax.all_gather(norm_gain, "dp", axis=0, tiled=True),
        lax.all_gather(q_weight, "dp", axis=0, tiled=True),
        lax.all_gather(k_weight, "dp", axis=0, tiled=True),
        lax.all_gather(v_weight, "dp", axis=0, tiled=True),
        lax.all_gather(o_weight, "dp", axis=0, tiled=True),
        lax.all_gather(q_gain, "dp", axis=0, tiled=True),
        lax.all_gather(k_gain, "dp", axis=0, tiled=True),
    )
    mlp_full = (
        lax.all_gather(mlp_gain, "dp", axis=0, tiled=True),
        lax.all_gather(gate_weight, "dp", axis=0, tiled=True),
        lax.all_gather(up_weight, "dp", axis=0, tiled=True),
        lax.all_gather(down_weight, "dp", axis=0, tiled=True),
    )
    head_size = attn_full[5].shape[0]
    head_count = attn_full[1].shape[1] // head_size
    kv_count = attn_full[2].shape[1] // head_size
    group_count = head_count // kv_count
    score_scale = head_size ** (-0.5)
    inputs = tokens.astype(jnp.float32)
    gain_one = attn_full[0].astype(jnp.float32)
    scale_one = inverse_rms(inputs)
    normed_one = inputs * scale_one
    attn_in = (normed_one * gain_one).astype(jnp.bfloat16)
    query_proj = jnp.dot(attn_in, attn_full[1], preferred_element_type=jnp.float32).reshape(
        row_count, head_count, head_size
    )
    key_proj = jnp.dot(attn_in, attn_full[2], preferred_element_type=jnp.float32).reshape(
        row_count, kv_count, head_size
    )
    value_proj = jnp.dot(attn_in, attn_full[3], preferred_element_type=jnp.float32).reshape(
        row_count, kv_count, head_size
    )
    before_segments = passed_along(segments[half_rows:], "dp", 1)
    own_place = device * row_count + jnp.arange(row_count, dtype=jnp.int32)
    window_segments = jnp.concatenate([before_segments, segments])
    window_place = jnp.concatenate([own_place[half_rows:] - row_count, own_place])
    counter = jnp.arange(half_rows + row_count, dtype=jnp.int32)
    changes = jnp.concatenate([jnp.ones((1,), bool), window_segments[1:] != window_segments[:-1]])
    changes = changes | (counter == half_rows) & (device == 0)
    starts = lax.cummax(jnp.where(changes, window_place, -3 * row_count), axis=0)
    offsets = (own_place - starts[half_rows:]).astype(jnp.float32)
    frequency = jnp.exp(
        jnp.arange(head_size // 2, dtype=jnp.float32) * (-2.0 * math.log(rope_base) / head_size)
    )
    angles = offsets[:, None] * frequency[None, :]
    cosines = jnp.cos(angles)[:, None, :]
    sines = jnp.sin(angles)[:, None, :]
    q_gain_full = attn_full[5].astype(jnp.float32)
    k_gain_full = attn_full[6].astype(jnp.float32)
    query_normed, query_scale, query_rot = head_forward(query_proj, q_gain_full, cosines, sines)
    key_normed, key_scale, key_rot = head_forward(key_proj, k_gain_full, cosines, sines)
    queries = query_rot.astype(jnp.bfloat16)
    keys_own = key_rot.astype(jnp.bfloat16)
    values_own = value_proj.astype(jnp.bfloat16)
    keys_before, values_before = passed_along(
        (keys_own[half_rows:], values_own[half_rows:]), "dp", 1
    )
    key_window = jnp.concatenate([keys_before, keys_own])
    value_window = jnp.concatenate([values_before, values_own])
    key_valid = (counter >= half_rows) | (device > 0)
    visible = (
        (segments[:, None] == window_segments[None, :])
        & (window_place[None, :] <= own_place[:, None])
        & key_valid[None, :]
    )

    def masked_scores(query_head, key_head):
        raw_scores = (
            jnp.einsum("qgd,cd->gqc", query_head, key_head, preferred_element_type=jnp.float32)
            * score_scale
        )
        return jnp.where(visible[None], raw_scores, -1e30)

    def forward_head(head_items):
        query_head, key_head, value_head = head_items
        raw_scores = masked_scores(query_head, key_head)
        row_max = jnp.max(raw_scores, axis=-1, keepdims=True)
        weights = jnp.exp(raw_scores - row_max)
        row_total = jnp.sum(weights, axis=-1, keepdims=True)
        probs_low = (weights / row_total).astype(jnp.bfloat16)
        mixed_head = jnp.einsum(
            "gqc,cd->qgd", probs_low, value_head, preferred_element_type=jnp.float32
        )
        return (mixed_head, (row_max + jnp.log(row_total))[..., 0])

    query_heads = jnp.moveaxis(queries.reshape(row_count, kv_count, group_count, head_size), 1, 0)
    key_heads = jnp.moveaxis(key_window, 1, 0)
    value_heads = jnp.moveaxis(value_window, 1, 0)
    mixed_heads, log_totals = lax.map(forward_head, (query_heads, key_heads, value_heads))
    attended_low = (
        jnp.moveaxis(mixed_heads, 0, 1)
        .reshape(row_count, head_count * head_size)
        .astype(jnp.bfloat16)
    )
    hidden_state = inputs + contract_cols(attended_low, attn_full[4])
    gain_two = mlp_full[0].astype(jnp.float32)
    scale_two = inverse_rms(hidden_state)
    normed_two = hidden_state * scale_two
    mlp_in = (normed_two * gain_two).astype(jnp.bfloat16)
    gate_proj = jnp.dot(mlp_in, mlp_full[1], preferred_element_type=jnp.float32)
    up_proj = jnp.dot(mlp_in, mlp_full[2], preferred_element_type=jnp.float32)
    sigmoid_gate = jax.nn.sigmoid(gate_proj)
    activated = (gate_proj * sigmoid_gate * up_proj).astype(jnp.bfloat16)
    mixed_out = (hidden_state + contract_cols(activated, mlp_full[3])).astype(jnp.bfloat16)
    out_grad = cotangent.astype(jnp.float32)
    mlp_full = (
        lax.all_gather(mlp_gain, "dp", axis=0, tiled=True),
        lax.all_gather(gate_weight, "dp", axis=0, tiled=True),
        lax.all_gather(up_weight, "dp", axis=0, tiled=True),
        lax.all_gather(down_weight, "dp", axis=0, tiled=True),
    )
    act_grad = jnp.dot(cotangent, mlp_full[3], preferred_element_type=jnp.float32)
    down_grad = contract_rows(cotangent, activated)
    gate_grad = (
        act_grad * up_proj * sigmoid_gate * (1.0 + gate_proj * (1.0 - sigmoid_gate))
    ).astype(jnp.bfloat16)
    up_grad = (act_grad * gate_proj * sigmoid_gate).astype(jnp.bfloat16)
    gate_w_grad = contract_rows(mlp_in, gate_grad)
    up_w_grad = contract_rows(mlp_in, up_grad)
    mlp_in_grad = contract_cols(gate_grad, mlp_full[1]) + contract_cols(up_grad, mlp_full[2])
    gain_two_grad = jnp.sum(mlp_in_grad * normed_two, axis=0)
    hidden_grad = out_grad + norm_back(mlp_in_grad * gain_two, normed_two, scale_two)
    mlp_sums = (
        lax.psum_scatter(gain_two_grad, "dp", scatter_dimension=0, tiled=True),
        lax.psum_scatter(gate_w_grad, "dp", scatter_dimension=0, tiled=True),
        lax.psum_scatter(up_w_grad, "dp", scatter_dimension=0, tiled=True),
        lax.psum_scatter(down_grad, "dp", scatter_dimension=0, tiled=True),
    )
    attn_full = (
        lax.all_gather(norm_gain, "dp", axis=0, tiled=True),
        lax.all_gather(q_weight, "dp", axis=0, tiled=True),
        lax.all_gather(k_weight, "dp", axis=0, tiled=True),
        lax.all_gather(v_weight, "dp", axis=0, tiled=True),
        lax.all_gather(o_weight, "dp", axis=0, tiled=True),
        lax.all_gather(q_gain, "dp", axis=0, tiled=True),
        lax.all_gather(k_gain, "dp", axis=0, tiled=True),
    )
    branch_low = hidden_grad.astype(jnp.bfloat16)
    o_w_grad = contract_rows(branch_low, attended_low)
    attended_grad = jnp.dot(branch_low, attn_full[4], preferred_element_type=jnp.float32).astype(
        jnp.bfloat16
    )
    grad_heads = jnp.moveaxis(
        attended_grad.reshape(row_count, kv_count, group_count, head_size), 1, 0
    )

    def backward_head(head_items):
        query_head, key_head, value_head, grad_head, log_total = head_items
        softmax = jnp.exp(masked_scores(query_head, key_head) - log_total[..., None])
        probs_low = softmax.astype(jnp.bfloat16)
        prob_grad = jnp.einsum(
            "qgd,cd->gqc", grad_head, value_head, preferred_element_type=jnp.float32
        )
        value_grad = jnp.einsum(
            "gqc,qgd->cd", probs_low, grad_head, preferred_element_type=jnp.float32
        )
        score_grad = softmax * (prob_grad - jnp.sum(softmax * prob_grad, axis=-1, keepdims=True))
        score_low = score_grad.astype(jnp.bfloat16)
        query_grad = (
            jnp.einsum("gqc,cd->qgd", score_low, key_head, preferred_element_type=jnp.float32)
            * score_scale
        )
        key_grad = (
            jnp.einsum("gqc,qgd->cd", score_low, query_head, preferred_element_type=jnp.float32)
            * score_scale
        )
        return (query_grad, key_grad, value_grad)

    query_heads_grad, key_heads_grad, value_heads_grad = lax.map(
        backward_head, (query_heads, key_heads, value_heads, grad_heads, log_totals)
    )
    query_grad = jnp.moveaxis(query_heads_grad, 0, 1).reshape(row_count, head_count, head_size)
    keys_grad = jnp.moveaxis(key_heads_grad, 0, 1)
    values_grad = jnp.moveaxis(value_heads_grad, 0, 1)
    keys_later, values_later = (
        passed_along(keys_grad[:half_rows].astype(jnp.bfloat16), "dp", -1).astype(jnp.float32),
        passed_along(values_grad[:half_rows].astype(jnp.bfloat16), "dp", -1).astype(jnp.float32),
    )
    padding = jnp.zeros((row_count - half_rows, kv_count, head_size), jnp.float32)
    key_total = keys_grad[half_rows:] + jnp.concatenate([padding, keys_later])
    value_total = values_grad[half_rows:] + jnp.concatenate([padding, values_later])
    value_low = value_total.reshape(row_count, kv_count * head_size).astype(jnp.bfloat16)
    query_back, q_gain_grad = head_backward(
        query_grad, query_normed, query_scale, q_gain_full, cosines, sines
    )
    key_back, k_gain_grad = head_backward(
        key_total, key_normed, key_scale, k_gain_full, cosines, sines
    )
    query_low = query_back.reshape(row_count, head_count * head_size).astype(jnp.bfloat16)
    key_low = key_back.reshape(row_count, kv_count * head_size).astype(jnp.bfloat16)
    q_w_grad = contract_rows(attn_in, query_low)
    k_w_grad = contract_rows(attn_in, key_low)
    v_w_grad = contract_rows(attn_in, value_low)
    attn_in_grad = (
        contract_cols(query_low, attn_full[1])
        + contract_cols(key_low, attn_full[2])
        + contract_cols(value_low, attn_full[3])
    )
    gain_one_grad = jnp.sum(attn_in_grad * normed_one, axis=0)
    input_grad = hidden_grad + norm_back(attn_in_grad * gain_one, normed_one, scale_one)
    attn_sums = (
        lax.psum_scatter(gain_one_grad, "dp", scatter_dimension=0, tiled=True),
        lax.psum_scatter(q_w_grad, "dp", scatter_dimension=0, tiled=True),
        lax.psum_scatter(k_w_grad, "dp", scatter_dimension=0, tiled=True),
        lax.psum_scatter(v_w_grad, "dp", scatter_dimension=0, tiled=True),
        lax.psum_scatter(o_w_grad, "dp", scatter_dimension=0, tiled=True),
        lax.psum_scatter(q_gain_grad, "dp", scatter_dimension=0, tiled=True),
        lax.psum_scatter(k_gain_grad, "dp", scatter_dimension=0, tiled=True),
    )
    return (
        mixed_out,
        input_grad.astype(jnp.bfloat16),
        attn_sums[0],
        attn_sums[1],
        attn_sums[2],
        attn_sums[3],
        attn_sums[4],
        attn_sums[5],
        attn_sums[6],
        mlp_sums[0],
        mlp_sums[1],
        mlp_sums[2],
        mlp_sums[3],
    )


def solution(mesh):
    placed = (
        P("dp", None),
        P("dp"),
        P("dp"),
        P("dp", None),
        P("dp", None),
        P("dp", None),
        P("dp", None),
        P("dp"),
        P("dp"),
        P("dp"),
        P("dp", None),
        P("dp", None),
        P("dp", None),
        P("dp", None),
    )
    return jax.shard_map(
        per_device,
        mesh=mesh,
        in_specs=placed,
        out_specs=(
            P("dp", None),
            P("dp", None),
            P("dp"),
            P("dp", None),
            P("dp", None),
            P("dp", None),
            P("dp", None),
            P("dp"),
            P("dp"),
            P("dp"),
            P("dp", None),
            P("dp", None),
            P("dp", None),
        ),
        check_vma=False,
    )
```

profile of v0, /device:TPU:0, one launch (start us, length us, event | category | flops | bytes accessed | tf_op | source)
XLA Modules:
  0.0 1688.0 jit_solution(8312626905563416366)
XLA Ops:
  17.2 41.9 %all-reduce.11 = (bf16[1024]{0:T(1024)(128)(2,1)S(1)}, bf16[128]{0:T(256)(128)(2,1)S(1)}, bf16[128]{0:T(256)(128)(2,1)S(1)}, bf16[1024]{0:T(1024)(128)(2,1)S(1)}) all-reduce(bf16[1024]{0:T(1024)(128)(2,1)S(1)} %dynamic-update-slice, bf16[128]{0:T(256)(128)(2,1)S(1)} %dynamic-update-slice.1, ...), channel_id=1, replica_groups=mesh['dp'=32] {'dp'}, use_global_device_ids=true, to_apply=%add.2 | all-reduce | flops 2304 | bytes 9216
  61.8 8.3 all-gather.10.cloned.1.call-done
  78.7 3.0 collective-permute-start.2
  81.7 46.7 %all-gather.8.cloned.1.call-done = bf16[1024,1024]{1,0:T(8,128)(2,1)} async-done(((bf16[32,1024]{1,0:T(8,128)(2,1)}), bf16[1024,1024]{1,0:T(8,128)(2,1)}) %all-gather.8.cloned.1.call-update) | async-done | bytes 2097168 | tf_op jit(solution)/shard_map/all_gather | solution.py:82
  134.3 2.9 maximum_bitcast_fusion.2
  138.5 53.6 %all-gather.12.cloned.1.call-done = bf16[1024,2048]{1,0:T(8,128)(2,1)} async-done(((bf16[32,2048]{1,0:T(8,128)(2,1)}), bf16[1024,2048]{1,0:T(8,128)(2,1)}) %all-gather.12.cloned.1.call-update) | async-done | bytes 4194320 | tf_op jit(solution)/shard_map/all_gather | solution.py:80
  192.1 4.6 fusion.95
  207.2 48.1 %while.30 = (s32[]{:T(128)}, bf16[8,512,2,128]{1,3,2,0:T(8,128)(2,1)}, f32[8,2,512]{2,1,0:T(2,128)S(1)}, bf16[8,768,128]{2,1,0:T(8,128)(2,1)}, bf16[8,768,128]{2...) while((s32[]{:T(128)}, ...), condition=%wide.region_8.9_spmd.clone.clone, body=%wide.region_5.8_spmd.clone.sunk.clone | while | flops 413662208 | bytes 12235633 | solution.py:168
  255.3 5.3 multiply_reduce_fusion.5
  263.2 63.1 %all-gather.16.cloned.1.call-done = bf16[1024,3072]{1,0:T(8,128)(2,1)} async-done(((bf16[32,3072]{1,0:T(8,128)(2,1)}), bf16[1024,3072]{1,0:T(8,128)(2,1)}) %all-gather.16.cloned.1.call-update) | async-done | bytes 6291472 | tf_op jit(solution)/shard_map/all_gather | solution.py:89
  326.2 9.1 fusion.101
  335.4 61.6 %all-gather.18.cloned.1.call-done = bf16[1024,3072]{1,0:T(8,128)(2,1)} async-done(((bf16[32,3072]{1,0:T(8,128)(2,1)}), bf16[1024,3072]{1,0:T(8,128)(2,1)}) %all-gather.18.cloned.1.call-update) | async-done | bytes 6291472 | tf_op jit(solution)/shard_map/all_gather | solution.py:90
  397.0 9.2 fusion.102
  406.2 61.7 %all-gather.20.cloned.1.call-done = bf16[1024,3072]{1,0:T(8,128)(2,1)} async-done(((bf16[32,3072]{1,0:T(8,128)(2,1)}), bf16[1024,3072]{1,0:T(8,128)(2,1)}) %all-gather.20.cloned.1.call-update) | async-done | bytes 6291472 | tf_op jit(solution)/shard_map/all_gather | solution.py:91
  467.9 11.8 multiply_convert_fusion
  479.7 8.1 fusion.103
  487.9 4.3 multiply_reduce_fusion.2
  495.1 3.7 convolution_convert_fusion
  498.8 4.5 reshape.263
  503.3 3.4 copy.188
  506.7 89.2 %while.31 = (s32[]{:T(128)}, f32[8,512,2,128]{1,3,2,0:T(8,128)}, f32[8,768,128]{2,1,0:T(8,128)}, f32[8,768,128]{1,2,0:T(8,128)}, bf16[8,768,128]{2,1,0:T(8,128)(...) while((s32[]{:T(128)}, f32[8,512,2,128]{1,3,2,0:T(8,128)}, ...), condition=%wide.region_13.14_spmd.clone.clone, body=%wide.region_11.13_spmd.clone.sunk.clone | while | flops 1015512064 | bytes 27365256 | solution.py:248
  604.4 3.3 fusion.80
  613.3 3.5 fusion.91
  619.5 9.0 collective-permute-done.4
  631.4 3.4 fusion.89
  635.5 4.4 fusion.100
  639.9 5.0 copy.142
  644.9 3.8 copy.143
  648.8 4.5 multiply_subtract_fusion
  653.5 3.7 multiply_reduce_fusion
  660.5 7.3 fusion.61
  669.3 5.7 fusion.93
  676.3 8.5 fusion.106
  684.8 8.3 fusion.107
  694.6 7.2 fusion.81
  701.9 10.1 convolution_bitcast_fusion.1
  712.0 12.9 copy.137
  725.0 5.3 fusion.104
  730.4 7.6 add_convert_fusion.1
  740.0 3.2 fusion.72
  743.1 52.3 %all-reduce.10 = (f32[1024]{0:T(1024)S(1)}, f32[128]{0:T(128)S(1)}, f32[128]{0:T(128)S(1)}, f32[1024]{0:T(1024)S(1)}) all-reduce(f32[1024]{0:T(1024)S(1)} %get-tuple-element.320, f32[128]{0:T(128)S(1)} %bitcast_reduce_fusion, f32[128]{0:T(128)S(1)} %bitcast_reduce_fusion.1, ...), channel_id=2, replica_groups=mesh['dp'=32] {'dp'}, use_global_device_ids=true, to_apply=%region_18.19.clone | all-reduce | flops 2304 | bytes 18432
  797.8 3.1 fusion.71
  800.9 104.1 %reduce-scatter.14.cloned.1.call-done = f32[32,1024]{1,0:T(8,128)} async-done(((f32[1024,1024]{1,0:T(8,128)}), f32[32,1024]{1,0:T(8,128)}) %reduce-scatter.14.cloned.1.call-update) | async-done | bytes 131088 | tf_op jit(solution)/shard_map/reduce_scatter | solution.py:284
  905.0 147.5 %reduce-scatter.10.cloned.1.call-done = f32[32,2048]{1,0:T(8,128)} async-done(((f32[1024,2048]{1,0:T(8,128)}), f32[32,2048]{1,0:T(8,128)}) %reduce-scatter.10.cloned.1.call-update) | async-done | bytes 262160 | tf_op jit(solution)/shard_map/reduce_scatter | solution.py:282
  1052.5 157.9 %reduce-scatter.18.cloned.1.call-done = f32[32,3072]{1,0:T(8,128)} async-done(((f32[1024,3072]{1,0:T(8,128)}), f32[32,3072]{1,0:T(8,128)}) %reduce-scatter.18.cloned.1.call-update) | async-done | bytes 393232 | tf_op jit(solution)/shard_map/reduce_scatter | solution.py:204
  1210.4 162.0 %reduce-scatter.20.cloned.1.call-done = f32[32,3072]{1,0:T(8,128)} async-done(((f32[1024,3072]{1,0:T(8,128)}), f32[32,3072]{1,0:T(8,128)}) %reduce-scatter.20.cloned.1.call-update) | async-done | bytes 393232 | tf_op jit(solution)/shard_map/reduce_scatter | solution.py:205
  1372.4 150.9 %reduce-scatter.16.cloned.1.call-done = f32[32,2048]{1,0:T(8,128)} async-done(((f32[1024,2048]{1,0:T(8,128)}), f32[32,2048]{1,0:T(8,128)}) %reduce-scatter.16.cloned.1.call-update) | async-done | bytes 262160 | tf_op jit(solution)/shard_map/reduce_scatter | solution.py:285
  1523.3 157.8 %reduce-scatter.22.cloned.1.call-done = f32[32,3072]{1,0:T(8,128)} async-done(((f32[1024,3072]{1,0:T(8,128)}), f32[32,3072]{1,0:T(8,128)}) %reduce-scatter.22.cloned.1.call-update) | async-done | bytes 393232
  (317 shorter events, 213.2 us)
Async XLA Ops:
  7.2 8.7 copy-start.6
  7.2 9.1 copy-start.38
  7.2 9.3 copy-start.39
  7.2 9.5 copy-start.40
  7.2 9.8 copy-start.41
  7.2 62.9 %all-gather.10.cloned.1.call-start = ((), (), s32[]{:S(2)}) async-start(), calls=%async_computation.8 | async-start | bytes 2162688 | tf_op jit(solution)/shard_map/all_gather | solution.py:81
  8.0 51.2 %copy-start.27 = (s32[512]{0:T(512)S(1)}, s32[512]{0:T(512)}, u32[]{:S(2)}) copy-start(s32[512]{0:T(512)} %param.19) | copy-start | bytes 6148
  8.0 120.4 %all-gather.8.cloned.1.call-start = ((), (), s32[]{:S(2)}) async-start(), calls=%async_computation.7 | async-start | bytes 2162688 | tf_op jit(solution)/shard_map/all_gather | solution.py:82
  8.7 183.4 %all-gather.12.cloned.1.call-start = ((), (), s32[]{:S(2)}) async-start(), calls=%async_computation.9 | async-start | bytes 4325376 | tf_op jit(solution)/shard_map/all_gather | solution.py:80
  9.5 245.9 %all-gather.14.cloned.1.call-start = ((), (), s32[]{:S(2)}) async-start(), calls=%async_computation.10 | async-start | bytes 4325376 | tf_op jit(solution)/shard_map/all_gather | solution.py:83
  10.0 316.2 %all-gather.16.cloned.1.call-start = ((), (), s32[]{:S(2)}) async-start(), calls=%async_computation.11 | async-start | bytes 6488064 | tf_op jit(solution)/shard_map/all_gather | solution.py:89
  10.6 386.4 %all-gather.18.cloned.1.call-start = ((), (), s32[]{:S(2)}) async-start(), calls=%async_computation.12 | async-start | bytes 6488064 | tf_op jit(solution)/shard_map/all_gather | solution.py:90
  11.2 456.7 %all-gather.20.cloned.1.call-start = ((), (), s32[]{:S(2)}) async-start(), calls=%async_computation.13 | async-start | bytes 6488064 | tf_op jit(solution)/shard_map/all_gather | solution.py:91
  11.9 47.2 %collective-permute-start.1 = (s32[256]{0:T(256)S(1)}, s32[256]{0:T(256)S(1)}, u32[]{:S(2)}, u32[]{:S(2)}) collective-permute-start(s32[256]{0:T(256)S(1)} %slice.74), channel_id=1, source_target_pairs={{0,1},{1,2},{2,3},{3,4},{4,5},{5,6},{6,7},{7,8},{8,9},{9,10},{10,1... | collective-permute-start | bytes 3080 | tf_op jit(solution)/shard_map/ppermute | solution.py:15
  14.3 786.6 %reduce-scatter.12.cloned.1.call-start = ((), (), s32[]{:S(2)}) async-start(), calls=%async_computation.15 | async-start | bytes 4325376 | tf_op jit(solution)/shard_map/reduce_scatter | solution.py:283
  59.1 140.8 %copy-start.30 = (f32[128]{0:T(128)}, f32[128]{0:T(128)S(1)}, u32[]{:S(2)}) copy-start(f32[128]{0:T(128)S(1)} %convert_element_type.102) | copy-start | bytes 1540
  59.1 16.7 copy-start.32
  73.0 2.9 copy-start.2
  78.7 55.6 %collective-permute-start.2 = (bf16[256,8,128]{2,0,1:T(8,128)(2,1)}, bf16[256,8,128]{2,0,1:T(8,128)(2,1)}, u32[]{:S(2)}, u32[]{:S(2)}) collective-permute-start(bf16[256,8,128]{2,0,1:T(8,128)(2,1)} %pad_maximum_fusion.2), channel_id=1, source_target_pairs={{0,1},{1,2},{2,3},{3,4},{4,5},{5,6},{6,7},{7,8},{8,9},{9,10},{10,1... | collective-permute-start | bytes 1572872 | tf_op jit(solution)/shard_map/ppermute | solution.py:15
  131.4 5.8 collective-permute-start
  196.7 2.0 copy-start.7
  201.3 2.0 copy-start.21
  479.7 8.1 copy-start.43
  479.7 8.1 copy-start.42
  479.7 8.1 copy-start.10
  479.7 8.1 copy-start.35
  487.9 4.3 copy-start.26
  492.2 2.9 copy-start.36
  506.7 91.8 %copy-start.33 = (f32[128]{0:T(128)S(1)}, f32[128]{0:T(128)}, u32[]{:S(2)}) copy-start(f32[128]{0:T(128)} %copy-done.32) | copy-start | bytes 1540
  506.7 91.9 %copy-start.29 = (f32[512,8]{0,1:T(8,128)S(1)}, f32[512,8]{0,1:T(8,128)}, u32[]{:S(2)}) copy-start(f32[512,8]{0,1:T(8,128)} %copy-done.28) | copy-start | bytes 49156
  597.2 3.8 collective-permute-start.3
  599.4 3.4 copy-start.19
  608.5 2.3 copy-start.12
  616.9 288.1 %reduce-scatter.14.cloned.1.call-start = ((), (), s32[]{:S(2)}) async-start(), calls=%async_computation.16 | async-start | bytes 4325376 | tf_op jit(solution)/shard_map/reduce_scatter | solution.py:284
  618.2 10.3 collective-permute-start.4
  634.9 417.6 %reduce-scatter.10.cloned.1.call-start = ((), (), s32[]{:S(2)}) async-start(), calls=%async_computation.14 | async-start | bytes 8650752 | tf_op jit(solution)/shard_map/reduce_scatter | solution.py:282
  648.8 4.7 copy-start.1
  648.8 4.7 copy-start.14
  658.3 2.2 copy-start.8
  675.1 535.4 %reduce-scatter.18.cloned.1.call-start = ((), (), s32[]{:S(2)}) async-start(), calls=%async_computation.18 | async-start | bytes 12976128 | tf_op jit(solution)/shard_map/reduce_scatter | solution.py:204
  684.7 687.6 %reduce-scatter.20.cloned.1.call-start = ((), (), s32[]{:S(2)}) async-start(), calls=%async_computation.19 | async-start | bytes 12976128 | tf_op jit(solution)/shard_map/reduce_scatter | solution.py:205
  693.1 830.2 %reduce-scatter.16.cloned.1.call-start = ((), (), s32[]{:S(2)}) async-start(), calls=%async_computation.17 | async-start | bytes 8650752 | tf_op jit(solution)/shard_map/reduce_scatter | solution.py:285
  701.9 979.2 %reduce-scatter.22.cloned.1.call-start = ((), (), s32[]{:S(2)}) async-start(), calls=%async_computation.20 | async-start | bytes 12976128
  725.0 5.4 copy-start.11
  725.0 5.4 copy-start.44
  730.4 7.6 copy-start.16
  730.4 7.6 copy-start.37
  740.0 3.2 copy-start.34
  (16 other events, 20.6 us)
Sparse Core Ops, SparseCore 0:
  10.9 59.1 all-gather.9
  73.0 55.3 all-gather.7
  131.3 60.7 all-gather.11
  194.8 60.4 all-gather.13
  258.0 68.1 all-gather.15
  328.9 68.0 all-gather.17
  399.9 67.9 all-gather.19
  617.0 148.1 reduce-scatter.11
  768.0 136.9 reduce-scatter.13
  907.7 144.7 reduce-scatter.9
  1059.1 151.2 reduce-scatter.17
  1217.9 154.4 reduce-scatter.19
  1375.2 147.9 reduce-scatter.15
  1529.7 151.2 reduce-scatter.21
where the time goes:
time: 1700 us; the launch traced here: 1690 us
  waiting for transfers between devices  1190 us (70%)
  matrix products  238 us (14%)
  blocking collectives  94.2 us (6%)
  other arithmetic  72.8 us (4%)
  local copies, waits for them, and re-layouts  66.7 us (4%)
    reduce_scatter x1, waiting for transfers between devices, per_device(): lax.psum_scatter(up_w_grad, 'dp', scatter_dimension=0, tiled=True)  162 us
    unnamed x15, waiting for transfers between devices  162 us
    reduce_scatter x1, waiting for transfers between devices, per_device(): lax.psum_scatter(gate_w_grad, 'dp', scatter_dimension=0, tiled=True)  158 us
    reduce_scatter x1, waiting for transfers between devices, per_device(): lax.psum_scatter(o_w_grad, 'dp', scatter_dimension=0, tiled=True)  151 us
    reduce_scatter x1, waiting for transfers between devices, per_device(): lax.psum_scatter(q_w_grad, 'dp', scatter_dimension=0, tiled=True)  148 us
    reduce_scatter x1, waiting for transfers between devices, per_device(): lax.psum_scatter(v_w_grad, 'dp', scatter_dimension=0, tiled=True)  104 us
    unnamed x2, blocking collectives  94.2 us
    all_gather x1, waiting for transfers between devices, per_device(): lax.all_gather(gate_weight, 'dp', axis=0, tiled=True)  63.1 us
  transfers between devices with their start and end apart: 19, of which 14 were waited for; matrix products, arithmetic and copies ran while one was open for 13% of the time, Pallas kernels for 0%

commit v1 on v0

v1 whole, which is shorter than its diff:
```python
import functools
import math

import jax
import jax.numpy as jnp
from jax import lax
from jax.experimental import pallas as pl
from jax.experimental.pallas import tpu as pltpu
from jax.sharding import PartitionSpec as P

epsilon = 1e-06
rope_base = 1000000.0
low = jnp.bfloat16
full = jnp.float32
vmem_limit = 48 * 1024 * 1024
barrier = lax.optimization_barrier


def dot(left_side, right_side, left_dim=1, right_dim=0, kind=full):
    return lax.dot_general(
        left_side,
        right_side,
        (((left_dim,), (right_dim,)), ((), ())),
        preferred_element_type=kind,
    )


def inverse_rms(values):
    return lax.rsqrt(jnp.mean(values * values, axis=-1, keepdims=True) + epsilon)


def rotate(values, cosines, sines):
    half_size = values.shape[-1] // 2
    first_half = values[..., :half_size]
    second = values[..., half_size:]
    return jnp.concatenate(
        [first_half * cosines - second * sines, second * cosines + first_half * sines], axis=-1
    )


def norm_back(gradient, normed, scales):
    return scales * (gradient - normed * jnp.mean(gradient * normed, axis=-1, keepdims=True))


class Slice:
    def __init__(self):
        self.count = lax.axis_size("dp")
        self.chips = self.count // 2
        self.side = 1
        while 4 * self.side * self.side < self.chips:
            self.side *= 2
        self.device = lax.axis_index("dp")
        self.core = self.device % 2
        self.chip = self.device // 2

    def flip(self, array, mask):
        return lax.ppermute(array, "dp", [(i, i ^ mask) for i in range(self.count)])

    def ring(self, array, by):
        step = 2 * self.side * self.side * by
        return lax.ppermute(
            array, "dp", [(i, (i + step) % self.count) for i in range(self.count)]
        )

    def chip_along(self, array, by):
        pairs = [(i, i + 2 * by) for i in range(self.count) if 0 <= i + 2 * by < self.count]
        return lax.ppermute(array, "dp", pairs)

    def pair(self, array):
        return self.flip(array, 1)

    def by_core(self, mine, other, axis=0):
        return jnp.where(
            self.core == 0,
            jnp.concatenate([mine, other], axis=axis),
            jnp.concatenate([other, mine], axis=axis),
        )

    def halves(self, array, axis=0):
        size = array.shape[axis] // 2
        mine = lax.dynamic_slice_in_dim(array, self.core * size, size, axis)
        other = lax.dynamic_slice_in_dim(array, (1 - self.core) * size, size, axis)
        return mine, other

    def mask_of(self, name, amount):
        return 2 * amount * (1 if name == "x" else self.side)

    def places(self, chip, unit):
        side = self.side
        entry = jnp.arange(self.chips * unit, dtype=jnp.int32)
        inner, block = entry % unit, entry // unit
        along_z, along_x, along_y = block % 4, block // 4 % side, block // (4 * side)
        own_x, own_y, own_z = chip % side, chip // side % side, chip // (side * side)
        source = (
            ((own_z - along_z + 4) % 4) * side * side + (own_y ^ along_y) * side + (own_x ^ along_x)
        )
        return source * unit + inner

    def gather_z(self, block):
        blocks = [block]
        for _ in range(3):
            blocks.append(self.ring(blocks[-1], 1))
        return blocks

    def gather_plane_first(self, block, name):
        return [block] + [
            self.flip(block, self.mask_of(name, m)) for m in range(1, self.side)
        ]

    def gather_plane_second(self, pieces, name):
        side = self.side
        rows = [pieces]
        for m in range(1, side):
            rows.append([self.flip(piece, self.mask_of(name, m)) for piece in pieces])
        if name == "y":
            return [rows[y][x] for y in range(side) for x in range(side)]
        return [rows[x][y] for y in range(side) for x in range(side)]

    def scatter(self, array, first):
        side = self.side
        pieces = jnp.split(array, side * side)
        current = {(y, x): pieces[y * side + x] for y in range(side) for x in range(side)}
        for name in (first, "y" if first == "x" else "x"):
            at = 1 if name == "x" else 0
            kept = {}
            for key in [key for key in current if key[at] == 0]:
                total = current[key].astype(full)
                for m in range(1, side):
                    sent = (key[0], m) if name == "x" else (m, key[1])
                    total = total + self.flip(current[sent], self.mask_of(name, m)).astype(full)
                kept[key] = total.astype(array.dtype)
            current = kept
        blocks = jnp.split(current[(0, 0)], 4)
        total = blocks[0].astype(full)
        for m in range(1, 4):
            total = total + self.ring(blocks[m], -m).astype(full)
        return total

    def finish(self, total):
        mine, other = self.halves(total)
        return self.by_core(mine, self.pair(other), axis=1)


def score_bias(query_segments, key_segments, rows, halo):
    key_count, query_count = key_segments.shape[0], query_segments.shape[1]
    key_place = lax.broadcasted_iota(jnp.int32, (key_count, query_count), 0) - halo
    query_place = lax.broadcasted_iota(jnp.int32, (key_count, query_count), 1)
    seen = (key_segments == query_segments) & (key_place <= query_place)
    return jnp.where(seen, 0.0, -1e30).astype(full)


def parts_of(rows, halo):
    return (((0, halo), 2 * halo), ((halo, rows), halo + rows))


def forward_kernel(scale, rows, halo, q_ref, k_ref, v_ref, qs_ref, ks_ref, out_ref, bias_ref):
    block = pl.program_id(1)
    start = pl.multiple_of(block * rows, rows)
    window = halo + rows
    head_size = k_ref.shape[1]

    @pl.when(pl.program_id(0) == 0)
    def _():
        bias_ref[block] = score_bias(
            qs_ref[...], ks_ref[pl.ds(start, window), :], rows, halo
        )

    for (low_row, high_row), key_count in parts_of(rows, halo):
        keys = k_ref[pl.ds(start, key_count), :]
        values = v_ref[pl.ds(start, key_count), :]
        bias = bias_ref[block, :key_count, low_row:high_row]
        for group in range(q_ref.shape[1] // head_size):
            lanes = slice(group * head_size, (group + 1) * head_size)
            query = q_ref[low_row:high_row, lanes]
            scores = dot(keys, query, 1, 1) * scale + bias
            weights = jnp.exp2(scores)
            total = jnp.sum(weights, axis=0, keepdims=True)
            probs = (weights * (1.0 / total)).astype(low)
            mixed = dot(values, probs, 0, 0)
            out_ref[low_row:high_row, lanes] = mixed.T.astype(low)


def backward_kernel(
    scale, rows, halo, q_ref, k_ref, v_ref, g_ref, qs_ref, ks_ref, dq_ref, dk_ref, dv_ref, bias_ref
):
    block = pl.program_id(1)
    start = pl.multiple_of(block * rows, rows)
    window = halo + rows
    head_size = k_ref.shape[1]
    factor = head_size ** (-0.5)

    @pl.when(pl.program_id(0) == 0)
    def _():
        bias_ref[block] = score_bias(
            qs_ref[...], ks_ref[pl.ds(start, window), :], rows, halo
        )

    @pl.when(block == 0)
    def _():
        dk_ref[...] = jnp.zeros_like(dk_ref)
        dv_ref[...] = jnp.zeros_like(dv_ref)

    for (low_row, high_row), key_count in parts_of(rows, halo):
        keys = k_ref[pl.ds(start, key_count), :]
        values = v_ref[pl.ds(start, key_count), :]
        bias = bias_ref[block, :key_count, low_row:high_row]
        key_sum = None
        value_sum = None
        for group in range(q_ref.shape[1] // head_size):
            lanes = slice(group * head_size, (group + 1) * head_size)
            query = q_ref[low_row:high_row, lanes]
            grad = g_ref[low_row:high_row, lanes]
            weights = jnp.exp2(dot(keys, query, 1, 1) * scale + bias)
            total = jnp.sum(weights, axis=0, keepdims=True)
            softmax = weights * (1.0 / total)
            prob_grad = dot(values, grad, 1, 1)
            product = softmax * prob_grad
            mean = jnp.sum(product, axis=0, keepdims=True)
            score_grad = (product - softmax * mean).astype(low)
            value_term = dot(softmax.astype(low), grad)
            key_term = dot(score_grad, query)
            value_sum = value_term if value_sum is None else value_sum + value_term
            key_sum = key_term if key_sum is None else key_sum + key_term
            dq_ref[low_row:high_row, lanes] = dot(keys, score_grad, 0, 0).T * factor
        dk_ref[pl.ds(start, key_count), :] += key_sum * factor
        dv_ref[pl.ds(start, key_count), :] += value_sum


def attention_specs(rows, halo, token_count, group_lanes, head_size):
    queries = pl.BlockSpec((rows, group_lanes), lambda h, b: (b, h))
    keys = pl.BlockSpec((halo + token_count, head_size), lambda h, b: (0, h))
    query_segments = pl.BlockSpec((1, rows), lambda h, b: (0, b))
    key_segments = pl.BlockSpec((halo + token_count, 1), lambda h, b: (0, 0))
    return queries, keys, query_segments, key_segments


def attention_forward(queries, keys, values, query_segments, key_segments, rows, halo, head_size):
    token_count = queries.shape[0]
    heads = keys.shape[1] // head_size
    q_spec, k_spec, qs_spec, ks_spec = attention_specs(
        rows, halo, token_count, queries.shape[1] // heads, head_size
    )
    scale = head_size ** (-0.5) / math.log(2.0)
    return pl.pallas_call(
        functools.partial(forward_kernel, scale, rows, halo),
        grid=(heads, token_count // rows),
        in_specs=[q_spec, k_spec, k_spec, qs_spec, ks_spec],
        out_specs=q_spec,
        out_shape=jax.ShapeDtypeStruct(queries.shape, low),
        scratch_shapes=[pltpu.VMEM((token_count // rows, halo + rows, rows), full)],
        compiler_params=pltpu.CompilerParams(vmem_limit_bytes=vmem_limit),
        cost_estimate=pl.CostEstimate(
            flops=4 * queries.size * (halo + rows),
            bytes_accessed=2 * (2 * queries.size + 2 * keys.size),
            transcendentals=queries.size // head_size * (halo + rows),
        ),
        name="attention_forward",
    )(queries, keys, values, query_segments, key_segments)


def attention_backward(
    queries, keys, values, grads, query_segments, key_segments, rows, halo, head_size
):
    token_count = queries.shape[0]
    heads = keys.shape[1] // head_size
    q_spec, k_spec, qs_spec, ks_spec = attention_specs(
        rows, halo, token_count, queries.shape[1] // heads, head_size
    )
    scale = head_size ** (-0.5) / math.log(2.0)
    return pl.pallas_call(
        functools.partial(backward_kernel, scale, rows, halo),
        grid=(heads, token_count // rows),
        in_specs=[q_spec, k_spec, k_spec, q_spec, qs_spec, ks_spec],
        out_specs=[q_spec, k_spec, k_spec],
        out_shape=[
            jax.ShapeDtypeStruct(queries.shape, full),
            jax.ShapeDtypeStruct(keys.shape, full),
            jax.ShapeDtypeStruct(keys.shape, full),
        ],
        scratch_shapes=[pltpu.VMEM((token_count // rows, halo + rows, rows), full)],
        compiler_params=pltpu.CompilerParams(vmem_limit_bytes=vmem_limit),
        cost_estimate=pl.CostEstimate(
            flops=10 * queries.size * (halo + rows),
            bytes_accessed=8 * queries.size + 12 * keys.size,
            transcendentals=queries.size // head_size * (halo + rows),
        ),
        name="attention_backward",
    )(queries, keys, values, grads, query_segments, key_segments)


def per_device(
    tokens,
    segments,
    norm_gain,
    q_weight,
    k_weight,
    v_weight,
    o_weight,
    q_gain,
    k_gain,
    mlp_gain,
    gate_weight,
    up_weight,
    down_weight,
    cotangent,
):
    net = Slice()
    row_count, width = tokens.shape
    halo = row_count // 2
    chip_rows = 2 * row_count
    weight_rows = q_weight.shape[0]
    head_size = q_gain.shape[0] * net.count
    gain_rows = q_gain.shape[0]

    def column_block(weight):
        mine, other = net.halves(weight, axis=1)
        return mine, other

    def extra_column(gain):
        return jnp.pad(gain[:, None], ((0, weight_rows - gain.shape[0]), (0, 0)))

    extras = jnp.concatenate(
        [extra_column(gain) for gain in (norm_gain, mlp_gain, q_gain, k_gain)]
        + [jnp.zeros((weight_rows, 124), low)],
        axis=1,
    )
    q_mine, q_other = net.halves(q_weight, 1)
    k_mine, k_other = net.halves(k_weight, 1)
    v_mine, v_other = net.halves(v_weight, 1)
    o_mine, o_other = net.halves(o_weight, 1)
    gate_mine, gate_other = net.halves(gate_weight, 1)
    up_mine, up_other = net.halves(up_weight, 1)
    down_mine, down_other = net.halves(down_weight, 1)

    def chip_block(mine, other):
        return net.by_core(jnp.concatenate(mine, 1), net.pair(jnp.concatenate(other, 1)))

    first_block = chip_block(
        [q_mine, extras, k_mine, v_mine], [q_other, extras, k_other, v_other]
    )
    q_cols = q_mine.shape[1]
    k_cols = k_mine.shape[1]
    o_cols = o_mine.shape[1]
    ff_cols = gate_mine.shape[1]
    rest = [[o_mine], [gate_mine, up_mine], [down_mine]]
    rest_other = [[o_other], [gate_other, up_other], [down_other]]
    blocks = [first_block] + [chip_block(mine, other) for mine, other in zip(rest, rest_other)]
    cuts = [q_cols + 128, o_cols // 2, ff_cols, ff_cols // 2]
    gathered = []
    held_z, held_plane = None, None
    for block, cut in zip(blocks, cuts):
        if held_z is not None:
            block, held_z = barrier((block, held_z))
        left = net.gather_z(block[:, :cut])
        right = net.gather_z(block[:, cut:])
        held_z = (left[-1], right[-1])
        left = jnp.concatenate(left)
        right = jnp.concatenate(right)
        if held_plane is not None:
            left, right, held_plane = barrier((left, right, held_plane))
        left = net.gather_plane_first(left, "y")
        right = net.gather_plane_first(right, "x")
        held_plane = (left[-1], right[-1])
        left = net.gather_plane_second(left, "x")
        right = net.gather_plane_second(right, "y")
        gathered.append((jnp.concatenate(left), jnp.concatenate(right)))
    (q_extra, kv_full), (o_left, o_right), (gate_full, up_full), (down_left, down_right) = gathered
    q_full = q_extra[:, :q_cols]
    gains = q_extra[:, q_cols : q_cols + 4].astype(full)
    o_full = jnp.concatenate([o_left, o_right], 1)
    down_full = jnp.concatenate([down_left, down_right], 1)

    places = net.places(net.chip, 2 * weight_rows)
    order = (jnp.arange(width, dtype=jnp.int32)[:, None] == places[None, :]).astype(low)
    head_places = net.places(net.chip, 2 * gain_rows)
    head_order = (
        jnp.arange(head_size, dtype=jnp.int32)[:, None] == head_places[None, :]
    ).astype(full)

    def head_gain(column):
        spread = column.reshape(net.count, weight_rows)[:, :gain_rows].reshape(1, head_size)
        return jnp.sum(head_order * spread, axis=1)

    gain_one = gains[:, 0]
    gain_two = gains[:, 1]
    q_gain_full = head_gain(gains[:, 2])
    k_gain_full = head_gain(gains[:, 3])

    chip_tokens = net.by_core(tokens, net.pair(tokens))
    before_tokens = net.chip_along(chip_tokens[chip_rows - halo :], 1)
    chip_segments = net.by_core(segments, net.pair(segments))
    before_segments = net.chip_along(chip_segments[chip_rows - halo :], 1)
    before_segments = jnp.where(net.chip > 0, before_segments, -1)
    window_tokens = jnp.concatenate([before_tokens, chip_tokens])
    window_segments = jnp.concatenate([before_segments, chip_segments])
    counter = jnp.arange(halo + chip_rows, dtype=jnp.int32)
    changes = jnp.concatenate([jnp.ones((1,), bool), window_segments[1:] != window_segments[:-1]])
    starts = lax.cummax(jnp.where(changes, counter, 0), axis=0)
    offsets = (counter - starts).astype(full)
    frequency = jnp.exp(
        jnp.arange(head_size // 2, dtype=full) * (-2.0 * math.log(rope_base) / head_size)
    )
    angles = offsets[:, None] * frequency[None, :]
    cosines = jnp.cos(angles)[:, None, :]
    sines = jnp.sin(angles)[:, None, :]
    q_cosines, q_sines = cosines[halo:], sines[halo:]
    query_segments = chip_segments[None, :]
    key_segments = window_segments[:, None]

    ordered = dot(window_tokens, order, kind=low)
    inputs = ordered.astype(full)
    attn_in = (inputs * inverse_rms(inputs) * gain_one).astype(low)
    chip_attn_in = attn_in[halo:]
    own_inputs = lax.dynamic_slice_in_dim(ordered, halo + net.core * row_count, row_count).astype(
        full
    )
    scale_one = inverse_rms(own_inputs)
    normed_one = own_inputs * scale_one
    own_cotangent = dot(cotangent, order, kind=low)
    chip_cotangent = jnp.concatenate([own_cotangent, net.pair(own_cotangent)])

    query_proj = dot(chip_attn_in, q_full).reshape(chip_rows, -1, head_size)
    kv_proj = dot(attn_in, kv_full)
    key_proj = kv_proj[:, :k_cols].reshape(halo + chip_rows, -1, head_size)
    values = kv_proj[:, k_cols:].astype(low)
    query_scale = inverse_rms(query_proj)
    query_normed = query_proj * query_scale
    key_scale = inverse_rms(key_proj)
    key_normed = key_proj * key_scale
    queries = (
        rotate(query_normed * q_gain_full, q_cosines, q_sines).astype(low).reshape(chip_rows, -1)
    )
    keys = (
        rotate(key_normed * k_gain_full, cosines, sines).astype(low).reshape(halo + chip_rows, -1)
    )
    attended = attention_forward(
        queries, keys, values, query_segments, key_segments, row_count, halo, head_size
    )

    attended_mine, attended_other = net.halves(attended)
    branch_sent = net.pair(dot(attended_other, o_full, 1, 1))
    hidden_state = own_inputs + (dot(attended_mine, o_full, 1, 1) + branch_sent)
    scale_two = inverse_rms(hidden_state)
    normed_two = hidden_state * scale_two
    mlp_own = (normed_two * gain_two).astype(low)
    mlp_in = jnp.concatenate([mlp_own, net.pair(mlp_own)])
    gate_proj = dot(mlp_in, gate_full)
    up_proj = dot(mlp_in, up_full)
    sigmoid_gate = jax.nn.sigmoid(gate_proj)
    activated = (gate_proj * sigmoid_gate * up_proj).astype(low)
    down_grad = dot(chip_cotangent, activated, 0, 0, low)
    act_grad = dot(chip_cotangent, down_full)
    gate_grad = (
        act_grad * up_proj * sigmoid_gate * (1.0 + gate_proj * (1.0 - sigmoid_gate))
    ).astype(low)
    up_grad = (act_grad * gate_proj * sigmoid_gate).astype(low)
    mlp_grad_sent = net.pair(
        dot(gate_grad[row_count:], gate_full, 1, 1) + dot(up_grad[row_count:], up_full, 1, 1)
    )
    mlp_in_grad = (
        dot(gate_grad[:row_count], gate_full, 1, 1)
        + dot(up_grad[:row_count], up_full, 1, 1)
        + mlp_grad_sent
    )
    gate_w_grad = dot(mlp_in, gate_grad, 0, 0, low)
    up_w_grad = dot(mlp_in, up_grad, 0, 0, low)
    out_sent = net.pair(dot(activated[row_count:], down_full, 1, 1))
    mixed_out = (
        hidden_state + (dot(activated[:row_count], down_full, 1, 1) + out_sent)
    ).astype(low)
    mixed_out = dot(mixed_out, order, 1, 1, low)

    gain_two_grad = jnp.sum(mlp_in_grad * normed_two, axis=0)
    hidden_grad = own_cotangent.astype(full) + norm_back(
        mlp_in_grad * gain_two, normed_two, scale_two
    )
    branch_own = hidden_grad.astype(low)
    branch_low = net.by_core(branch_own, net.pair(branch_own))
    attended_grad = dot(branch_low, o_full, kind=low)
    o_w_grad = dot(branch_low, attended, 0, 0, low)
    query_grad, key_grad, value_grad = attention_backward(
        queries,
        keys,
        values,
        attended_grad,
        query_segments,
        key_segments,
        row_count,
        halo,
        head_size,
    )
    query_back = rotate(query_grad.reshape(query_proj.shape), q_cosines, -q_sines)
    key_back = rotate(key_grad.reshape(key_proj.shape), cosines, -sines)
    q_gain_grad = jnp.sum(query_back * query_normed, axis=(0, 1))
    k_gain_grad = jnp.sum(key_back * key_normed, axis=(0, 1))
    query_low = (
        norm_back(query_back * q_gain_full, query_normed, query_scale)
        .astype(low)
        .reshape(chip_rows, -1)
    )
    key_low = (
        norm_back(key_back * k_gain_full, key_normed, key_scale)
        .astype(low)
        .reshape(halo + chip_rows, -1)
    )
    value_low = value_grad.astype(low)
    kv_low = jnp.concatenate([key_low, value_low], axis=1)
    q_w_grad = dot(chip_attn_in, query_low, 0, 0, low)
    kv_w_grad = dot(attn_in, kv_low, 0, 0, low)

    before_grad = net.chip_along(dot(kv_low[:halo], kv_full, 1, 1, low), -1)
    next_places = net.places(net.chip + 1, 2 * weight_rows)
    next_order = (next_places[:, None] == places[None, :]).astype(low)
    before_grad = dot(before_grad, next_order)
    chip_grad = dot(query_low, q_full, 1, 1) + dot(kv_low[halo:], kv_full, 1, 1)
    chip_grad = jnp.concatenate(
        [chip_grad[: chip_rows - halo], chip_grad[chip_rows - halo :] + before_grad]
    )
    grad_mine, grad_other = net.halves(chip_grad)
    attn_in_grad = grad_mine + net.pair(grad_other)
    gain_one_grad = jnp.sum(attn_in_grad * normed_one, axis=0)
    input_grad = (hidden_grad + norm_back(attn_in_grad * gain_one, normed_one, scale_one)).astype(
        low
    )
    input_grad = dot(input_grad, order, 1, 1, low)

    down_cut = ff_cols // 2
    o_cut = o_cols // 2
    down_sum = jnp.concatenate(
        [net.scatter(down_grad[:, :down_cut], "x"), net.scatter(down_grad[:, down_cut:], "y")], 1
    )
    gate_sum = net.scatter(gate_w_grad, "x")
    up_sum = net.scatter(up_w_grad, "y")
    o_sum = jnp.concatenate(
        [net.scatter(o_w_grad[:, :o_cut], "x"), net.scatter(o_w_grad[:, o_cut:], "y")], 1
    )
    q_sum = net.scatter(q_w_grad, "x")
    kv_sum = net.scatter(kv_w_grad, "y")

    def head_sum(gradient):
        return jnp.sum(head_order * gradient[:, None], axis=0).reshape(net.chips, 2, gain_rows)

    gain_sum = jnp.concatenate(
        [
            gain_one_grad.reshape(net.chips, 2, weight_rows),
            gain_two_grad.reshape(net.chips, 2, weight_rows),
            head_sum(q_gain_grad),
            head_sum(k_gain_grad),
        ],
        axis=2,
    )
    gain_sum = net.scatter(gain_sum, "x").reshape(2, -1)
    gain_mine, gain_other = net.halves(gain_sum)
    gain_sum = (gain_mine + net.pair(gain_other))[0]
    return (
        mixed_out,
        input_grad,
        gain_sum[:weight_rows],
        net.finish(q_sum),
        net.finish(kv_sum[:, :k_cols]),
        net.finish(kv_sum[:, k_cols:]),
        net.finish(o_sum),
        gain_sum[2 * weight_rows : 2 * weight_rows + gain_rows],
        gain_sum[2 * weight_rows + gain_rows :],
        gain_sum[weight_rows : 2 * weight_rows],
        net.finish(gate_sum),
        net.finish(up_sum),
        net.finish(down_sum),
    )


def solution(mesh):
    rows = P("dp", None)
    line = P("dp")
    return jax.shard_map(
        per_device,
        mesh=mesh,
        in_specs=(
            rows, line, line, rows, rows, rows, rows, line, line, line, rows, rows, rows, rows,
        ),
        out_specs=(
            rows, rows, line, rows, rows, rows, rows, line, line, line, rows, rows, rows,
        ),
        check_vma=False,
    )
```

time: 1700 us -> 682 us (0.40)
  waiting for transfers between devices: 1190 us -> 259 us
  matrix products: 238 us -> 125 us
  starting transfers between devices: 11.1 us -> 116 us
  blocking collectives: 94.2 us -> 0 us
  Pallas kernels: 0 us -> 43.5 us
    reduce_scatter x6 -> x0, waiting for transfers between devices: 722 us -> none  [the longest x1 162 us: per_device(): lax.psum_scatter(up_w_grad, 'dp', scatter_dimension=0, tiled=True)]
    all_gather x7 -> x0, waiting for transfers between devices: 295 us -> none  [the longest x1 63.1 us: per_device(): lax.all_gather(gate_weight, 'dp', axis=0, tiled=True)]
    ppermute x5 -> x126, waiting for transfers between devices: 10.6 us -> 259 us  [the longest x51 132 us: ring(): lax.ppermute(array, 'dp', [(i, (i + step) % self.count) for i in range(se...]
    unnamed x15 -> x0, waiting for transfers between devices: 162 us -> none
    dot_general x77 -> x27, matrix products: 238 us -> 125 us  [dot(): lax.dot_general(left_side, right_side, (((left_dim,), (right_dim,)), ((),...]
    ppermute x5 -> x126, starting transfers between devices: 10.5 us -> 116 us  [the longest x72 62.8 us: flip(): return lax.ppermute(array, 'dp', [(i, i ^ mask) for i in range(self.count)])]
    unnamed x2 -> x0, blocking collectives: 94.2 us -> none
    pallas_call x0 -> x2, Pallas kernels: none -> 43.5 us  [the longest x1 26 us: attention_backward(): pl.pallas_call(functools.partial(backward_kernel, scale, rows, halo), gri...]
  transfers between devices with their start and end apart: 19 -> 126, of which waited for: 14 -> 61; matrix products, arithmetic and copies ran while one was open for 13% -> 26% of each run, Pallas kernels for 0% -> 3%
where the time goes in v1:
time: 682 us; the launch traced here: 674 us
  waiting for transfers between devices  259 us (38%)
  matrix products  125 us (18%)
  starting transfers between devices  116 us (17%)
  other arithmetic  67.9 us (10%)
  local copies, waits for them, and re-layouts  58.9 us (9%)
  Pallas kernels  43.5 us (6%)
    ppermute x51, waiting for transfers between devices, ring(): lax.ppermute(array, 'dp', [(i, (i + step) % self.count) for i in range(se...  132 us
    ppermute x72, waiting for transfers between devices, flip(): return lax.ppermute(array, 'dp', [(i, i ^ mask) for i in range(self.count)])  125 us
    dot_general x27, matrix products, dot(): lax.dot_general(left_side, right_side, (((left_dim,), (right_dim,)), ((),...  125 us
    ppermute x72, starting transfers between devices, flip(): return lax.ppermute(array, 'dp', [(i, i ^ mask) for i in range(self.count)])  62.8 us
    ppermute x51, starting transfers between devices, ring(): lax.ppermute(array, 'dp', [(i, (i + step) % self.count) for i in range(se...  45.9 us
    pallas_call x1, Pallas kernels, attention_backward(): pl.pallas_call(functools.partial(backward_kernel, scale, rows, halo), gri...  26 us
    pallas_call x1, Pallas kernels, attention_forward(): pl.pallas_call(functools.partial(forward_kernel, scale, rows, halo), grid...  17.5 us
  transfers between devices with their start and end apart: 126, of which 61 were waited for; matrix products, arithmetic and copies ran while one was open for 26% of the time, Pallas kernels for 3%

profile of v1, /device:TPU:0, one launch (start us, length us, event | category | flops | bytes accessed | tf_op | source)
XLA Modules:
  0.0 673.9 jit_solution(9242516214131195988)
XLA Ops:
  39.7 6.6 collective-permute-done.11
  47.7 6.8 %collective-permute-done.12 = bf16[64,1024]{1,0:T(8,128)(2,1)S(1)} collective-permute-done((bf16[64,1024]{1,0:T(8,128)(2,1)S(1)}, bf16[64,1024]{1,0:T(8,128)(2,1)S(1)}, u32[]{:S(2)}, u32[]{:S(2)}) %collective-permute-start.12) | collective-permute-done | bytes 131104 | tf_op jit(solution)/shard_map/ppermute | solution.py:61
  56.6 5.8 collective-permute-done.13
  64.6 6.0 collective-permute-done.18
  71.3 5.3 collective-permute-done.19
  77.3 5.3 collective-permute-done.20
  89.8 4.7 collective-permute-done.33
  98.8 7.0 %collective-permute-done.34 = bf16[64,1536]{1,0:T(8,128)(2,1)S(1)} collective-permute-done((bf16[64,1536]{1,0:T(8,128)(2,1)S(1)}, bf16[64,1536]{1,0:T(8,128)(2,1)S(1)}, u32[]{:S(2)}, u32[]{:S(2)}) %collective-permute-start.34) | collective-permute-done | bytes 196640 | tf_op jit(solution)/shard_map/ppermute | solution.py:61
  108.0 8.0 %collective-permute-done.35 = bf16[64,1536]{1,0:T(8,128)(2,1)S(1)} collective-permute-done((bf16[64,1536]{1,0:T(8,128)(2,1)S(1)}, bf16[64,1536]{1,0:T(8,128)(2,1)S(1)}, u32[]{:S(2)}, u32[]{:S(2)}) %collective-permute-start.35) | collective-permute-done | bytes 196640 | tf_op jit(solution)/shard_map/ppermute | solution.py:61
  118.2 4.5 collective-permute-start.27
  132.2 10.5 %collective-permute-done.8 = bf16[256,1152]{1,0:T(8,128)(2,1)S(1)} collective-permute-done((bf16[256,1152]{1,0:T(8,128)(2,1)S(1)}, bf16[256,1152]{1,0:T(8,128)(2,1)S(1)}, u32[]{:S(2)}, u32[]{:S(2)}) %collective-permute-start.8) | collective-permute-done | bytes 589856 | tf_op jit(solution)/shard_map/ppermute | solution.py:57
  153.0 5.0 multiply_reduce_fusion.1
  186.8 17.5 %attention_forward.1 = bf16[1024,1024]{1,0:T(8,128)(2,1)S(1)} custom-call(bf16[1024,1024]{1,0:T(8,128)(2,1)} %copy.94.q_ref, bf16[1280,512]{1,0:T(8,128)(2,1)S(1)} %bitcast.116, bf16[1280,512]{1,0:T(8,128)(2,1)S(1)} %slice.379.v_ref, s32[1,1024]{1,0:T(1,128)S(1)} %broadcast_select_fusion.qs_ref, s32[1280,1]{1,0:T(8,128)S(1)} %broadcast_in_dim.28.ks_ref), custom_call_target="tpu_custom_call" | custom-call | flops 3221225472 | bytes 6815744 | tf_op jit(solution)/shard_map/attention_forward/pallas_call | solution.py:244
  207.0 4.7 fusion.72
  216.7 5.1 collective-permute-done.50
  223.2 5.0 collective-permute-done.51
  228.2 6.4 collective-permute-done.48
  235.4 8.3 %collective-permute-done.40 = bf16[256,1536]{1,0:T(8,128)(2,1)S(1)} collective-permute-done((bf16[256,1536]{1,0:T(8,128)(2,1)S(1)}, bf16[256,1536]{1,0:T(8,128)(2,1)S(1)}, u32[]{:S(2)}, u32[]{:S(2)}) %collective-permute-start.40) | collective-permute-done | bytes 786464 | tf_op jit(solution)/shard_map/ppermute | solution.py:57
  243.9 5.1 multiply_reduce_fusion.6
  249.2 6.5 collective-permute-done.39
  255.9 4.6 collective-permute-done.43
  260.5 16.8 %collective-permute-done.44 = bf16[256,1536]{1,0:T(8,128)(2,1)S(1)} collective-permute-done((bf16[256,1536]{1,0:T(8,128)(2,1)S(1)}, bf16[256,1536]{1,0:T(8,128)(2,1)S(1)}, u32[]{:S(2)}, u32[]{:S(2)}) %collective-permute-start.44) | collective-permute-done | bytes 786464 | tf_op jit(solution)/shard_map/ppermute | solution.py:57
  279.6 4.6 collective-permute-done.53
  284.4 4.9 collective-permute-done.55
  289.7 6.2 fusion.146
  295.9 6.2 fusion.147
  303.8 14.6 %multiply_convert_fusion.1 = (bf16[1024,1536]{1,0:T(8,128)(2,1)}, bf16[1024,1536]{1,0:T(8,128)(2,1)}, bf16[1024,1536]{1,0:T(8,128)(2,1)}) fusion(f32[1024,1536]{1,0:T(8,128)} %fusion.147, f32[1024,1536]{1,0:T(8,128)} %fusion.146, bf16[256,768]{1,0:T(8,128)(2,1)} %collective-permute-done.57, bf16[256,768]{1,0:T(8,128)(2,1)} %copy-done.93, ...), kind=kOutput, calls=%fused_computation.5 | convolution fusion | flops 3275751424 | bytes 27262976 | tf_op jit(solution)/shard_map/dot_general | solution.py:20
  318.4 6.1 fusion.64
  345.6 4.6 fusion.56
  360.4 6.4 collective-permute-done.121
  370.8 11.5 %collective-permute-done.115 = bf16[256,768]{1,0:T(8,128)(2,1)S(1)} collective-permute-done((bf16[256,768]{1,0:T(8,128)(2,1)S(1)}, bf16[256,768]{1,0:T(8,128)(2,1)S(1)}, u32[]{:S(2)}, u32[]{:S(2)}) %collective-permute-start.115) | collective-permute-done | bytes 393248 | tf_op jit(solution)/shard_map/ppermute | solution.py:57
  400.6 19.1 %collective-permute-done.108 = bf16[256,1536]{1,0:T(8,128)(2,1)S(1)} collective-permute-done((bf16[256,1536]{1,0:T(8,128)(2,1)S(1)}, bf16[256,1536]{1,0:T(8,128)(2,1)S(1)}, u32[]{:S(2)}, u32[]{:S(2)}) %collective-permute-start.108) | collective-permute-done | bytes 786464 | tf_op jit(solution)/shard_map/ppermute | solution.py:57
  424.9 5.6 collective-permute-done.109
  433.0 9.7 %collective-permute-done.110 = bf16[64,1536]{1,0:T(8,128)(2,1)S(1)} collective-permute-done((bf16[64,1536]{1,0:T(8,128)(2,1)S(1)}, bf16[64,1536]{1,0:T(8,128)(2,1)S(1)}, u32[]{:S(2)}, u32[]{:S(2)}) %collective-permute-start.110) | collective-permute-done | bytes 196640 | tf_op jit(solution)/shard_map/ppermute | solution.py:61
  445.4 6.4 collective-permute-done.103
  458.9 7.6 %fusion.8 = bf16[512,1024]{1,0:T(8,128)(2,1)} fusion(s32[1024]{0:T(1024)S(1)} %copy-done.82, f32[512,1024]{1,0:T(8,128)} %copy-done.8, f32[512,1024]{1,0:T(8,128)} %collective-permute-done.58, bf16[1024,1536]{1,0:T(8,128)(2,1)} %get-tuple-element.54, bf16[256,768]{1,0:T(8,128)(2,1)} %collective-permute-done.57, bf16[256,768]{1,0:T(8,128)(2,1)} %copy-done.93, ...), kind=kOutput, calls=%fused_computation.27 | convolution fusion | flops 2712141824 | bytes 9965568 | tf_op jit(solution)/shard_map/dot_general | solution.py:20
  466.5 6.7 fusion.82.g_ref
  473.2 26.0 %attention_backward.1 = (f32[1024,1024]{1,0:T(8,128)}, f32[1280,512]{1,0:T(8,128)}, f32[1280,512]{1,0:T(8,128)}) custom-call(bf16[1024,1024]{1,0:T(8,128)(2,1)S(1)} %copy-done.2, bf16[1280,512]{1,0:T(8,128)(2,1)S(1)} %bitcast.117, bf16[1280,512]{1,0:T(8,128)(2,1)S(1)} %slice.379.v_ref, bf16[1024,1024]{1,0:T(8,128)(2,1)} %fusion.82.g_ref, ...), custom_call_target="tpu_custom_call" | custom-call | flops 8053063680 | bytes 16252928 | tf_op jit(solution)/shard_map/attention_backward/pallas_call | solution.py:270
  504.8 5.1 multiply_reduce_fusion.2
  522.9 4.4 fusion.31
  527.3 4.8 fusion.81
  538.4 5.4 copy.95
  553.7 4.4 convolution_add_fusion
  571.0 12.6 %collective-permute-done.94 = bf16[256,512]{1,0:T(8,128)(2,1)S(1)} collective-permute-done((bf16[256,512]{1,0:T(8,128)(2,1)S(1)}, bf16[256,512]{1,0:T(8,128)(2,1)S(1)}, u32[]{:S(2)}, u32[]{:S(2)}) %collective-permute-start.94) | collective-permute-done | bytes 262176 | tf_op jit(solution)/shard_map/ppermute | solution.py:57
  589.7 5.2 collective-permute-done.72
  616.1 6.6 collective-permute-done.80
  633.0 8.3 %collective-permute-done.82 = bf16[64,1024]{1,0:T(8,128)(2,1)S(1)} collective-permute-done((bf16[64,1024]{1,0:T(8,128)(2,1)S(1)}, bf16[64,1024]{1,0:T(8,128)(2,1)S(1)}, u32[]{:S(2)}, u32[]{:S(2)}) %collective-permute-start.82) | collective-permute-done | bytes 131104 | tf_op jit(solution)/shard_map/ppermute | solution.py:61
  666.2 6.0 fusion.6
  (636 shorter events, 305.8 us)
Async XLA Ops:
  6.3 25.2 %collective-permute-start.2 = (bf16[32,2176]{1,0:T(8,128)(2,1)}, bf16[32,2176]{1,0:T(8,128)(2,1)}, u32[]{:S(2)}, u32[]{:S(2)}) collective-permute-start(bf16[32,2176]{1,0:T(8,128)(2,1)} %concatenate.231), channel_id=1, source_target_pairs={{0,1},{1,0},{2,3},{3,2},{4,5},{5,4},{6,7},{7,6},{8,9},{9,8},{10,11... | collective-permute-start | bytes 417800 | tf_op jit(solution)/shard_map/ppermute | solution.py:57
  8.2 20.6 %collective-permute-start.17 = (bf16[32,1024]{1,0:T(8,128)(2,1)}, bf16[32,1024]{1,0:T(8,128)(2,1)}, u32[]{:S(2)}, u32[]{:S(2)}) collective-permute-start(bf16[32,1024]{1,0:T(8,128)(2,1)} %get-tuple-element.149), channel_id=1, source_target_pairs={{0,1},{1,0},{2,3},{3,2},{4,5},{5,4},{6,7},{7,6},{8,9},{9,8},{10,11... | collective-permute-start | bytes 196616 | tf_op jit(solution)/shard_map/ppermute | solution.py:57
  10.7 27.9 %collective-permute-start.32 = (bf16[32,3072]{1,0:T(8,128)(2,1)}, bf16[32,3072]{1,0:T(8,128)(2,1)}, u32[]{:S(2)}, u32[]{:S(2)}) collective-permute-start(bf16[32,3072]{1,0:T(8,128)(2,1)} %pad_maximum_fusion.18), channel_id=1, source_target_pairs={{0,1},{1,0},{2,3},{3,2},{4,5},{5,4},{6,7},{7,6},{8,9},{9,8},{10,11... | collective-permute-start | bytes 589832 | tf_op jit(solution)/shard_map/ppermute | solution.py:57
  23.3 63.8 %collective-permute-start = (bf16[512,1024]{1,0:T(8,128)(2,1)}, bf16[512,1024]{1,0:T(8,128)(2,1)S(1)}, u32[]{:S(2)}, u32[]{:S(2)}) collective-permute-start(bf16[512,1024]{1,0:T(8,128)(2,1)} %param.14), channel_id=1, source_target_pairs={{0,1},{1,0},{2,3},{3,2},{4,5},{5,4},{6,7},{7,6},{8,9},{9,8},{10,11... | collective-permute-start | bytes 3145736 | tf_op jit(solution)/shard_map/ppermute | solution.py:57
  62.5 24.6 %collective-permute-start.14 = (bf16[256,1024]{1,0:T(8,128)(2,1)S(1)}, bf16[256,1024]{1,0:T(8,128)(2,1)S(1)}, u32[]{:S(2)}, u32[]{:S(2)}) collective-permute-start(bf16[256,1024]{1,0:T(8,128)(2,1)S(1)} %pad_maximum_fusion.13), channel_id=1, source_target_pairs={{0,2},{1,3},{2,0},{3,1},{4,6},{5,7},{6,4},{7,5},{8,10},{9,11},{10,... | collective-permute-start | bytes 1572872 | tf_op jit(solution)/shard_map/ppermute | solution.py:57
  62.5 34.1 %collective-permute-start.15 = (bf16[256,1024]{1,0:T(8,128)(2,1)S(1)}, bf16[256,1024]{1,0:T(8,128)(2,1)S(1)}, u32[]{:S(2)}, u32[]{:S(2)}) collective-permute-start(bf16[256,1024]{1,0:T(8,128)(2,1)S(1)} %pad_maximum_fusion.13), channel_id=1, source_target_pairs={{0,4},{1,5},{2,6},{3,7},{4,0},{5,1},{6,2},{7,3},{8,12},{9,13},{10,... | collective-permute-start | bytes 1572872 | tf_op jit(solution)/shard_map/ppermute | solution.py:57
  82.6 25.2 %collective-permute-start.7 = (bf16[256,1152]{1,0:T(8,128)(2,1)S(1)}, bf16[256,1152]{1,0:T(8,128)(2,1)S(1)}, u32[]{:S(2)}, u32[]{:S(2)}) collective-permute-start(bf16[256,1152]{1,0:T(8,128)(2,1)S(1)} %pad_maximum_fusion.12), channel_id=1, source_target_pairs={{0,4},{1,5},{2,6},{3,7},{4,0},{5,1},{6,2},{7,3},{8,12},{9,13},{10,... | collective-permute-start | bytes 1769480 | tf_op jit(solution)/shard_map/ppermute | solution.py:57
  94.5 207.6 %collective-permute-start.59 = (bf16[512,1024]{1,0:T(8,128)(2,1)}, bf16[512,1024]{1,0:T(8,128)(2,1)}, u32[]{:S(2)}, u32[]{:S(2)}) collective-permute-start(bf16[512,1024]{1,0:T(8,128)(2,1)} %fusion.63), channel_id=1, source_target_pairs={{0,1},{1,0},{2,3},{3,2},{4,5},{5,4},{6,7},{7,6},{8,9},{9,8},{10,11... | collective-permute-start | bytes 3145736 | tf_op jit(solution)/shard_map/ppermute | solution.py:57
  96.8 26.6 %collective-permute-start.1 = (bf16[256,1024]{1,0:T(8,128)(2,1)S(1)}, bf16[256,1024]{1,0:T(8,128)(2,1)S(1)}, u32[]{:S(2)}, u32[]{:S(2)}) collective-permute-start(bf16[256,1024]{1,0:T(8,128)(2,1)S(1)} %slice.244), channel_id=1, source_target_pairs={{0,2},{1,3},{2,4},{3,5},{4,6},{5,7},{6,8},{7,9},{8,10},{9,11},{10,... | collective-permute-start | bytes 1572872 | tf_op jit(solution)/shard_map/ppermute | solution.py:67
  105.8 21.3 %collective-permute-start.16 = (bf16[256,1024]{1,0:T(8,128)(2,1)S(1)}, bf16[256,1024]{1,0:T(8,128)(2,1)S(1)}, u32[]{:S(2)}, u32[]{:S(2)}) collective-permute-start(bf16[256,1024]{1,0:T(8,128)(2,1)S(1)} %collective-permute-done.14), channel_id=1, source_target_pairs={{0,4},{1,5},{2,6},{3,7},{4,0},{5,1},{6,2},{7,3},{8,12},{9,13},{10,... | collective-permute-start | bytes 1572872 | tf_op jit(solution)/shard_map/ppermute | solution.py:57
  123.3 19.4 %collective-permute-start.8 = (bf16[256,1152]{1,0:T(8,128)(2,1)S(1)}, bf16[256,1152]{1,0:T(8,128)(2,1)S(1)}, u32[]{:S(2)}, u32[]{:S(2)}) collective-permute-start(bf16[256,1152]{1,0:T(8,128)(2,1)S(1)} %collective-permute-done.7), channel_id=1, source_target_pairs={{0,2},{1,3},{2,0},{3,1},{4,6},{5,7},{6,4},{7,5},{8,10},{9,11},{10,... | collective-permute-start | bytes 1769480 | tf_op jit(solution)/shard_map/ppermute | solution.py:57
  127.1 77.2 %collective-permute-start.24 = (bf16[256,512]{1,0:T(8,128)(2,1)}, bf16[256,512]{1,0:T(8,128)(2,1)}, u32[]{:S(2)}, u32[]{:S(2)}) collective-permute-start(bf16[256,512]{1,0:T(8,128)(2,1)} %pad_maximum_fusion.16), channel_id=1, source_target_pairs={{0,2},{1,3},{2,0},{3,1},{4,6},{5,7},{6,4},{7,5},{8,10},{9,11},{10,... | collective-permute-start | bytes 786440 | tf_op jit(solution)/shard_map/ppermute | solution.py:57
  129.2 77.7 %collective-permute-start.28 = (bf16[256,512]{1,0:T(8,128)(2,1)}, bf16[256,512]{1,0:T(8,128)(2,1)}, u32[]{:S(2)}, u32[]{:S(2)}) collective-permute-start(bf16[256,512]{1,0:T(8,128)(2,1)} %pad_maximum_fusion.17), channel_id=1, source_target_pairs={{0,4},{1,5},{2,6},{3,7},{4,0},{5,1},{6,2},{7,3},{8,12},{9,13},{10,... | collective-permute-start | bytes 786440 | tf_op jit(solution)/shard_map/ppermute | solution.py:57
  131.3 75.7 %collective-permute-start.26 = (bf16[256,512]{1,0:T(8,128)(2,1)}, bf16[256,512]{1,0:T(8,128)(2,1)}, u32[]{:S(2)}, u32[]{:S(2)}) collective-permute-start(bf16[256,512]{1,0:T(8,128)(2,1)} %collective-permute-done.25), channel_id=1, source_target_pairs={{0,2},{1,3},{2,0},{3,1},{4,6},{5,7},{6,4},{7,5},{8,10},{9,11},{10,... | collective-permute-start | bytes 786440 | tf_op jit(solution)/shard_map/ppermute | solution.py:57
  142.7 64.3 %collective-permute-start.29 = (bf16[256,512]{1,0:T(8,128)(2,1)}, bf16[256,512]{1,0:T(8,128)(2,1)}, u32[]{:S(2)}, u32[]{:S(2)}) collective-permute-start(bf16[256,512]{1,0:T(8,128)(2,1)} %collective-permute-done.27), channel_id=1, source_target_pairs={{0,4},{1,5},{2,6},{3,7},{4,0},{5,1},{6,2},{7,3},{8,12},{9,13},{10,... | collective-permute-start | bytes 786440 | tf_op jit(solution)/shard_map/ppermute | solution.py:57
  211.8 31.8 %collective-permute-start.30 = (f32[512,1024]{1,0:T(8,128)S(1)}, f32[512,1024]{1,0:T(8,128)S(1)}, u32[]{:S(2)}, u32[]{:S(2)}) collective-permute-start(f32[512,1024]{1,0:T(8,128)S(1)} %fusion.72), channel_id=1, source_target_pairs={{0,1},{1,0},{2,3},{3,2},{4,5},{5,4},{6,7},{7,6},{8,9},{9,8},{10,11... | collective-permute-start | bytes 6291464 | tf_op jit(solution)/shard_map/ppermute | solution.py:57
  212.1 23.2 %collective-permute-start.42 = (bf16[256,1536]{1,0:T(8,128)(2,1)S(1)}, bf16[256,1536]{1,0:T(8,128)(2,1)S(1)}, u32[]{:S(2)}, u32[]{:S(2)}) collective-permute-start(bf16[256,1536]{1,0:T(8,128)(2,1)S(1)} %pad_maximum_fusion.11), channel_id=1, source_target_pairs={{0,2},{1,3},{2,0},{3,1},{4,6},{5,7},{6,4},{7,5},{8,10},{9,11},{10,... | collective-permute-start | bytes 2359304 | tf_op jit(solution)/shard_map/ppermute | solution.py:57
  223.1 20.5 %collective-permute-start.40 = (bf16[256,1536]{1,0:T(8,128)(2,1)S(1)}, bf16[256,1536]{1,0:T(8,128)(2,1)S(1)}, u32[]{:S(2)}, u32[]{:S(2)}) collective-permute-start(bf16[256,1536]{1,0:T(8,128)(2,1)S(1)} %pad_maximum_fusion.10), channel_id=1, source_target_pairs={{0,4},{1,5},{2,6},{3,7},{4,0},{5,1},{6,2},{7,3},{8,12},{9,13},{10,... | collective-permute-start | bytes 2359304 | tf_op jit(solution)/shard_map/ppermute | solution.py:57
  234.6 25.9 %collective-permute-start.43 = (bf16[256,1536]{1,0:T(8,128)(2,1)S(1)}, bf16[256,1536]{1,0:T(8,128)(2,1)S(1)}, u32[]{:S(2)}, u32[]{:S(2)}) collective-permute-start(bf16[256,1536]{1,0:T(8,128)(2,1)S(1)} %pad_maximum_fusion.11), channel_id=1, source_target_pairs={{0,4},{1,5},{2,6},{3,7},{4,0},{5,1},{6,2},{7,3},{8,12},{9,13},{10,... | collective-permute-start | bytes 2359304 | tf_op jit(solution)/shard_map/ppermute | solution.py:57
  235.3 20.5 %collective-permute-start.39 = (bf16[256,1536]{1,0:T(8,128)(2,1)S(1)}, bf16[256,1536]{1,0:T(8,128)(2,1)S(1)}, u32[]{:S(2)}, u32[]{:S(2)}) collective-permute-start(bf16[256,1536]{1,0:T(8,128)(2,1)S(1)} %pad_maximum_fusion.10), channel_id=1, source_target_pairs={{0,2},{1,3},{2,0},{3,1},{4,6},{5,7},{6,4},{7,5},{8,10},{9,11},{10,... | collective-permute-start | bytes 2359304 | tf_op jit(solution)/shard_map/ppermute | solution.py:57
  243.6 33.7 %collective-permute-start.44 = (bf16[256,1536]{1,0:T(8,128)(2,1)S(1)}, bf16[256,1536]{1,0:T(8,128)(2,1)S(1)}, u32[]{:S(2)}, u32[]{:S(2)}) collective-permute-start(bf16[256,1536]{1,0:T(8,128)(2,1)S(1)} %collective-permute-done.42), channel_id=1, source_target_pairs={{0,4},{1,5},{2,6},{3,7},{4,0},{5,1},{6,2},{7,3},{8,12},{9,13},{10,... | collective-permute-start | bytes 2359304 | tf_op jit(solution)/shard_map/ppermute | solution.py:57
  243.6 34.0 %collective-permute-start.41 = (bf16[256,1536]{1,0:T(8,128)(2,1)S(1)}, bf16[256,1536]{1,0:T(8,128)(2,1)S(1)}, u32[]{:S(2)}, u32[]{:S(2)}) collective-permute-start(bf16[256,1536]{1,0:T(8,128)(2,1)S(1)} %collective-permute-done.40), channel_id=1, source_target_pairs={{0,2},{1,3},{2,0},{3,1},{4,6},{5,7},{6,4},{7,5},{8,10},{9,11},{10,... | collective-permute-start | bytes 2359304 | tf_op jit(solution)/shard_map/ppermute | solution.py:57
  255.8 33.9 %collective-permute-start.31 = (bf16[512,1024]{1,0:T(8,128)(2,1)S(1)}, bf16[512,1024]{1,0:T(8,128)(2,1)S(1)}, u32[]{:S(2)}, u32[]{:S(2)}) collective-permute-start(bf16[512,1024]{1,0:T(8,128)(2,1)S(1)} %multiply_convert_fusion.3), channel_id=1, source_target_pairs={{0,1},{1,0},{2,3},{3,2},{4,5},{5,4},{6,7},{7,6},{8,9},{9,8},{10,11... | collective-permute-start | bytes 3145736 | tf_op jit(solution)/shard_map/ppermute | solution.py:57
  260.5 23.7 %collective-permute-start.53 = (bf16[256,768]{1,0:T(8,128)(2,1)S(1)}, bf16[256,768]{1,0:T(8,128)(2,1)S(1)}, u32[]{:S(2)}, u32[]{:S(2)}) collective-permute-start(bf16[256,768]{1,0:T(8,128)(2,1)S(1)} %pad_maximum_fusion.14), channel_id=1, source_target_pairs={{0,4},{1,5},{2,6},{3,7},{4,0},{5,1},{6,2},{7,3},{8,12},{9,13},{10,... | collective-permute-start | bytes 1179656 | tf_op jit(solution)/shard_map/ppermute | solution.py:57
  277.7 24.4 %collective-permute-start.52 = (bf16[256,768]{1,0:T(8,128)(2,1)S(1)}, bf16[256,768]{1,0:T(8,128)(2,1)S(1)}, u32[]{:S(2)}, u32[]{:S(2)}) collective-permute-start(bf16[256,768]{1,0:T(8,128)(2,1)S(1)} %pad_maximum_fusion.14), channel_id=1, source_target_pairs={{0,2},{1,3},{2,0},{3,1},{4,6},{5,7},{6,4},{7,5},{8,10},{9,11},{10,... | collective-permute-start | bytes 1179656 | tf_op jit(solution)/shard_map/ppermute | solution.py:57
  324.6 29.9 %collective-permute-start.120 = (bf16[256,768]{1,0:T(8,128)(2,1)S(1)}, bf16[256,768]{1,0:T(8,128)(2,1)S(1)}, u32[]{:S(2)}, u32[]{:S(2)}) collective-permute-start(bf16[256,768]{1,0:T(8,128)(2,1)S(1)} %get-tuple-element.73), channel_id=1, source_target_pairs={{0,4},{1,5},{2,6},{3,7},{4,0},{5,1},{6,2},{7,3},{8,12},{9,13},{10,... | collective-permute-start | bytes 1179656 | tf_op jit(solution)/shard_map/ppermute | solution.py:57
  326.7 31.6 %collective-permute-start.114 = (bf16[256,768]{1,0:T(8,128)(2,1)S(1)}, bf16[256,768]{1,0:T(8,128)(2,1)S(1)}, u32[]{:S(2)}, u32[]{:S(2)}) collective-permute-start(bf16[256,768]{1,0:T(8,128)(2,1)S(1)} %get-tuple-element.74), channel_id=1, source_target_pairs={{0,2},{1,3},{2,0},{3,1},{4,6},{5,7},{6,4},{7,5},{8,10},{9,11},{10,... | collective-permute-start | bytes 1179656 | tf_op jit(solution)/shard_map/ppermute | solution.py:57
  328.4 31.6 %collective-permute-start.119 = (bf16[256,768]{1,0:T(8,128)(2,1)S(1)}, bf16[256,768]{1,0:T(8,128)(2,1)S(1)}, u32[]{:S(2)}, u32[]{:S(2)}) collective-permute-start(bf16[256,768]{1,0:T(8,128)(2,1)S(1)} %get-tuple-element.72), channel_id=1, source_target_pairs={{0,4},{1,5},{2,6},{3,7},{4,0},{5,1},{6,2},{7,3},{8,12},{9,13},{10,... | collective-permute-start | bytes 1179656 | tf_op jit(solution)/shard_map/ppermute | solution.py:57
  328.5 42.3 %collective-permute-start.113 = (bf16[256,768]{1,0:T(8,128)(2,1)S(1)}, bf16[256,768]{1,0:T(8,128)(2,1)S(1)}, u32[]{:S(2)}, u32[]{:S(2)}) collective-permute-start(bf16[256,768]{1,0:T(8,128)(2,1)S(1)} %get-tuple-element.75), channel_id=1, source_target_pairs={{0,2},{1,3},{2,0},{3,1},{4,6},{5,7},{6,4},{7,5},{8,10},{9,11},{10,... | collective-permute-start | bytes 1179656 | tf_op jit(solution)/shard_map/ppermute | solution.py:57
  335.8 33.0 %collective-permute-start.107 = (bf16[256,1536]{1,0:T(8,128)(2,1)S(1)}, bf16[256,1536]{1,0:T(8,128)(2,1)S(1)}, u32[]{:S(2)}, u32[]{:S(2)}) collective-permute-start(bf16[256,1536]{1,0:T(8,128)(2,1)S(1)} %get-tuple-element.77), channel_id=1, source_target_pairs={{0,4},{1,5},{2,6},{3,7},{4,0},{5,1},{6,2},{7,3},{8,12},{9,13},{10,... | collective-permute-start | bytes 2359304 | tf_op jit(solution)/shard_map/ppermute | solution.py:57
  358.3 41.5 %collective-permute-start.106 = (bf16[256,1536]{1,0:T(8,128)(2,1)S(1)}, bf16[256,1536]{1,0:T(8,128)(2,1)S(1)}, u32[]{:S(2)}, u32[]{:S(2)}) collective-permute-start(bf16[256,1536]{1,0:T(8,128)(2,1)S(1)} %get-tuple-element.76), channel_id=1, source_target_pairs={{0,4},{1,5},{2,6},{3,7},{4,0},{5,1},{6,2},{7,3},{8,12},{9,13},{10,... | collective-permute-start | bytes 2359304 | tf_op jit(solution)/shard_map/ppermute | solution.py:57
  360.1 37.3 %collective-permute-start.100 = (bf16[256,1536]{1,0:T(8,128)(2,1)S(1)}, bf16[256,1536]{1,0:T(8,128)(2,1)S(1)}, u32[]{:S(2)}, u32[]{:S(2)}) collective-permute-start(bf16[256,1536]{1,0:T(8,128)(2,1)S(1)} %get-tuple-element.79), channel_id=1, source_target_pairs={{0,2},{1,3},{2,0},{3,1},{4,6},{5,7},{6,4},{7,5},{8,10},{9,11},{10,... | collective-permute-start | bytes 2359304 | tf_op jit(solution)/shard_map/ppermute | solution.py:57
  389.5 34.4 %collective-permute-start.99 = (bf16[256,1536]{1,0:T(8,128)(2,1)S(1)}, bf16[256,1536]{1,0:T(8,128)(2,1)S(1)}, u32[]{:S(2)}, u32[]{:S(2)}) collective-permute-start(bf16[256,1536]{1,0:T(8,128)(2,1)S(1)} %get-tuple-element.78), channel_id=1, source_target_pairs={{0,2},{1,3},{2,0},{3,1},{4,6},{5,7},{6,4},{7,5},{8,10},{9,11},{10,... | collective-permute-start | bytes 2359304 | tf_op jit(solution)/shard_map/ppermute | solution.py:57
  392.3 61.8 %collective-permute-start.60 = (f32[512,1024]{1,0:T(8,128)S(1)}, f32[512,1024]{1,0:T(8,128)S(1)}, u32[]{:S(2)}, u32[]{:S(2)}) collective-permute-start(f32[512,1024]{1,0:T(8,128)S(1)} %fusion.60), channel_id=1, source_target_pairs={{0,1},{1,0},{2,3},{3,2},{4,5},{5,4},{6,7},{7,6},{8,9},{9,8},{10,11... | collective-permute-start | bytes 6291464 | tf_op jit(solution)/shard_map/ppermute | solution.py:57
  395.7 24.0 %collective-permute-start.108 = (bf16[256,1536]{1,0:T(8,128)(2,1)S(1)}, bf16[256,1536]{1,0:T(8,128)(2,1)S(1)}, u32[]{:S(2)}, u32[]{:S(2)}) collective-permute-start(bf16[256,1536]{1,0:T(8,128)(2,1)S(1)} %add_convert_fusion.4), channel_id=1, source_target_pairs={{0,2},{1,3},{2,0},{3,1},{4,6},{5,7},{6,4},{7,5},{8,10},{9,11},{10,... | collective-permute-start | bytes 2359304 | tf_op jit(solution)/shard_map/ppermute | solution.py:57
  398.9 60.0 %collective-permute-start.58 = (f32[512,1024]{1,0:T(8,128)}, f32[512,1024]{1,0:T(8,128)}, u32[]{:S(2)}, u32[]{:S(2)}) collective-permute-start(f32[512,1024]{1,0:T(8,128)} %fusion.56), channel_id=1, source_target_pairs={{0,1},{1,0},{2,3},{3,2},{4,5},{5,4},{6,7},{7,6},{8,9},{9,8},{10,11... | collective-permute-start | bytes 6291464 | tf_op jit(solution)/shard_map/ppermute | solution.py:57
  399.8 24.2 %collective-permute-start.101 = (bf16[256,1536]{1,0:T(8,128)(2,1)S(1)}, bf16[256,1536]{1,0:T(8,128)(2,1)S(1)}, u32[]{:S(2)}, u32[]{:S(2)}) collective-permute-start(bf16[256,1536]{1,0:T(8,128)(2,1)S(1)} %add_convert_fusion.7), channel_id=1, source_target_pairs={{0,4},{1,5},{2,6},{3,7},{4,0},{5,1},{6,2},{7,3},{8,12},{9,13},{10,... | collective-permute-start | bytes 2359304 | tf_op jit(solution)/shard_map/ppermute | solution.py:57
  533.3 27.8 %collective-permute-start.93 = (bf16[256,512]{1,0:T(8,128)(2,1)}, bf16[256,512]{1,0:T(8,128)(2,1)}, u32[]{:S(2)}, u32[]{:S(2)}) collective-permute-start(bf16[256,512]{1,0:T(8,128)(2,1)} %get-tuple-element.83), channel_id=1, source_target_pairs={{0,4},{1,5},{2,6},{3,7},{4,0},{5,1},{6,2},{7,3},{8,12},{9,13},{10,... | collective-permute-start | bytes 786440 | tf_op jit(solution)/shard_map/ppermute | solution.py:57
  533.3 34.3 %collective-permute-start.87 = (bf16[256,512]{1,0:T(8,128)(2,1)}, bf16[256,512]{1,0:T(8,128)(2,1)S(1)}, u32[]{:S(2)}, u32[]{:S(2)}) collective-permute-start(bf16[256,512]{1,0:T(8,128)(2,1)} %get-tuple-element.84), channel_id=1, source_target_pairs={{0,2},{1,3},{2,0},{3,1},{4,6},{5,7},{6,4},{7,5},{8,10},{9,11},{10,... | collective-permute-start | bytes 786440 | tf_op jit(solution)/shard_map/ppermute | solution.py:57
  535.2 34.5 %collective-permute-start.92 = (bf16[256,512]{1,0:T(8,128)(2,1)}, bf16[256,512]{1,0:T(8,128)(2,1)}, u32[]{:S(2)}, u32[]{:S(2)}) collective-permute-start(bf16[256,512]{1,0:T(8,128)(2,1)} %get-tuple-element.82), channel_id=1, source_target_pairs={{0,4},{1,5},{2,6},{3,7},{4,0},{5,1},{6,2},{7,3},{8,12},{9,13},{10,... | collective-permute-start | bytes 786440 | tf_op jit(solution)/shard_map/ppermute | solution.py:57
  537.2 59.9 %collective-permute-start.86 = (bf16[256,512]{1,0:T(8,128)(2,1)}, bf16[256,512]{1,0:T(8,128)(2,1)}, u32[]{:S(2)}, u32[]{:S(2)}) collective-permute-start(bf16[256,512]{1,0:T(8,128)(2,1)} %get-tuple-element.85), channel_id=1, source_target_pairs={{0,2},{1,3},{2,0},{3,1},{4,6},{5,7},{6,4},{7,5},{8,10},{9,11},{10,... | collective-permute-start | bytes 786440 | tf_op jit(solution)/shard_map/ppermute | solution.py:57
  538.4 25.2 %collective-permute-start.79 = (bf16[256,1024]{1,0:T(8,128)(2,1)}, bf16[256,1024]{1,0:T(8,128)(2,1)}, u32[]{:S(2)}, u32[]{:S(2)}) collective-permute-start(bf16[256,1024]{1,0:T(8,128)(2,1)} %get-tuple-element.87), channel_id=1, source_target_pairs={{0,4},{1,5},{2,6},{3,7},{4,0},{5,1},{6,2},{7,3},{8,12},{9,13},{10,... | collective-permute-start | bytes 1572872 | tf_op jit(solution)/shard_map/ppermute | solution.py:57
  561.1 26.0 %collective-permute-start.62 = (bf16[256,1024]{1,0:T(8,128)(2,1)S(1)}, bf16[256,1024]{1,0:T(8,128)(2,1)S(1)}, u32[]{:S(2)}, u32[]{:S(2)}) collective-permute-start(bf16[256,1024]{1,0:T(8,128)(2,1)S(1)} %copy-done.39), channel_id=1, source_target_pairs={{2,0},{3,1},{4,2},{5,3},{6,4},{7,5},{8,6},{9,7},{10,8},{11,9},{12,... | collective-permute-start | bytes 1572872 | tf_op jit(solution)/shard_map/ppermute | solution.py:67
  563.6 20.0 %collective-permute-start.94 = (bf16[256,512]{1,0:T(8,128)(2,1)S(1)}, bf16[256,512]{1,0:T(8,128)(2,1)S(1)}, u32[]{:S(2)}, u32[]{:S(2)}) collective-permute-start(bf16[256,512]{1,0:T(8,128)(2,1)S(1)} %add_convert_fusion.22), channel_id=1, source_target_pairs={{0,2},{1,3},{2,0},{3,1},{4,6},{5,7},{6,4},{7,5},{8,10},{9,11},{10,... | collective-permute-start | bytes 786440 | tf_op jit(solution)/shard_map/ppermute | solution.py:57
  567.6 48.5 %collective-permute-start.78 = (bf16[256,1024]{1,0:T(8,128)(2,1)S(1)}, bf16[256,1024]{1,0:T(8,128)(2,1)S(1)}, u32[]{:S(2)}, u32[]{:S(2)}) collective-permute-start(bf16[256,1024]{1,0:T(8,128)(2,1)S(1)} %copy-done.40), channel_id=1, source_target_pairs={{0,4},{1,5},{2,6},{3,7},{4,0},{5,1},{6,2},{7,3},{8,12},{9,13},{10,... | collective-permute-start | bytes 1572872 | tf_op jit(solution)/shard_map/ppermute | solution.py:57
  569.7 25.2 %collective-permute-start.72 = (bf16[256,1024]{1,0:T(8,128)(2,1)S(1)}, bf16[256,1024]{1,0:T(8,128)(2,1)S(1)}, u32[]{:S(2)}, u32[]{:S(2)}) collective-permute-start(bf16[256,1024]{1,0:T(8,128)(2,1)S(1)} %get-tuple-element.89), channel_id=1, source_target_pairs={{0,2},{1,3},{2,0},{3,1},{4,6},{5,7},{6,4},{7,5},{8,10},{9,11},{10,... | collective-permute-start | bytes 1572872 | tf_op jit(solution)/shard_map/ppermute | solution.py:57
  583.6 40.7 %collective-permute-start.71 = (bf16[256,1024]{1,0:T(8,128)(2,1)S(1)}, bf16[256,1024]{1,0:T(8,128)(2,1)S(1)}, u32[]{:S(2)}, u32[]{:S(2)}) collective-permute-start(bf16[256,1024]{1,0:T(8,128)(2,1)S(1)} %get-tuple-element.88), channel_id=1, source_target_pairs={{0,2},{1,3},{2,0},{3,1},{4,6},{5,7},{6,4},{7,5},{8,10},{9,11},{10,... | collective-permute-start | bytes 1572872 | tf_op jit(solution)/shard_map/ppermute | solution.py:57
  615.2 33.7 %collective-permute-start.63 = (f32[512,1024]{1,0:T(8,128)S(1)}, f32[512,1024]{1,0:T(8,128)S(1)}, u32[]{:S(2)}, u32[]{:S(2)}) collective-permute-start(f32[512,1024]{1,0:T(8,128)S(1)} %fusion.33), channel_id=1, source_target_pairs={{0,1},{1,0},{2,3},{3,2},{4,5},{5,4},{6,7},{7,6},{8,9},{9,8},{10,11... | collective-permute-start | bytes 6291464 | tf_op jit(solution)/shard_map/ppermute | solution.py:57
  (182 other events, 2294.2 us)

commit v2 on v1

v2 whole, which is shorter than its diff:
```python
import functools
import math

import jax
import jax.numpy as jnp
from jax import lax
from jax.experimental import pallas as pl
from jax.experimental.pallas import tpu as pltpu
from jax.sharding import PartitionSpec as P

epsilon = 1e-06
rope_base = 1000000.0
low = jnp.bfloat16
full = jnp.float32
vmem_limit = 48 * 1024 * 1024
barrier = lax.optimization_barrier


def dot(left_side, right_side, left_dim=1, right_dim=0, kind=full):
    return lax.dot_general(
        left_side,
        right_side,
        (((left_dim,), (right_dim,)), ((), ())),
        preferred_element_type=kind,
    )


def inverse_rms(values):
    return lax.rsqrt(jnp.mean(values * values, axis=-1, keepdims=True) + epsilon)


def rotate(values, cosines, sines):
    half_size = values.shape[-1] // 2
    first_half = values[..., :half_size]
    second = values[..., half_size:]
    return jnp.concatenate(
        [first_half * cosines - second * sines, second * cosines + first_half * sines], axis=-1
    )


def norm_back(gradient, normed, scales):
    return scales * (gradient - normed * jnp.mean(gradient * normed, axis=-1, keepdims=True))


class Slice:
    def __init__(self):
        self.count = lax.axis_size("dp")
        self.chips = self.count // 2
        self.side = 1
        while 4 * self.side * self.side < self.chips:
            self.side *= 2
        self.device = lax.axis_index("dp")
        self.core = self.device % 2
        self.chip = self.device // 2

    def flip(self, array, mask):
        return lax.ppermute(array, "dp", [(i, i ^ mask) for i in range(self.count)])

    def ring(self, array, by):
        step = 2 * self.side * self.side * by
        return lax.ppermute(
            array, "dp", [(i, (i + step) % self.count) for i in range(self.count)]
        )

    def chip_along(self, array, by):
        pairs = [(i, i + 2 * by) for i in range(self.count) if 0 <= i + 2 * by < self.count]
        return lax.ppermute(array, "dp", pairs)

    def pair(self, array):
        return self.flip(array, 1)

    def by_core(self, mine, other, axis=0):
        return jnp.where(
            self.core == 0,
            jnp.concatenate([mine, other], axis=axis),
            jnp.concatenate([other, mine], axis=axis),
        )

    def halves(self, array, axis=0):
        size = array.shape[axis] // 2
        mine = lax.dynamic_slice_in_dim(array, self.core * size, size, axis)
        other = lax.dynamic_slice_in_dim(array, (1 - self.core) * size, size, axis)
        return mine, other

    def mask_of(self, name, amount):
        return 2 * amount * (1 if name == "x" else self.side)

    def places(self, chip, unit):
        side = self.side
        entry = jnp.arange(self.chips * unit, dtype=jnp.int32)
        inner, block = entry % unit, entry // unit
        along_z, along_x, along_y = block % 4, block // 4 % side, block // (4 * side)
        own_x, own_y, own_z = chip % side, chip // side % side, chip // (side * side)
        source = (
            ((own_z - along_z + 4) % 4) * side * side + (own_y ^ along_y) * side + (own_x ^ along_x)
        )
        return source * unit + inner

    def gather_z(self, block, steps=3):
        blocks = [block]
        for _ in range(steps):
            blocks.append(self.ring(blocks[-1], 1))
        return blocks

    def plane_first(self, block, name):
        return [block] + [self.flip(block, self.mask_of(name, m)) for m in range(1, self.side)]

    def plane_second(self, pieces, name):
        side = self.side
        rows = [pieces]
        for m in range(1, side):
            rows.append([self.flip(piece, self.mask_of(name, m)) for piece in pieces])
        if name == "y":
            return [rows[y][x] for y in range(side) for x in range(side)]
        return [rows[x][y] for y in range(side) for x in range(side)]

    def quarters(self, pieces):
        each = len(pieces) // 4
        if each == 1:
            return pieces
        return [jnp.concatenate(pieces[at * each : (at + 1) * each]) for at in range(4)]

    def pieces(self, array):
        side = self.side
        parts = jnp.split(array, side * side)
        return {(y, x): parts[y * side + x] for y in range(side) for x in range(side)}

    def scatter_send(self, current, name):
        at = 1 if name == "x" else 0
        brought = {}
        for key in [key for key in current if key[at] == 0]:
            sent = [(key[0], m) if name == "x" else (m, key[1]) for m in range(1, self.side)]
            brought[key] = [
                self.flip(current[other], self.mask_of(name, m + 1))
                for m, other in enumerate(sent)
            ]
        return brought

    def scatter_add(self, current, brought):
        return {
            key: sum([term.astype(full) for term in terms], current[key].astype(full)).astype(
                current[key].dtype
            )
            for key, terms in brought.items()
        }

    def scatter_ring(self, blocks, step):
        return self.ring(blocks[3 - step], -1)

    def scatter_z(self, block):
        blocks = jnp.split(block, 4)
        return [blocks[0]] + [self.ring(blocks[m], -m) for m in range(1, 4)]

    def finish(self, total):
        mine, other = self.halves(total)
        return self.by_core(mine, self.pair(other), axis=1)


def score_bias(query_segments, key_segments, rows, halo):
    key_count, query_count = key_segments.shape[0], query_segments.shape[1]
    key_place = lax.broadcasted_iota(jnp.int32, (key_count, query_count), 0) - halo
    query_place = lax.broadcasted_iota(jnp.int32, (key_count, query_count), 1)
    seen = (key_segments == query_segments) & (key_place <= query_place)
    return jnp.where(seen, 0.0, -1e30).astype(full)


def parts_of(rows, halo):
    return (((0, halo), 2 * halo), ((halo, rows), halo + rows))


def spread(refs, columns=slice(None)):
    return jnp.concatenate([ref[:, columns] for ref in refs], axis=0)


def reorder(refs, quarter, unit):
    size = refs[0].shape[0] // 4
    return jnp.concatenate(
        [
            ref[row : row + unit, :]
            for row in range(quarter * size, (quarter + 1) * size, unit)
            for ref in refs
        ],
        axis=0,
    )


def turn(values, cosines, sines):
    return values * cosines + pltpu.roll(values, values.shape[1] // 2, 1) * sines


def row_rms(values):
    return lax.rsqrt(jnp.mean(values * values, axis=1, keepdims=True) + epsilon)


def call(kernel, name, grid, ins, outs, flops, bytes_accessed, scratch=(), transcendentals=0):
    return pl.pallas_call(
        kernel,
        grid=grid,
        in_specs=[pl.BlockSpec(block, index) for _, block, index in ins],
        out_specs=[pl.BlockSpec(block, index) for _, _, block, index in outs],
        out_shape=[jax.ShapeDtypeStruct(shape, kind) for shape, kind, _, _ in outs],
        scratch_shapes=list(scratch),
        compiler_params=pltpu.CompilerParams(vmem_limit_bytes=vmem_limit),
        cost_estimate=pl.CostEstimate(
            flops=flops, bytes_accessed=bytes_accessed, transcendentals=transcendentals
        ),
        name=name,
    )(*[array for array, _, _ in ins])


def whole_block(array):
    return (array, array.shape, lambda *at: (0,) * array.ndim)


def project_kernel(q_cols, k_cols, x_ref, cos_ref, sin_ref, pick_ref, *refs):
    q_refs, kv_refs = refs[:4], refs[4:8]
    in_ref, q_ref, k_ref, v_ref, qp_ref, kp_ref, rows_ref, heads_ref = refs[8:]
    size = q_refs[0].shape[0]
    head_size = heads_ref.shape[1]
    step = pl.program_id(0)

    @pl.when(step == 0)
    def _():
        heads = jnp.zeros(heads_ref.shape, full)
        for at, ref in enumerate(q_refs):
            rows = ref[:, q_cols : q_cols + 128].astype(full).T[:8]
            rows_ref[:, at * size : (at + 1) * size] = rows
            heads = heads + dot(rows.astype(low), pick_ref[at * size : (at + 1) * size, :])
        heads_ref[...] = heads

    x = x_ref[...].astype(full)
    attn_in = (x * row_rms(x) * rows_ref[0:1, :]).astype(low)
    in_ref[...] = attn_in
    cosines, sines = cos_ref[...], sin_ref[...]

    def product(weights, columns):
        total = None
        for at, ref in enumerate(weights):
            term = dot(attn_in[:, at * size : (at + 1) * size], ref[:, columns])
            total = term if total is None else total + term
        return total

    def heads_of(projected, gain, proj_ref, out_ref, start):
        proj_ref[:, start : start + projected.shape[1]] = projected.astype(low)
        for column in range(0, projected.shape[1], head_size):
            head = projected[:, column : column + head_size]
            head = turn(head * row_rms(head) * gain, cosines, sines)
            out_ref[:, start + column : start + column + head_size] = head.astype(low)

    heads_of(product(kv_refs, slice(0, k_cols)), heads_ref[3:4, :], kp_ref, k_ref, 0)
    v_ref[...] = product(kv_refs, slice(k_cols, None)).astype(low)

    @pl.when(step > 0)
    def _():
        for start in range(0, q_cols, 512):
            heads_of(
                product(q_refs, slice(start, start + 512)), heads_ref[2:3, :], qp_ref, q_ref, start
            )


def project(ordered, cosines, sines, pick, q_parts, kv_parts, q_cols, k_cols, halo):
    row_count, width = ordered.shape
    own = row_count - halo
    head_size = cosines.shape[1]
    tile = lambda i: (i, 0)
    later = lambda i: (jnp.maximum(i - 1, 0), 0)
    fixed = lambda i: (0, 0)
    return call(
        functools.partial(project_kernel, q_cols, k_cols),
        "project",
        (row_count // halo,),
        [
            (ordered, (halo, width), tile),
            (cosines, (halo, head_size), tile),
            (sines, (halo, head_size), tile),
            whole_block(pick),
        ]
        + [whole_block(part) for part in q_parts + kv_parts],
        [
            ((row_count, width), low, (halo, width), tile),
            ((own, q_cols), low, (halo, q_cols), later),
            ((row_count, k_cols), low, (halo, k_cols), tile),
            ((row_count, k_cols), low, (halo, k_cols), tile),
            ((own, q_cols), low, (halo, q_cols), later),
            ((row_count, k_cols), low, (halo, k_cols), tile),
            ((8, width), full, (8, width), fixed),
            ((8, head_size), full, (8, head_size), fixed),
        ],
        2 * row_count * width * (q_cols + 2 * k_cols),
        20 << 20,
    )


def gate_kernel(xm_ref, xo_ref, *refs):
    gate_refs, up_refs = refs[:4], refs[4:8]
    act_ref, to_gate_ref, to_up_ref = refs[8:]
    gate_weight, up_weight = spread(gate_refs), spread(up_refs)
    half = xm_ref.shape[0]
    for at, ref in enumerate((xm_ref, xo_ref)):
        rows = slice(at * half, (at + 1) * half)
        gate = dot(ref[...], gate_weight)
        up = dot(ref[...], up_weight)
        sigma = 1.0 / (1.0 + jnp.exp(-gate))
        silu = gate * sigma
        act_ref[rows, :] = (silu * up).astype(low)
        to_gate_ref[rows, :] = (up * sigma * (1.0 + gate * (1.0 - sigma))).astype(low)
        to_up_ref[rows, :] = silu.astype(low)


def gate_forward(mine, other, gate_parts, up_parts, tile=256):
    half, width = mine.shape
    columns = gate_parts[0].shape[1]
    wide = lambda j: (0, j)
    return call(
        gate_kernel,
        "gate_forward",
        (columns // tile,),
        [whole_block(mine), whole_block(other)]
        + [(part, (part.shape[0], tile), wide) for part in gate_parts + up_parts],
        [((2 * half, columns), low, (2 * half, tile), wide)] * 3,
        8 * half * width * columns,
        16 << 20,
        transcendentals=2 * half * columns,
    )


def mlp_back_kernel(unit, gm_ref, go_ref, to_gate_ref, to_up_ref, *refs):
    down_refs, gate_refs, up_refs = refs[:4], refs[4:8], refs[8:12]
    gate_out, up_out, mine_out, other_out = refs[12:]
    half = gm_ref.shape[0]
    size = gate_refs[0].shape[0]
    down = jnp.concatenate([reorder(down_refs, at, unit) for at in range(4)], axis=0)

    @pl.when(pl.program_id(0) == 0)
    def _():
        mine_out[...] = jnp.zeros_like(mine_out)
        other_out[...] = jnp.zeros_like(other_out)

    for at, (ref, out) in enumerate(((gm_ref, mine_out), (go_ref, other_out))):
        rows = slice(at * half, (at + 1) * half)
        act_grad = dot(ref[...], down)
        gate_grad = (act_grad * to_gate_ref[rows, :].astype(full)).astype(low)
        up_grad = (act_grad * to_up_ref[rows, :].astype(full)).astype(low)
        gate_out[rows, :] = gate_grad
        up_out[rows, :] = up_grad
        for at, (gate_ref, up_ref) in enumerate(zip(gate_refs, up_refs)):
            out[:, at * size : (at + 1) * size] += dot(gate_grad, gate_ref[...], 1, 1) + dot(
                up_grad, up_ref[...], 1, 1
            )


def mlp_backward(
    mine, other, to_gate, to_up, down_parts, gate_parts, up_parts, unit, tile=256
):
    half, width = mine.shape
    columns = to_gate.shape[1]
    wide = lambda j: (0, j)
    fixed = lambda j: (0, 0)
    return call(
        functools.partial(mlp_back_kernel, unit),
        "mlp_backward",
        (columns // tile,),
        [whole_block(mine), whole_block(other)]
        + [(factor, (2 * half, tile), wide) for factor in (to_gate, to_up)]
        + [(part, (part.shape[0], tile), wide) for part in down_parts + gate_parts + up_parts],
        [((2 * half, columns), low, (2 * half, tile), wide)] * 2
        + [((half, width), full, (half, width), fixed)] * 2,
        12 * half * width * columns,
        30 << 20,
    )


def down_kernel(unit, act_ref, *refs):
    down_refs, out_ref = refs[:4], refs[4]
    size = down_refs[0].shape[0]
    for at in range(4):
        out_ref[:, at * size : (at + 1) * size] = dot(
            act_ref[...], reorder(down_refs, at, unit), 1, 1
        )


def down_forward(activated, start, parts, unit, rows, tile=256):
    columns = activated.shape[1]
    width = 4 * parts[0].shape[0]
    first = start // tile
    return call(
        functools.partial(down_kernel, unit),
        "down_forward",
        (rows // tile,),
        [(activated, (tile, columns), lambda i: (i + first, 0))]
        + [whole_block(part) for part in parts],
        [((rows, width), full, (tile, width), lambda i: (i, 0))],
        2 * rows * columns * width,
        8 << 20,
    )[0]


def mix_kernel(core_ref, att_ref, *refs):
    left_refs, right_refs, out_ref = refs[:4], refs[4:8], refs[8]
    size, cut = left_refs[0].shape
    for at, (left, right) in enumerate(zip(left_refs, right_refs)):
        out_ref[:, at * size : (at + 1) * size] = dot(att_ref[:, :cut], left[...], 1, 1) + dot(
            att_ref[:, cut:], right[...], 1, 1
        )


def mix_forward(which, attended, left, right, tile=256):
    rows, columns = attended.shape[0] // 2, attended.shape[1]
    width = 4 * left[0].shape[0]
    steps = rows // tile
    fixed = lambda i, core: (0, 0)
    return pl.pallas_call(
        mix_kernel,
        grid_spec=pltpu.PrefetchScalarGridSpec(
            num_scalar_prefetch=1,
            grid=(steps,),
            in_specs=[pl.BlockSpec((tile, columns), lambda i, core: (core[0] * steps + i, 0))]
            + [pl.BlockSpec(part.shape, fixed) for part in left + right],
            out_specs=pl.BlockSpec((tile, width), lambda i, core: (i, 0)),
        ),
        out_shape=jax.ShapeDtypeStruct((rows, width), full),
        compiler_params=pltpu.CompilerParams(vmem_limit_bytes=vmem_limit),
        cost_estimate=pl.CostEstimate(
            flops=2 * rows * columns * width, bytes_accessed=6 << 20, transcendentals=0
        ),
        name="mix_forward",
    )(which, attended, *left, *right)


def mix_back_kernel(branch_ref, *refs):
    left_refs, right_refs, out_ref = refs[:4], refs[4:8], refs[8]
    size, cut = left_refs[0].shape
    for columns, weights in ((slice(0, cut), left_refs), (slice(cut, None), right_refs)):
        out_ref[:, columns] = dot(branch_ref[...], spread(weights)).astype(low)


def mix_backward(branch, left, right, tile=256):
    rows, width = branch.shape
    columns = left[0].shape[1] + right[0].shape[1]
    rows_of = lambda i: (i, 0)
    return call(
        mix_back_kernel,
        "mix_backward",
        (rows // tile,),
        [(branch, (tile, width), rows_of)] + [whole_block(part) for part in left + right],
        [((rows, columns), low, (tile, columns), rows_of)],
        2 * rows * columns * width,
        6 << 20,
    )[0]


def forward_kernel(scale, rows, halo, q_ref, k_ref, v_ref, qs_ref, ks_ref, out_ref, bias_ref):
    block = pl.program_id(1)
    start = pl.multiple_of(block * rows, rows)
    window = halo + rows
    head_size = k_ref.shape[1]

    @pl.when(pl.program_id(0) == 0)
    def _():
        bias_ref[block] = score_bias(
            qs_ref[...], ks_ref[pl.ds(start, window), :], rows, halo
        )

    for (low_row, high_row), key_count in parts_of(rows, halo):
        keys = k_ref[pl.ds(start, key_count), :]
        values = v_ref[pl.ds(start, key_count), :]
        bias = bias_ref[block, :key_count, low_row:high_row]
        for group in range(q_ref.shape[1] // head_size):
            lanes = slice(group * head_size, (group + 1) * head_size)
            query = q_ref[low_row:high_row, lanes]
            scores = dot(keys, query, 1, 1) * scale + bias
            weights = jnp.exp2(scores)
            total = jnp.sum(weights, axis=0, keepdims=True)
            probs = (weights * (1.0 / total)).astype(low)
            mixed = dot(values, probs, 0, 0)
            out_ref[low_row:high_row, lanes] = mixed.T.astype(low)


def head_back(gradient, projected, gain, cosines, sines):
    scales = row_rms(projected)
    normed = projected * scales
    back = turn(gradient, cosines, -sines)
    gain_grad = jnp.sum(back * normed, axis=0, keepdims=True)
    back = back * gain
    mean = jnp.mean(back * normed, axis=1, keepdims=True)
    return scales * (back - normed * mean), gain_grad


def backward_kernel(
    scale, rows, halo, *refs
):
    q_ref, k_ref, v_ref, g_ref, qp_ref, kp_ref, cos_ref, sin_ref, heads_ref, qs_ref, ks_ref = refs[
        :11
    ]
    dq_ref, dk_ref, dv_ref, gains_ref, bias_ref, key_ref, value_ref = refs[11:]
    head = pl.program_id(0)
    block = pl.program_id(1)
    start = pl.multiple_of(block * rows, rows)
    window = halo + rows
    head_size = k_ref.shape[1]
    factor = head_size ** (-0.5)

    @pl.when(head == 0)
    def _():
        bias_ref[block] = score_bias(
            qs_ref[...], ks_ref[pl.ds(start, window), :], rows, halo
        )

    @pl.when((head == 0) & (block == 0))
    def _():
        gains_ref[...] = jnp.zeros_like(gains_ref)

    @pl.when(block == 0)
    def _():
        key_ref[...] = jnp.zeros_like(key_ref)
        value_ref[...] = jnp.zeros_like(value_ref)

    for (low_row, high_row), key_count in parts_of(rows, halo):
        keys = k_ref[pl.ds(start, key_count), :]
        values = v_ref[pl.ds(start, key_count), :]
        bias = bias_ref[block, :key_count, low_row:high_row]
        here = pl.ds(start + (halo + low_row), high_row - low_row)
        cosines, sines = cos_ref[here, :], sin_ref[here, :]
        key_sum = None
        value_sum = None
        for group in range(q_ref.shape[1] // head_size):
            lanes = slice(group * head_size, (group + 1) * head_size)
            query = q_ref[low_row:high_row, lanes]
            grad = g_ref[low_row:high_row, lanes]
            weights = jnp.exp2(dot(keys, query, 1, 1) * scale + bias)
            total = jnp.sum(weights, axis=0, keepdims=True)
            softmax = weights * (1.0 / total)
            prob_grad = dot(values, grad, 1, 1)
            product = softmax * prob_grad
            mean = jnp.sum(product, axis=0, keepdims=True)
            score_grad = (product - softmax * mean).astype(low)
            value_term = dot(softmax.astype(low), grad)
            key_term = dot(score_grad, query)
            value_sum = value_term if value_sum is None else value_sum + value_term
            key_sum = key_term if key_sum is None else key_sum + key_term
            query_grad = dot(keys, score_grad, 0, 0).T * factor
            query_grad, gain_grad = head_back(
                query_grad,
                qp_ref[low_row:high_row, lanes].astype(full),
                heads_ref[2:3, :],
                cosines,
                sines,
            )
            dq_ref[low_row:high_row, lanes] = query_grad.astype(low)
            gains_ref[0:1, :] += gain_grad
        key_ref[pl.ds(start, key_count), :] += key_sum * factor
        value_ref[pl.ds(start, key_count), :] += value_sum

    @pl.when(block == pl.num_programs(1) - 1)
    def _():
        dv_ref[...] = value_ref[...].astype(low)
        for row in range(0, k_ref.shape[0], halo):
            here = slice(row, row + halo)
            key_grad, gain_grad = head_back(
                key_ref[here, :],
                kp_ref[here, :].astype(full),
                heads_ref[3:4, :],
                cos_ref[here, :],
                sin_ref[here, :],
            )
            dk_ref[here, :] = key_grad.astype(low)
            gains_ref[1:2, :] += gain_grad


def attention_specs(rows, halo, token_count, group_lanes, head_size):
    queries = pl.BlockSpec((rows, group_lanes), lambda h, b: (b, h))
    keys = pl.BlockSpec((halo + token_count, head_size), lambda h, b: (0, h))
    query_segments = pl.BlockSpec((1, rows), lambda h, b: (0, b))
    key_segments = pl.BlockSpec((halo + token_count, 1), lambda h, b: (0, 0))
    return queries, keys, query_segments, key_segments


def attention_forward(queries, keys, values, query_segments, key_segments, rows, halo, head_size):
    token_count = queries.shape[0]
    heads = keys.shape[1] // head_size
    q_spec, k_spec, qs_spec, ks_spec = attention_specs(
        rows, halo, token_count, queries.shape[1] // heads, head_size
    )
    scale = head_size ** (-0.5) / math.log(2.0)
    return pl.pallas_call(
        functools.partial(forward_kernel, scale, rows, halo),
        grid=(heads, token_count // rows),
        in_specs=[q_spec, k_spec, k_spec, qs_spec, ks_spec],
        out_specs=q_spec,
        out_shape=jax.ShapeDtypeStruct(queries.shape, low),
        scratch_shapes=[pltpu.VMEM((token_count // rows, halo + rows, rows), full)],
        compiler_params=pltpu.CompilerParams(vmem_limit_bytes=vmem_limit),
        cost_estimate=pl.CostEstimate(
            flops=4 * queries.size * (halo + rows),
            bytes_accessed=2 * (2 * queries.size + 2 * keys.size),
            transcendentals=queries.size // head_size * (halo + rows),
        ),
        name="attention_forward",
    )(queries, keys, values, query_segments, key_segments)


def attention_backward(
    queries, keys, values, grads, query_proj, key_proj, cosines, sines, heads_gain,
    query_segments, key_segments, rows, halo, head_size,
):
    token_count = queries.shape[0]
    heads = keys.shape[1] // head_size
    lanes = queries.shape[1] // heads
    window = halo + token_count
    scale = head_size ** (-0.5) / math.log(2.0)
    q_at, k_at, fixed = lambda h, b: (b, h), lambda h, b: (0, h), lambda h, b: (0, 0)
    return call(
        functools.partial(backward_kernel, scale, rows, halo),
        "attention_backward",
        (heads, token_count // rows),
        [
            (queries, (rows, lanes), q_at),
            (keys, (window, head_size), k_at),
            (values, (window, head_size), k_at),
            (grads, (rows, lanes), q_at),
            (query_proj, (rows, lanes), q_at),
            (key_proj, (window, head_size), k_at),
            whole_block(cosines),
            whole_block(sines),
            whole_block(heads_gain),
            (query_segments, (1, rows), lambda h, b: (0, b)),
            whole_block(key_segments),
        ],
        [
            (queries.shape, low, (rows, lanes), q_at),
            (keys.shape, low, (window, head_size), k_at),
            (keys.shape, low, (window, head_size), k_at),
            ((8, head_size), full, (8, head_size), fixed),
        ],
        10 * queries.size * (halo + rows),
        24 << 20,
        scratch=[
            pltpu.VMEM((token_count // rows, halo + rows, rows), full),
            pltpu.VMEM((window, head_size), full),
            pltpu.VMEM((window, head_size), full),
        ],
        transcendentals=queries.size // head_size * (halo + rows),
    )


def per_device(
    tokens,
    segments,
    norm_gain,
    q_weight,
    k_weight,
    v_weight,
    o_weight,
    q_gain,
    k_gain,
    mlp_gain,
    gate_weight,
    up_weight,
    down_weight,
    cotangent,
):
    net = Slice()
    row_count, width = tokens.shape
    halo = row_count // 2
    chip_rows = 2 * row_count
    weight_rows = q_weight.shape[0]
    head_size = q_gain.shape[0] * net.count
    gain_rows = q_gain.shape[0]

    q_cols, k_cols, o_cols, ff_cols = (
        weight.shape[1] // 2 for weight in (q_weight, k_weight, o_weight, gate_weight)
    )
    o_cut, ff_cut = o_cols // 2, ff_cols // 2

    column = lax.broadcasted_iota(jnp.int32, (weight_rows, 128), 1)
    extras = jnp.zeros((weight_rows, 128), low)
    for at, gain in enumerate((norm_gain, mlp_gain, q_gain, k_gain)):
        gain = jnp.pad(gain, (0, weight_rows - gain.shape[0]))
        extras = jnp.where(column == at, gain[:, None], extras)

    def chip_block(weights, extra=()):
        split = [net.halves(weight, 1) for weight in weights]
        mine = jnp.concatenate([part[0] for part in split[:1]] + list(extra) + [part[0] for part in split[1:]], 1)
        other = jnp.concatenate([part[1] for part in split[:1]] + list(extra) + [part[1] for part in split[1:]], 1)
        return net.by_core(mine, net.pair(other))

    block_qkv = chip_block([q_weight, k_weight, v_weight], [extras])
    (
        block_qkv, tokens, segments, cotangent, o_weight, gate_weight, up_weight, down_weight
    ) = barrier(
        (block_qkv, tokens, segments, cotangent, o_weight, gate_weight, up_weight, down_weight)
    )
    block_down = chip_block([down_weight])
    block_o = chip_block([o_weight])
    block_mlp = chip_block([gate_weight, up_weight])

    numbers = jnp.broadcast_to(segments.astype(low)[:, None], (row_count, 128))
    both = jnp.concatenate([tokens, numbers], 1)
    both = net.by_core(both, net.pair(both))
    before = net.chip_along(both[chip_rows - halo :], 1)
    chip_tokens, before_tokens = both[:, :width], before[:, :width]
    chip_segments = both[:, width].astype(jnp.int32)
    before_segments = jnp.where(net.chip > 0, before[:, width].astype(jnp.int32), -1)
    window_tokens = jnp.concatenate([before_tokens, chip_tokens])
    window_segments = jnp.concatenate([before_segments, chip_segments])
    counter = jnp.arange(halo + chip_rows, dtype=jnp.int32)
    changes = jnp.concatenate([jnp.ones((1,), bool), window_segments[1:] != window_segments[:-1]])
    starts = lax.cummax(jnp.where(changes, counter, 0), axis=0)
    offsets = (counter - starts).astype(full)
    frequency = jnp.exp(
        (jnp.arange(head_size, dtype=jnp.int32) % (head_size // 2)).astype(full)
        * (-2.0 * math.log(rope_base) / head_size)
    )
    angles = offsets[:, None] * frequency[None, :]
    cosines = jnp.cos(angles)
    sines = jnp.sin(angles) * jnp.where(jnp.arange(head_size) < head_size // 2, -1.0, 1.0)
    query_segments = chip_segments[None, :]
    key_segments = window_segments[:, None]
    places = net.places(net.chip, 2 * weight_rows)
    order = (jnp.arange(width, dtype=jnp.int32)[:, None] == places[None, :]).astype(low)
    head_places = net.places(net.chip, 2 * gain_rows)
    head_order = (
        jnp.arange(head_size, dtype=jnp.int32)[:, None] == head_places[None, :]
    ).astype(full)
    entry = jnp.arange(width, dtype=jnp.int32)
    gain_place = places // weight_rows * gain_rows + entry % weight_rows
    pick = (
        (entry % weight_rows < gain_rows)[:, None]
        & (gain_place[:, None] == jnp.arange(head_size, dtype=jnp.int32)[None, :])
    ).astype(low)
    ordered = dot(window_tokens, order, kind=low)
    own_cotangent = dot(cotangent, order, kind=low)
    other_cotangent = net.pair(own_cotangent)
    chip_cotangent = jnp.concatenate([own_cotangent, other_cotangent])

    z_qkv = net.gather_z(block_qkv)
    down_left = net.plane_second(net.plane_first(block_down[:, :ff_cut], "x"), "y")
    down_right = net.plane_second(net.plane_first(block_down[:, ff_cut:], "y"), "x")
    z_qkv, down_left, down_right, ordered, chip_cotangent, cosines, sines = barrier(
        (z_qkv, down_left, down_right, ordered, chip_cotangent, cosines, sines)
    )
    plane_down = jnp.concatenate(
        [jnp.concatenate(down_left), jnp.concatenate(down_right)], 1
    )

    def cut_planes(blocks, cut):
        return (
            jnp.concatenate([block[:, :cut] for block in blocks]),
            jnp.concatenate([block[:, cut:] for block in blocks]),
        )

    q_left, kv_right = cut_planes(z_qkv, q_cols + 128)
    q_left = net.plane_first(q_left, "y")
    kv_right = net.plane_first(kv_right, "x")
    z_o = net.gather_z(block_o)
    q_left, kv_right, z_o = barrier((q_left, kv_right, z_o))

    q_left = net.plane_second(q_left, "x")
    kv_right = net.plane_second(kv_right, "y")
    o_left, o_right = cut_planes(z_o, o_cut)
    o_left = net.plane_first(o_left, "y")
    o_right = net.plane_first(o_right, "x")
    z_mlp = net.gather_z(block_mlp, 2)
    q_left, kv_right, o_left, o_right, z_mlp = barrier((q_left, kv_right, o_left, o_right, z_mlp))

    o_left = net.plane_second(o_left, "x")
    o_right = net.plane_second(o_right, "y")
    z_mlp = z_mlp + [net.ring(z_mlp[-1], 1)]
    q_parts, kv_parts = net.quarters(q_left), net.quarters(kv_right)
    attn_in, queries, keys, values, query_proj, key_proj, gain_rows_full, heads_gain = project(
        ordered, cosines, sines, pick, q_parts, kv_parts, q_cols, k_cols, halo
    )
    queries, keys, values, o_left, o_right, z_mlp = barrier(
        (queries, keys, values, o_left, o_right, z_mlp)
    )
    gain_one, gain_two = gain_rows_full[0], gain_rows_full[1]

    gate_left, up_right = cut_planes(z_mlp, ff_cols)
    gate_left = net.plane_first(gate_left, "y")
    up_right = net.plane_first(up_right, "x")
    z_down = net.gather_z(plane_down, 1)
    attended = attention_forward(
        queries, keys, values, query_segments, key_segments, row_count, halo, head_size
    )
    attended, gate_left, up_right, z_down = barrier((attended, gate_left, up_right, z_down))

    gate_left = net.plane_second(gate_left, "x")
    up_right = net.plane_second(up_right, "y")
    z_down = z_down[:1] + net.gather_z(z_down[1], 2)
    own_inputs = lax.dynamic_slice_in_dim(ordered, halo + net.core * row_count, row_count).astype(
        full
    )
    o_left, o_right = net.quarters(o_left), net.quarters(o_right)
    which = net.core.astype(jnp.int32).reshape(1)
    branch_sent = net.pair(mix_forward(1 - which, attended, o_left, o_right))
    hidden_state = own_inputs + (mix_forward(which, attended, o_left, o_right) + branch_sent)
    scale_two = inverse_rms(hidden_state)
    normed_two = hidden_state * scale_two
    mlp_own = (normed_two * gain_two).astype(low)
    mlp_other = net.pair(mlp_own)
    mlp_own, mlp_other, gate_left, up_right, z_down = barrier(
        (mlp_own, mlp_other, gate_left, up_right, z_down)
    )

    unit = block_down.shape[0]
    gate_parts, up_parts = net.quarters(gate_left), net.quarters(up_right)
    activated, to_gate, to_up = gate_forward(mlp_own, mlp_other, gate_parts, up_parts)
    mlp_in = jnp.concatenate([mlp_own, mlp_other])
    down_grad = dot(chip_cotangent, activated, 0, 0, low)
    activated, to_gate, to_up, mlp_in, down_grad, z_down = barrier(
        (activated, to_gate, to_up, mlp_in, down_grad, z_down)
    )

    down_a, down_b = net.pieces(down_grad[:, :ff_cut]), net.pieces(down_grad[:, ff_cut:])
    down_a_in = net.scatter_send(down_a, "x")
    down_b_in = net.scatter_send(down_b, "y")
    gate_grad, up_grad, mlp_grad_mine, mlp_grad_other = mlp_backward(
        own_cotangent, other_cotangent, to_gate, to_up, z_down, gate_parts, up_parts, unit
    )
    gate_w_grad = dot(mlp_in, gate_grad, 0, 0, low)
    up_w_grad = dot(mlp_in, up_grad, 0, 0, low)
    mlp_grad_mine, mlp_grad_other, gate_w_grad, up_w_grad, down_a_in, down_b_in = barrier(
        (mlp_grad_mine, mlp_grad_other, gate_w_grad, up_w_grad, down_a_in, down_b_in)
    )

    gate_p, up_p = net.pieces(gate_w_grad), net.pieces(up_w_grad)
    gate_p_in = net.scatter_send(gate_p, "x")
    up_p_in = net.scatter_send(up_p, "y")
    down_a = net.scatter_add(down_a, down_a_in)
    down_b = net.scatter_add(down_b, down_b_in)
    mlp_in_grad = mlp_grad_mine + net.pair(mlp_grad_other)
    hidden_grad = own_cotangent.astype(full) + norm_back(
        mlp_in_grad * gain_two, normed_two, scale_two
    )
    branch_own = hidden_grad.astype(low)
    branch_low = net.by_core(branch_own, net.pair(branch_own))
    attended_grad = mix_backward(branch_low, o_left, o_right)
    o_w_grad = dot(branch_low, attended, 0, 0, low)
    attended_grad, o_w_grad, mlp_in_grad, gate_p_in, up_p_in, down_a, down_b = barrier(
        (attended_grad, o_w_grad, mlp_in_grad, gate_p_in, up_p_in, down_a, down_b)
    )

    gate_p = net.scatter_add(gate_p, gate_p_in)
    up_p = net.scatter_add(up_p, up_p_in)
    down_a_in = net.scatter_send(down_a, "y")
    down_b_in = net.scatter_send(down_b, "x")
    gate_p_in = net.scatter_send(gate_p, "y")
    up_p_in = net.scatter_send(up_p, "x")
    query_low, key_low, value_low, gain_grads = attention_backward(
        queries, keys, values, attended_grad, query_proj, key_proj, cosines, sines, heads_gain,
        query_segments, key_segments, row_count, halo, head_size,
    )
    query_low, key_low, value_low, down_a_in, down_b_in, gate_p_in, up_p_in = barrier(
        (query_low, key_low, value_low, down_a_in, down_b_in, gate_p_in, up_p_in)
    )

    o_a, o_b = net.pieces(o_w_grad[:, :o_cut]), net.pieces(o_w_grad[:, o_cut:])
    o_a_in = net.scatter_send(o_a, "x")
    o_b_in = net.scatter_send(o_b, "y")
    down_a = net.scatter_add(down_a, down_a_in)[(0, 0)]
    down_b = net.scatter_add(down_b, down_b_in)[(0, 0)]
    z_down_in = net.scatter_z(jnp.concatenate([down_a, down_b], 1))
    kv_low = jnp.concatenate([key_low, value_low], axis=1)
    q_w_grad = dot(attn_in[halo:], query_low, 0, 0, low)
    kv_w_grad = dot(attn_in, kv_low, 0, 0, low)
    query_low, kv_low, q_w_grad, kv_w_grad, o_a_in, o_b_in, z_down_in = barrier(
        (query_low, kv_low, q_w_grad, kv_w_grad, o_a_in, o_b_in, z_down_in)
    )

    q_p, kv_p = net.pieces(q_w_grad), net.pieces(kv_w_grad)
    q_p_in = net.scatter_send(q_p, "x")
    kv_p_in = net.scatter_send(kv_p, "y")
    o_a = net.scatter_add(o_a, o_a_in)
    o_b = net.scatter_add(o_b, o_b_in)
    o_a_in = net.scatter_send(o_a, "y")
    o_b_in = net.scatter_send(o_b, "x")
    gate_p = net.scatter_add(gate_p, gate_p_in)[(0, 0)]
    up_p = net.scatter_add(up_p, up_p_in)[(0, 0)]
    z_mlp_in = net.scatter_z(jnp.concatenate([gate_p, up_p], 1))
    q_full = jnp.concatenate([part[:, :q_cols] for part in q_parts])
    kv_full = jnp.concatenate(kv_parts)
    scale_one = inverse_rms(own_inputs)
    normed_one = own_inputs * scale_one
    before_grad = net.chip_along(dot(kv_low[:halo], kv_full, 1, 1, low), -1)
    next_places = net.places(net.chip + 1, 2 * weight_rows)
    next_order = (next_places[:, None] == places[None, :]).astype(low)
    before_grad = dot(before_grad, next_order)
    chip_grad = dot(query_low, q_full, 1, 1) + dot(kv_low[halo:], kv_full, 1, 1)
    chip_grad = jnp.concatenate(
        [chip_grad[: chip_rows - halo], chip_grad[chip_rows - halo :] + before_grad]
    )
    grad_mine, grad_other = net.halves(chip_grad)
    attn_in_grad = grad_mine + net.pair(grad_other)
    gain_one_grad = jnp.sum(attn_in_grad * normed_one, axis=0)
    gain_two_grad = jnp.sum(mlp_in_grad * normed_two, axis=0)
    input_grad = (hidden_grad + norm_back(attn_in_grad * gain_one, normed_one, scale_one)).astype(
        low
    )
    input_grad = dot(input_grad, order, 1, 1, low)
    q_p_in, kv_p_in, o_a_in, o_b_in, z_mlp_in, input_grad, gain_one_grad = barrier(
        (q_p_in, kv_p_in, o_a_in, o_b_in, z_mlp_in, input_grad, gain_one_grad)
    )

    def head_sum(gradient):
        return jnp.sum(head_order * gradient[:, None], axis=0).reshape(net.chips, 2, gain_rows)

    gain_sum = jnp.concatenate(
        [
            gain_one_grad.reshape(net.chips, 2, weight_rows),
            gain_two_grad.reshape(net.chips, 2, weight_rows),
            head_sum(gain_grads[0]),
            head_sum(gain_grads[1]),
        ],
        axis=2,
    )
    gain_p = net.pieces(gain_sum)
    gain_p = net.scatter_add(gain_p, net.scatter_send(gain_p, "x"))
    q_p = net.scatter_add(q_p, q_p_in)
    kv_p = net.scatter_add(kv_p, kv_p_in)
    q_p_in = net.scatter_send(q_p, "y")
    kv_p_in = net.scatter_send(kv_p, "x")
    o_a = net.scatter_add(o_a, o_a_in)[(0, 0)]
    o_b = net.scatter_add(o_b, o_b_in)[(0, 0)]
    z_o_in = net.scatter_z(jnp.concatenate([o_a, o_b], 1))

    def total(blocks):
        return sum([block.astype(full) for block in blocks[1:]], blocks[0].astype(full))

    down_out = net.finish(total(z_down_in))
    mlp_sum = total(z_mlp_in)
    gate_out = net.finish(mlp_sum[:, :ff_cols])
    up_out = net.finish(mlp_sum[:, ff_cols:])
    out_sent = net.pair(down_forward(activated, row_count, z_down, unit, row_count))
    mixed_out = hidden_state + (down_forward(activated, 0, z_down, unit, row_count) + out_sent)
    mixed_out = mixed_out.astype(low)
    mixed_out = dot(mixed_out, order, 1, 1, low)
    q_p_in, kv_p_in, z_o_in, gain_p, down_out, gate_out, up_out, mixed_out = barrier(
        (q_p_in, kv_p_in, z_o_in, gain_p, down_out, gate_out, up_out, mixed_out)
    )

    gain_p = net.scatter_add(gain_p, net.scatter_send(gain_p, "y"))
    gain_sum = total(net.scatter_z(gain_p[(0, 0)])).reshape(2, -1)
    gain_mine, gain_other = net.halves(gain_sum)
    gain_sum = (gain_mine + net.pair(gain_other))[0]
    q_p = net.scatter_add(q_p, q_p_in)[(0, 0)]
    kv_p = net.scatter_add(kv_p, kv_p_in)[(0, 0)]
    qkv_sum = total(net.scatter_z(jnp.concatenate([q_p, kv_p], 1)))
    o_out = net.finish(total(z_o_in))
    return (
        mixed_out,
        input_grad,
        gain_sum[:weight_rows],
        net.finish(qkv_sum[:, :q_cols]),
        net.finish(qkv_sum[:, q_cols : q_cols + k_cols]),
        net.finish(qkv_sum[:, q_cols + k_cols :]),
        o_out,
        gain_sum[2 * weight_rows : 2 * weight_rows + gain_rows],
        gain_sum[2 * weight_rows + gain_rows :],
        gain_sum[weight_rows : 2 * weight_rows],
        gate_out,
        up_out,
        down_out,
    )


def solution(mesh):
    rows = P("dp", None)
    line = P("dp")
    return jax.shard_map(
        per_device,
        mesh=mesh,
        in_specs=(
            rows, line, line, rows, rows, rows, rows, line, line, line, rows, rows, rows, rows,
        ),
        out_specs=(
            rows, rows, line, rows, rows, rows, rows, line, line, line, rows, rows, rows,
        ),
        check_vma=False,
    )
```

time: 682 us -> 561 us (0.82)
  matrix products: 125 us -> 47.7 us
  Pallas kernels: 43.5 us -> 108 us
  waiting for transfers between devices: 259 us -> 207 us
  local copies, waits for them, and re-layouts: 58.9 us -> 35.7 us
  starting transfers between devices: 116 us -> 97.4 us
  other arithmetic: 67.9 us -> 51.7 us
    dot_general x27 -> x14, matrix products: 125 us -> 47.7 us  [dot(): lax.dot_general(left_side, right_side, (((left_dim,), (right_dim,)), ((),...]
    pallas_call x1 -> x9, Pallas kernels: 26 us -> 90.6 us  [the longest x7 84.1 us: call(): pl.pallas_call(kernel, grid=grid, in_specs=[pl.BlockSpec(block, index) fo...]
    ppermute x51 -> x27, waiting for transfers between devices: 132 us -> 96.2 us  [ring(): lax.ppermute(array, 'dp', [(i, (i + step) % self.count) for i in range(se...]
    ppermute x72 -> x71, waiting for transfers between devices: 125 us -> 101 us  [flip(): return lax.ppermute(array, 'dp', [(i, i ^ mask) for i in range(self.count)])]
    ppermute x51 -> x27, starting transfers between devices: 45.9 us -> 29.8 us  [ring(): lax.ppermute(array, 'dp', [(i, (i + step) % self.count) for i in range(se...]
    convert_element_type x17 -> x16, other arithmetic: 7.49 us -> 20 us  [the longest x13 18.7 us: scatter_add(): sum([term.astype(full) for term in terms], current[key].astype(full))]
    reshape x3 -> x0, local copies, waits for them, and re-layouts: 12.3 us -> none  [the longest x1 5.43 us: per_device(): query_grad.reshape(query_proj.shape)]
    mul x6 -> x1, local copies, waits for them, and re-layouts: 9.18 us -> 0.01 us  [head_sum(): head_order * gradient[:, None]]
  transfers between devices with their start and end apart: 126 -> 100, of which waited for: 61 -> 33; matrix products, arithmetic and copies ran while one was open for 26% -> 18% of each run, Pallas kernels for 3% -> 17%
where the time goes in v2:
time: 561 us; the launch traced here: 551 us
  waiting for transfers between devices  207 us (37%)
  Pallas kernels  108 us (19%)
  starting transfers between devices  97.4 us (17%)
  other arithmetic  51.7 us (9%)
  matrix products  47.7 us (9%)
  local copies, waits for them, and re-layouts  35.7 us (6%)
    ppermute x71, waiting for transfers between devices, flip(): return lax.ppermute(array, 'dp', [(i, i ^ mask) for i in range(self.count)])  101 us
    ppermute x27, waiting for transfers between devices, ring(): lax.ppermute(array, 'dp', [(i, (i + step) % self.count) for i in range(se...  96.2 us
    pallas_call x7, Pallas kernels, call(): pl.pallas_call(kernel, grid=grid, in_specs=[pl.BlockSpec(block, index) fo...  84.1 us
    ppermute x71, starting transfers between devices, flip(): return lax.ppermute(array, 'dp', [(i, i ^ mask) for i in range(self.count)])  62.6 us
    dot_general x14, matrix products, dot(): lax.dot_general(left_side, right_side, (((left_dim,), (right_dim,)), ((),...  47.7 us
    ppermute x27, starting transfers between devices, ring(): lax.ppermute(array, 'dp', [(i, (i + step) % self.count) for i in range(se...  29.8 us
    convert_element_type x13, other arithmetic, scatter_add(): sum([term.astype(full) for term in terms], current[key].astype(full))  18.7 us
    pallas_call x1, Pallas kernels, attention_forward(): pl.pallas_call(functools.partial(forward_kernel, scale, rows, halo), grid...  17.7 us
  transfers between devices with their start and end apart: 100, of which 33 were waited for; matrix products, arithmetic and copies ran while one was open for 18% of the time, Pallas kernels for 17%

profile of v2, /device:TPU:0, one launch (start us, length us, event | category | flops | bytes accessed | tf_op | source)
XLA Modules:
  0.0 550.8 jit_solution(4697897763214725017)
XLA Ops:
  9.7 2.7 collective-permute-start.1
  14.6 4.6 maximum_select_fusion
  19.3 3.4 collective-permute-start.12
  30.0 11.0 %collective-permute-done.9 = bf16[64,768]{1,0:T(8,128)(2,1)} collective-permute-done((bf16[64,768]{1,0:T(8,128)(2,1)S(1)}, bf16[64,768]{1,0:T(8,128)(2,1)}, u32[]{:S(2)}, u32[]{:S(2)}) %collective-permute-start.9) | collective-permute-done | bytes 98336 | tf_op jit(solution)/shard_map/ppermute | solution.py:57
  43.0 2.6 collective-permute-start.7
  49.2 4.3 fusion.3.x_ref
  64.8 13.3 %collective-permute-done.17 = bf16[64,1024]{1,0:T(8,128)(2,1)S(1)} collective-permute-done((bf16[64,1024]{1,0:T(8,128)(2,1)S(1)}, bf16[64,1024]{1,0:T(8,128)(2,1)S(1)}, u32[]{:S(2)}, u32[]{:S(2)}) %collective-permute-start.17) | collective-permute-done | bytes 131104 | tf_op jit(solution)/shard_map/ppermute | solution.py:61
  78.0 6.8 %collective-permute-done.18 = bf16[64,1024]{1,0:T(8,128)(2,1)S(1)} collective-permute-done((bf16[64,1024]{1,0:T(8,128)(2,1)S(1)}, bf16[64,1024]{1,0:T(8,128)(2,1)S(1)}, u32[]{:S(2)}, u32[]{:S(2)}) %collective-permute-start.18) | collective-permute-done | bytes 131104 | tf_op jit(solution)/shard_map/ppermute | solution.py:61
  85.0 8.0 %collective-permute-done.19 = bf16[64,1024]{1,0:T(8,128)(2,1)S(1)} collective-permute-done((bf16[64,1024]{1,0:T(8,128)(2,1)S(1)}, bf16[64,1024]{1,0:T(8,128)(2,1)S(1)}, u32[]{:S(2)}, u32[]{:S(2)}) %collective-permute-start.19) | collective-permute-done | bytes 131104 | tf_op jit(solution)/shard_map/ppermute | solution.py:61
  99.1 3.3 collective-permute-done.25.refs_5_
  104.5 18.8 %collective-permute-done.24.refs_2_ = bf16[256,512]{1,0:T(8,128)(2,1)S(1)} collective-permute-done((bf16[256,512]{1,0:T(8,128)(2,1)S(1)}, bf16[256,512]{1,0:T(8,128)(2,1)S(1)}, u32[]{:S(2)}, u32[]{:S(2)}) %collective-permute-start.24) | collective-permute-done | bytes 262176 | tf_op jit(solution)/shard_map/ppermute | solution.py:57
  129.0 11.2 %project.1 = (bf16[1280,1024]{1,0:T(8,128)(2,1)}, bf16[1024,1024]{1,0:T(8,128)(2,1)}, bf16[1280,512]{1,0:T(8,128)(2,1)}, bf16[1280,512]{1,0:T(8,128)(2,1)}, bf16...) custom-call(bf16[1280,1024]{1,0:T(8,128)(2,1)} %fusion.3.x_ref, ...), custom_call_target="tpu_custom_call" | custom-call | flops 5368709120 | bytes 20971520 | tf_op jit(solution)/shard_map/project/pallas_call | solution.py:196
  143.5 17.7 %attention_forward.1.att_ref = bf16[1024,1024]{1,0:T(8,128)(2,1)S(1)} custom-call(bf16[1024,1024]{1,0:T(8,128)(2,1)} %get-tuple-element.227.q_ref.refs_0_, bf16[1280,512]{1,0:T(8,128)(2,1)S(1)} %copy-done.54, bf16[1280,512]{1,0:T(8,128)(2,1)S(1)} %copy-done.56, s32[1,1024]{1,0:T(1,128)S(1)} %bitcast.46, s32[1280,1]{1,0:T(8,128)S(1)} %broadcast_in_dim.83.ks_ref.refs_10_), custom_call_target="tpu_custom_call" | custom-call | flops 3221225472 | bytes 6815744 | tf_op jit(solution)/shard_map/attention_forward/pallas_call | solution.py:585
  162.6 4.0 mix_forward.3
  171.6 2.5 mix_forward.2
  180.8 7.9 %collective-permute-done.43.refs_2_ = bf16[256,1536]{1,0:T(8,128)(2,1)S(1)} collective-permute-done((bf16[256,1536]{1,0:T(8,128)(2,1)S(1)}, bf16[256,1536]{1,0:T(8,128)(2,1)S(1)}, u32[]{:S(2)}, u32[]{:S(2)}) %collective-permute-start.43) | collective-permute-done | bytes 786464 | tf_op jit(solution)/shard_map/ppermute | solution.py:61
  190.1 2.5 collective-permute-start.44
  192.6 11.1 %collective-permute-done.40.refs_3_.refs_7_ = bf16[256,1536]{1,0:T(8,128)(2,1)S(1)} collective-permute-done((bf16[256,1536]{1,0:T(8,128)(2,1)S(1)}, bf16[256,1536]{1,0:T(8,128)(2,1)S(1)}, u32[]{:S(2)}, u32[]{:S(2)}) %collective-permute-start.40) | collective-permute-done | bytes 786464 | tf_op jit(solution)/shard_map/ppermute | solution.py:57
  203.7 11.8 %collective-permute-done.42.refs_7_.refs_11_ = bf16[256,1536]{1,0:T(8,128)(2,1)S(1)} collective-permute-done((bf16[256,1536]{1,0:T(8,128)(2,1)S(1)}, bf16[256,1536]{1,0:T(8,128)(2,1)S(1)}, u32[]{:S(2)}, u32[]{:S(2)}) %collective-permute-start.42) | collective-permute-done | bytes 786464 | tf_op jit(solution)/shard_map/ppermute | solution.py:57
  218.2 12.6 %gate_forward.1 = (bf16[1024,1536]{1,0:T(8,128)(2,1)}, bf16[1024,1536]{1,0:T(8,128)(2,1)}, bf16[1024,1536]{1,0:T(8,128)(2,1)}) custom-call(bf16[512,1024]{1,0:T(8,128)(2,1)} %copy-done.63, bf16[512,1024]{1,0:T(8,128)(2,1)} %copy-done.83, bf16[256,1536]{1,0:T(8,128)(2,1)S(1)} %copy-done.30, bf16[256,1536]{1,0:T(8,128)(2,1)S(1)} %collective-permute-done.39.refs_1_.refs_5_, ...), custom_call_target="tpu_custom_call" | custom-call | flops 6442450944 | bytes 16777216 | tf_op jit(solution)/shard_map/gate_forward/pallas_call | solution.py:196
  230.7 5.6 %fusion.147 = bf16[1024,1536]{1,0:T(8,128)(2,1)S(1)} fusion(bf16[1024,1024]{1,0:T(8,128)(2,1)S(1)} %copy-done.71, bf16[1024,1536]{1,0:T(8,128)(2,1)} %get-tuple-element.343.act_ref), kind=kOutput, calls=%fused_computation.357 | convolution fusion | flops 3221225472 | bytes 8388608 | tf_op jit(solution)/shard_map/dot_general | solution.py:20
  240.6 18.7 %mlp_backward.1 = (bf16[1024,1536]{1,0:T(8,128)(2,1)}, bf16[1024,1536]{1,0:T(8,128)(2,1)}, f32[512,1024]{1,0:T(8,128)}, f32[512,1024]{1,0:T(8,128)}) custom-call(bf16[512,1024]{1,0:T(8,128)(2,1)} %copy-done.64, bf16[512,1024]{1,0:T(8,128)(2,1)} %copy-done.82, bf16[1024,1536]{1,0:T(8,128)(2,1)} %get-tuple-element.276.to_gate_ref, ...), custom_call_target="tpu_custom_call" | custom-call | flops 9663676416 | bytes 31457280 | tf_op jit(solution)/shard_map/mlp_backward/pallas_call | solution.py:196
  259.3 6.9 %fusion.149 = bf16[1024,1536]{1,0:T(8,128)(2,1)} fusion(bf16[1024,1024]{1,0:T(8,128)(2,1)S(1)} %copy-done.77, bf16[1024,1536]{1,0:T(8,128)(2,1)} %get-tuple-element.286), kind=kOutput, calls=%fused_computation.359 | convolution fusion | flops 3221225472 | bytes 8388608 | tf_op jit(solution)/shard_map/dot_general | solution.py:20
  266.2 5.0 fusion.148
  276.9 3.2 down_forward.3
  280.5 3.6 down_forward.2
  294.9 2.8 add_convert_fusion.16
  298.2 3.9 fusion
  304.7 4.4 mix_backward.1.refs_3_
  309.1 4.7 fusion.150
  313.9 8.2 %collective-permute-done.52 = bf16[256,1536]{1,0:T(8,128)(2,1)} collective-permute-done((bf16[256,1536]{1,0:T(8,128)(2,1)}, bf16[256,1536]{1,0:T(8,128)(2,1)}, u32[]{:S(2)}, u32[]{:S(2)}) %collective-permute-start.52) | collective-permute-done | bytes 786464 | tf_op jit(solution)/shard_map/ppermute | solution.py:57
  322.0 7.5 %collective-permute-done.54 = bf16[256,1536]{1,0:T(8,128)(2,1)} collective-permute-done((bf16[256,1536]{1,0:T(8,128)(2,1)}, bf16[256,1536]{1,0:T(8,128)(2,1)}, u32[]{:S(2)}, u32[]{:S(2)}) %collective-permute-start.54) | collective-permute-done | bytes 786464 | tf_op jit(solution)/shard_map/ppermute | solution.py:57
  340.3 30.4 %attention_backward.1 = (bf16[1024,1024]{1,0:T(8,128)(2,1)}, bf16[1280,512]{1,0:T(8,128)(2,1)S(1)}, bf16[1280,512]{1,0:T(8,128)(2,1)S(1)}, f32[8,128]{1,0:T(8,128)S(1)}) custom-call(bf16[1024,1024]{1,0:T(8,128)(2,1)} %get-tuple-element.227.q_ref.refs_0_, bf16[1280,512]{1,0:T(8,128)(2,1)S(1)} %copy-done.55, ...), custom_call_target="tpu_custom_call" | custom-call | flops 8053063680 | bytes 25165824 | tf_op jit(solution)/shard_map/attention_backward/pallas_call | solution.py:196
  378.0 3.9 collective-permute-start.63
  382.3 3.2 fusion.151
  395.0 7.8 %collective-permute-done.64 = bf16[64,1536]{1,0:T(8,128)(2,1)S(1)} collective-permute-done((bf16[64,1536]{1,0:T(8,128)(2,1)S(1)}, bf16[64,1536]{1,0:T(8,128)(2,1)S(1)}, u32[]{:S(2)}, u32[]{:S(2)}) %collective-permute-start.64) | collective-permute-done | bytes 196640 | tf_op jit(solution)/shard_map/ppermute | solution.py:61
  410.4 9.5 %collective-permute-done.75 = bf16[256,1024]{1,0:T(8,128)(2,1)S(1)} collective-permute-done((bf16[256,1024]{1,0:T(8,128)(2,1)S(1)}, bf16[256,1024]{1,0:T(8,128)(2,1)S(1)}, u32[]{:S(2)}, u32[]{:S(2)}) %collective-permute-start.75) | collective-permute-done | bytes 524320 | tf_op jit(solution)/shard_map/ppermute | solution.py:67
  428.3 2.8 collective-permute-start.71
  433.4 3.1 collective-permute-start.66
  436.5 22.4 %collective-permute-done.73 = bf16[64,3072]{1,0:T(8,128)(2,1)S(1)} collective-permute-done((bf16[64,3072]{1,0:T(8,128)(2,1)S(1)}, bf16[64,3072]{1,0:T(8,128)(2,1)S(1)}, u32[]{:S(2)}, u32[]{:S(2)}) %collective-permute-start.73) | collective-permute-done | bytes 393248 | tf_op jit(solution)/shard_map/ppermute | solution.py:61
  461.1 3.9 fusion.1
  465.0 7.4 %collective-permute-done.67 = bf16[256,1024]{1,0:T(8,128)(2,1)S(1)} collective-permute-done((bf16[256,1024]{1,0:T(8,128)(2,1)S(1)}, bf16[256,1024]{1,0:T(8,128)(2,1)S(1)}, u32[]{:S(2)}, u32[]{:S(2)}) %collective-permute-start.67) | collective-permute-done | bytes 524320 | tf_op jit(solution)/shard_map/ppermute | solution.py:57
  473.8 10.2 %collective-permute-done.69 = bf16[256,1024]{1,0:T(8,128)(2,1)S(1)} collective-permute-done((bf16[256,1024]{1,0:T(8,128)(2,1)S(1)}, bf16[256,1024]{1,0:T(8,128)(2,1)S(1)}, u32[]{:S(2)}, u32[]{:S(2)}) %collective-permute-start.69) | collective-permute-done | bytes 524320 | tf_op jit(solution)/shard_map/ppermute | solution.py:57
  494.3 3.2 collective-permute-done.82
  505.1 3.0 collective-permute-done.81
  517.7 3.2 collective-permute-done.90
  526.9 5.6 %collective-permute-done.93 = bf16[64,2048]{1,0:T(8,128)(2,1)S(1)} collective-permute-done((bf16[64,2048]{1,0:T(8,128)(2,1)S(1)}, bf16[64,2048]{1,0:T(8,128)(2,1)S(1)}, u32[]{:S(2)}, u32[]{:S(2)}) %collective-permute-start.93) | collective-permute-done | bytes 262176 | tf_op jit(solution)/shard_map/ppermute | solution.py:61
  532.5 14.2 %collective-permute-done.94 = bf16[64,2048]{1,0:T(8,128)(2,1)S(1)} collective-permute-done((bf16[64,2048]{1,0:T(8,128)(2,1)S(1)}, bf16[64,2048]{1,0:T(8,128)(2,1)S(1)}, u32[]{:S(2)}, u32[]{:S(2)}) %collective-permute-start.94) | collective-permute-done | bytes 262176 | tf_op jit(solution)/shard_map/ppermute | solution.py:61
  (576 shorter events, 178.8 us)
Async XLA Ops:
  9.0 17.3 %collective-permute-start.13 = (bf16[512,1024]{1,0:T(8,128)(2,1)S(1)}, bf16[512,1024]{1,0:T(8,128)(2,1)S(1)}, u32[]{:S(2)}, u32[]{:S(2)}) collective-permute-start(bf16[512,1024]{1,0:T(8,128)(2,1)S(1)} %fusion.2.gm_ref), channel_id=1, source_target_pairs={{0,1},{1,0},{2,3},{3,2},{4,5},{5,4},{6,7},{7,6},{8,9},{9,8},{10,11... | collective-permute-start | bytes 3145736 | tf_op jit(solution)/shard_map/ppermute | solution.py:57
  19.3 26.3 %collective-permute-start.12 = (bf16[256,1152]{1,0:T(8,128)(2,1)S(1)}, bf16[256,1152]{1,0:T(8,128)(2,1)S(1)}, u32[]{:S(2)}, u32[]{:S(2)}) collective-permute-start(bf16[256,1152]{1,0:T(8,128)(2,1)S(1)} %slice.267), channel_id=1, source_target_pairs={{0,2},{1,3},{2,4},{3,5},{4,6},{5,7},{6,8},{7,9},{8,10},{9,11},{10,... | collective-permute-start | bytes 1769480 | tf_op jit(solution)/shard_map/ppermute | solution.py:67
  22.8 18.2 %collective-permute-start.5 = (bf16[64,768]{1,0:T(8,128)(2,1)S(1)}, bf16[64,768]{1,0:T(8,128)(2,1)}, u32[]{:S(2)}, u32[]{:S(2)}) collective-permute-start(bf16[64,768]{1,0:T(8,128)(2,1)S(1)} %get-tuple-element.234), channel_id=1, source_target_pairs={{0,2},{1,3},{2,0},{3,1},{4,6},{5,7},{6,4},{7,5},{8,10},{9,11},{10,... | collective-permute-start | bytes 294920 | tf_op jit(solution)/shard_map/ppermute | solution.py:57
  24.3 31.5 %collective-permute-start.6 = (bf16[64,768]{1,0:T(8,128)(2,1)S(1)}, bf16[64,768]{1,0:T(8,128)(2,1)}, u32[]{:S(2)}, u32[]{:S(2)}) collective-permute-start(bf16[64,768]{1,0:T(8,128)(2,1)S(1)} %get-tuple-element.234), channel_id=1, source_target_pairs={{0,4},{1,5},{2,6},{3,7},{4,0},{5,1},{6,2},{7,3},{8,12},{9,13},{10,... | collective-permute-start | bytes 294920 | tf_op jit(solution)/shard_map/ppermute | solution.py:57
  60.5 32.5 %collective-permute-start.15 = (bf16[256,1024]{1,0:T(8,128)(2,1)S(1)}, bf16[256,1024]{1,0:T(8,128)(2,1)S(1)}, u32[]{:S(2)}, u32[]{:S(2)}) collective-permute-start(bf16[256,1024]{1,0:T(8,128)(2,1)S(1)} %pad_maximum_fusion.6.refs_4_), channel_id=1, source_target_pairs={{0,2},{1,3},{2,0},{3,1},{4,6},{5,7},{6,4},{7,5},{8,10},{9,11},{10,... | collective-permute-start | bytes 1572872 | tf_op jit(solution)/shard_map/ppermute | solution.py:57
  61.0 32.1 %collective-permute-start.14 = (bf16[256,1152]{1,0:T(8,128)(2,1)S(1)}, bf16[256,1152]{1,0:T(8,128)(2,1)S(1)}, u32[]{:S(2)}, u32[]{:S(2)}) collective-permute-start(bf16[256,1152]{1,0:T(8,128)(2,1)S(1)} %pad_maximum_fusion.5.refs_0_), channel_id=1, source_target_pairs={{0,4},{1,5},{2,6},{3,7},{4,0},{5,1},{6,2},{7,3},{8,12},{9,13},{10,... | collective-permute-start | bytes 1769480 | tf_op jit(solution)/shard_map/ppermute | solution.py:57
  62.3 22.5 %collective-permute-start.27 = (bf16[64,3072]{1,0:T(8,128)(2,1)S(1)}, bf16[64,3072]{1,0:T(8,128)(2,1)S(1)}, u32[]{:S(2)}, u32[]{:S(2)}) collective-permute-start(bf16[64,3072]{1,0:T(8,128)(2,1)S(1)} %maximum_select_fusion.2), channel_id=1, source_target_pairs={{0,8},{1,9},{2,10},{3,11},{4,12},{5,13},{6,14},{7,15},{8,16},{9,17... | collective-permute-start | bytes 1179656 | tf_op jit(solution)/shard_map/ppermute | solution.py:61
  95.0 28.4 %collective-permute-start.20 = (bf16[256,1152]{1,0:T(8,128)(2,1)S(1)}, bf16[256,1152]{1,0:T(8,128)(2,1)S(1)}, u32[]{:S(2)}, u32[]{:S(2)}) collective-permute-start(bf16[256,1152]{1,0:T(8,128)(2,1)S(1)} %pad_maximum_fusion.5.refs_0_), channel_id=1, source_target_pairs={{0,2},{1,3},{2,0},{3,1},{4,6},{5,7},{6,4},{7,5},{8,10},{9,11},{10,... | collective-permute-start | bytes 1769480 | tf_op jit(solution)/shard_map/ppermute | solution.py:57
  95.3 29.6 %collective-permute-start.21 = (bf16[256,1152]{1,0:T(8,128)(2,1)S(1)}, bf16[256,1152]{1,0:T(8,128)(2,1)S(1)}, u32[]{:S(2)}, u32[]{:S(2)}) collective-permute-start(bf16[256,1152]{1,0:T(8,128)(2,1)S(1)} %collective-permute-done.14.refs_2_), channel_id=1, source_target_pairs={{0,2},{1,3},{2,0},{3,1},{4,6},{5,7},{6,4},{7,5},{8,10},{9,11},{10,... | collective-permute-start | bytes 1769480 | tf_op jit(solution)/shard_map/ppermute | solution.py:57
  97.1 26.3 %collective-permute-start.22 = (bf16[256,1024]{1,0:T(8,128)(2,1)S(1)}, bf16[256,1024]{1,0:T(8,128)(2,1)S(1)}, u32[]{:S(2)}, u32[]{:S(2)}) collective-permute-start(bf16[256,1024]{1,0:T(8,128)(2,1)S(1)} %pad_maximum_fusion.6.refs_4_), channel_id=1, source_target_pairs={{0,4},{1,5},{2,6},{3,7},{4,0},{5,1},{6,2},{7,3},{8,12},{9,13},{10,... | collective-permute-start | bytes 1572872 | tf_op jit(solution)/shard_map/ppermute | solution.py:57
  98.4 24.9 %collective-permute-start.23 = (bf16[256,1024]{1,0:T(8,128)(2,1)S(1)}, bf16[256,1024]{1,0:T(8,128)(2,1)S(1)}, u32[]{:S(2)}, u32[]{:S(2)}) collective-permute-start(bf16[256,1024]{1,0:T(8,128)(2,1)S(1)} %collective-permute-done.15.refs_5_), channel_id=1, source_target_pairs={{0,4},{1,5},{2,6},{3,7},{4,0},{5,1},{6,2},{7,3},{8,12},{9,13},{10,... | collective-permute-start | bytes 1572872 | tf_op jit(solution)/shard_map/ppermute | solution.py:57
  102.5 20.9 %collective-permute-start.24 = (bf16[256,512]{1,0:T(8,128)(2,1)S(1)}, bf16[256,512]{1,0:T(8,128)(2,1)S(1)}, u32[]{:S(2)}, u32[]{:S(2)}) collective-permute-start(bf16[256,512]{1,0:T(8,128)(2,1)S(1)} %pad_maximum_fusion.9.refs_0_), channel_id=1, source_target_pairs={{0,4},{1,5},{2,6},{3,7},{4,0},{5,1},{6,2},{7,3},{8,12},{9,13},{10,... | collective-permute-start | bytes 786440 | tf_op jit(solution)/shard_map/ppermute | solution.py:57
  140.3 22.2 %collective-permute-start.36 = (bf16[256,1536]{1,0:T(8,128)(2,1)S(1)}, bf16[256,1536]{1,0:T(8,128)(2,1)S(1)}, u32[]{:S(2)}, u32[]{:S(2)}) collective-permute-start(bf16[256,1536]{1,0:T(8,128)(2,1)S(1)} %maximum_maximum_fusion.refs_0_), channel_id=1, source_target_pairs={{0,8},{1,9},{2,10},{3,11},{4,12},{5,13},{6,14},{7,15},{8,16},{9,17... | collective-permute-start | bytes 2359304 | tf_op jit(solution)/shard_map/ppermute | solution.py:61
  140.7 21.8 %collective-permute-start.35 = (bf16[256,1536]{1,0:T(8,128)(2,1)S(1)}, bf16[256,1536]{1,0:T(8,128)(2,1)S(1)}, u32[]{:S(2)}, u32[]{:S(2)}) collective-permute-start(bf16[256,1536]{1,0:T(8,128)(2,1)S(1)} %pad_maximum_fusion.4.refs_4_.refs_8_), channel_id=1, source_target_pairs={{0,2},{1,3},{2,0},{3,1},{4,6},{5,7},{6,4},{7,5},{8,10},{9,11},{10,... | collective-permute-start | bytes 2359304 | tf_op jit(solution)/shard_map/ppermute | solution.py:57
  142.6 20.0 %collective-permute-start.34 = (bf16[256,1536]{1,0:T(8,128)(2,1)S(1)}, bf16[256,1536]{1,0:T(8,128)(2,1)S(1)}, u32[]{:S(2)}, u32[]{:S(2)}) collective-permute-start(bf16[256,1536]{1,0:T(8,128)(2,1)S(1)} %pad_maximum_fusion.3.refs_0_.refs_4_), channel_id=1, source_target_pairs={{0,4},{1,5},{2,6},{3,7},{4,0},{5,1},{6,2},{7,3},{8,12},{9,13},{10,... | collective-permute-start | bytes 2359304 | tf_op jit(solution)/shard_map/ppermute | solution.py:57
  166.7 22.0 %collective-permute-start.43 = (bf16[256,1536]{1,0:T(8,128)(2,1)S(1)}, bf16[256,1536]{1,0:T(8,128)(2,1)S(1)}, u32[]{:S(2)}, u32[]{:S(2)}) collective-permute-start(bf16[256,1536]{1,0:T(8,128)(2,1)S(1)} %collective-permute-done.36.refs_1_), channel_id=1, source_target_pairs={{0,8},{1,9},{2,10},{3,11},{4,12},{5,13},{6,14},{7,15},{8,16},{9,17... | collective-permute-start | bytes 2359304 | tf_op jit(solution)/shard_map/ppermute | solution.py:61
  166.7 23.4 %collective-permute-start.39 = (bf16[256,1536]{1,0:T(8,128)(2,1)}, bf16[256,1536]{1,0:T(8,128)(2,1)S(1)}, u32[]{:S(2)}, u32[]{:S(2)}) collective-permute-start(bf16[256,1536]{1,0:T(8,128)(2,1)} %copy-done.29), channel_id=1, source_target_pairs={{0,2},{1,3},{2,0},{3,1},{4,6},{5,7},{6,4},{7,5},{8,10},{9,11},{10,... | collective-permute-start | bytes 2359304 | tf_op jit(solution)/shard_map/ppermute | solution.py:57
  176.9 38.7 %collective-permute-start.38 = (bf16[512,1024]{1,0:T(8,128)(2,1)S(1)}, bf16[512,1024]{1,0:T(8,128)(2,1)S(1)}, u32[]{:S(2)}, u32[]{:S(2)}) collective-permute-start(bf16[512,1024]{1,0:T(8,128)(2,1)S(1)} %multiply_convert_fusion.xm_ref), channel_id=1, source_target_pairs={{0,1},{1,0},{2,3},{3,2},{4,5},{5,4},{6,7},{7,6},{8,9},{9,8},{10,11... | collective-permute-start | bytes 3145736 | tf_op jit(solution)/shard_map/ppermute | solution.py:57
  178.3 25.4 %collective-permute-start.40 = (bf16[256,1536]{1,0:T(8,128)(2,1)S(1)}, bf16[256,1536]{1,0:T(8,128)(2,1)S(1)}, u32[]{:S(2)}, u32[]{:S(2)}) collective-permute-start(bf16[256,1536]{1,0:T(8,128)(2,1)S(1)} %copy-done.50), channel_id=1, source_target_pairs={{0,2},{1,3},{2,0},{3,1},{4,6},{5,7},{6,4},{7,5},{8,10},{9,11},{10,... | collective-permute-start | bytes 2359304 | tf_op jit(solution)/shard_map/ppermute | solution.py:57
  179.3 24.4 %collective-permute-start.41 = (bf16[256,1536]{1,0:T(8,128)(2,1)S(1)}, bf16[256,1536]{1,0:T(8,128)(2,1)S(1)}, u32[]{:S(2)}, u32[]{:S(2)}) collective-permute-start(bf16[256,1536]{1,0:T(8,128)(2,1)S(1)} %copy-done.28), channel_id=1, source_target_pairs={{0,4},{1,5},{2,6},{3,7},{4,0},{5,1},{6,2},{7,3},{8,12},{9,13},{10,... | collective-permute-start | bytes 2359304 | tf_op jit(solution)/shard_map/ppermute | solution.py:57
  188.7 26.9 %collective-permute-start.42 = (bf16[256,1536]{1,0:T(8,128)(2,1)S(1)}, bf16[256,1536]{1,0:T(8,128)(2,1)S(1)}, u32[]{:S(2)}, u32[]{:S(2)}) collective-permute-start(bf16[256,1536]{1,0:T(8,128)(2,1)S(1)} %copy-done.48), channel_id=1, source_target_pairs={{0,4},{1,5},{2,6},{3,7},{4,0},{5,1},{6,2},{7,3},{8,12},{9,13},{10,... | collective-permute-start | bytes 2359304 | tf_op jit(solution)/shard_map/ppermute | solution.py:57
  190.1 25.5 %collective-permute-start.44 = (bf16[256,1536]{1,0:T(8,128)(2,1)S(1)}, bf16[256,1536]{1,0:T(8,128)(2,1)S(1)}, u32[]{:S(2)}, u32[]{:S(2)}) collective-permute-start(bf16[256,1536]{1,0:T(8,128)(2,1)S(1)} %collective-permute-done.43.refs_2_), channel_id=1, source_target_pairs={{0,8},{1,9},{2,10},{3,11},{4,12},{5,13},{6,14},{7,15},{8,16},{9,17... | collective-permute-start | bytes 2359304 | tf_op jit(solution)/shard_map/ppermute | solution.py:61
  236.5 34.8 %collective-permute-start.45 = (bf16[256,768]{1,0:T(8,128)(2,1)S(1)}, bf16[256,768]{1,0:T(8,128)(2,1)}, u32[]{:S(2)}, u32[]{:S(2)}) collective-permute-start(bf16[256,768]{1,0:T(8,128)(2,1)S(1)} %get-tuple-element.379), channel_id=1, source_target_pairs={{0,2},{1,3},{2,0},{3,1},{4,6},{5,7},{6,4},{7,5},{8,10},{9,11},{10,... | collective-permute-start | bytes 1179656 | tf_op jit(solution)/shard_map/ppermute | solution.py:57
  237.6 33.7 %collective-permute-start.46 = (bf16[256,768]{1,0:T(8,128)(2,1)S(1)}, bf16[256,768]{1,0:T(8,128)(2,1)}, u32[]{:S(2)}, u32[]{:S(2)}) collective-permute-start(bf16[256,768]{1,0:T(8,128)(2,1)S(1)} %get-tuple-element.378), channel_id=1, source_target_pairs={{0,2},{1,3},{2,0},{3,1},{4,6},{5,7},{6,4},{7,5},{8,10},{9,11},{10,... | collective-permute-start | bytes 1179656 | tf_op jit(solution)/shard_map/ppermute | solution.py:57
  238.6 32.7 %collective-permute-start.47 = (bf16[256,768]{1,0:T(8,128)(2,1)S(1)}, bf16[256,768]{1,0:T(8,128)(2,1)}, u32[]{:S(2)}, u32[]{:S(2)}) collective-permute-start(bf16[256,768]{1,0:T(8,128)(2,1)S(1)} %get-tuple-element.377), channel_id=1, source_target_pairs={{0,4},{1,5},{2,6},{3,7},{4,0},{5,1},{6,2},{7,3},{8,12},{9,13},{10,... | collective-permute-start | bytes 1179656 | tf_op jit(solution)/shard_map/ppermute | solution.py:57
  239.9 31.3 %collective-permute-start.48 = (bf16[256,768]{1,0:T(8,128)(2,1)S(1)}, bf16[256,768]{1,0:T(8,128)(2,1)}, u32[]{:S(2)}, u32[]{:S(2)}) collective-permute-start(bf16[256,768]{1,0:T(8,128)(2,1)S(1)} %get-tuple-element.376), channel_id=1, source_target_pairs={{0,4},{1,5},{2,6},{3,7},{4,0},{5,1},{6,2},{7,3},{8,12},{9,13},{10,... | collective-permute-start | bytes 1179656 | tf_op jit(solution)/shard_map/ppermute | solution.py:57
  280.1 17.6 %collective-permute-start.87 = (f32[512,1024]{1,0:T(8,128)S(1)}, f32[512,1024]{1,0:T(8,128)}, u32[]{:S(2)}, u32[]{:S(2)}) collective-permute-start(f32[512,1024]{1,0:T(8,128)S(1)} %down_forward.3), channel_id=1, source_target_pairs={{0,1},{1,0},{2,3},{3,2},{4,5},{5,4},{6,7},{7,6},{8,9},{9,8},{10,11... | collective-permute-start | bytes 6291464 | tf_op jit(solution)/shard_map/ppermute | solution.py:57
  285.4 28.5 %collective-permute-start.51 = (bf16[256,1536]{1,0:T(8,128)(2,1)}, bf16[256,1536]{1,0:T(8,128)(2,1)S(1)}, u32[]{:S(2)}, u32[]{:S(2)}) collective-permute-start(bf16[256,1536]{1,0:T(8,128)(2,1)} %get-tuple-element.375), channel_id=1, source_target_pairs={{0,2},{1,3},{2,0},{3,1},{4,6},{5,7},{6,4},{7,5},{8,10},{9,11},{10,... | collective-permute-start | bytes 2359304 | tf_op jit(solution)/shard_map/ppermute | solution.py:57
  286.5 35.6 %collective-permute-start.52 = (bf16[256,1536]{1,0:T(8,128)(2,1)}, bf16[256,1536]{1,0:T(8,128)(2,1)}, u32[]{:S(2)}, u32[]{:S(2)}) collective-permute-start(bf16[256,1536]{1,0:T(8,128)(2,1)} %get-tuple-element.374), channel_id=1, source_target_pairs={{0,2},{1,3},{2,0},{3,1},{4,6},{5,7},{6,4},{7,5},{8,10},{9,11},{10,... | collective-permute-start | bytes 2359304 | tf_op jit(solution)/shard_map/ppermute | solution.py:57
  293.5 28.6 %collective-permute-start.53 = (bf16[256,1536]{1,0:T(8,128)(2,1)}, bf16[256,1536]{1,0:T(8,128)(2,1)}, u32[]{:S(2)}, u32[]{:S(2)}) collective-permute-start(bf16[256,1536]{1,0:T(8,128)(2,1)} %get-tuple-element.373), channel_id=1, source_target_pairs={{0,4},{1,5},{2,6},{3,7},{4,0},{5,1},{6,2},{7,3},{8,12},{9,13},{10,... | collective-permute-start | bytes 2359304 | tf_op jit(solution)/shard_map/ppermute | solution.py:57
  297.6 31.9 %collective-permute-start.54 = (bf16[256,1536]{1,0:T(8,128)(2,1)}, bf16[256,1536]{1,0:T(8,128)(2,1)}, u32[]{:S(2)}, u32[]{:S(2)}) collective-permute-start(bf16[256,1536]{1,0:T(8,128)(2,1)} %get-tuple-element.372), channel_id=1, source_target_pairs={{0,4},{1,5},{2,6},{3,7},{4,0},{5,1},{6,2},{7,3},{8,12},{9,13},{10,... | collective-permute-start | bytes 2359304 | tf_op jit(solution)/shard_map/ppermute | solution.py:57
  331.7 43.3 %collective-permute-start.58 = (bf16[256,1536]{1,0:T(8,128)(2,1)}, bf16[256,1536]{1,0:T(8,128)(2,1)}, u32[]{:S(2)}, u32[]{:S(2)}) collective-permute-start(bf16[256,1536]{1,0:T(8,128)(2,1)} %add_convert_fusion.5), channel_id=1, source_target_pairs={{0,2},{1,3},{2,0},{3,1},{4,6},{5,7},{6,4},{7,5},{8,10},{9,11},{10,... | collective-permute-start | bytes 2359304 | tf_op jit(solution)/shard_map/ppermute | solution.py:57
  335.3 40.4 %collective-permute-start.57 = (bf16[256,1536]{1,0:T(8,128)(2,1)}, bf16[256,1536]{1,0:T(8,128)(2,1)}, u32[]{:S(2)}, u32[]{:S(2)}) collective-permute-start(bf16[256,1536]{1,0:T(8,128)(2,1)} %add_convert_fusion.6), channel_id=1, source_target_pairs={{0,4},{1,5},{2,6},{3,7},{4,0},{5,1},{6,2},{7,3},{8,12},{9,13},{10,... | collective-permute-start | bytes 2359304 | tf_op jit(solution)/shard_map/ppermute | solution.py:57
  336.7 35.8 %collective-permute-start.55 = (bf16[256,768]{1,0:T(8,128)(2,1)}, bf16[256,768]{1,0:T(8,128)(2,1)}, u32[]{:S(2)}, u32[]{:S(2)}) collective-permute-start(bf16[256,768]{1,0:T(8,128)(2,1)} %get-tuple-element.303), channel_id=1, source_target_pairs={{0,4},{1,5},{2,6},{3,7},{4,0},{5,1},{6,2},{7,3},{8,12},{9,13},{10,... | collective-permute-start | bytes 1179656 | tf_op jit(solution)/shard_map/ppermute | solution.py:57
  337.3 36.3 %collective-permute-start.56 = (bf16[256,768]{1,0:T(8,128)(2,1)}, bf16[256,768]{1,0:T(8,128)(2,1)}, u32[]{:S(2)}, u32[]{:S(2)}) collective-permute-start(bf16[256,768]{1,0:T(8,128)(2,1)} %get-tuple-element.304), channel_id=1, source_target_pairs={{0,2},{1,3},{2,0},{3,1},{4,6},{5,7},{6,4},{7,5},{8,10},{9,11},{10,... | collective-permute-start | bytes 1179656 | tf_op jit(solution)/shard_map/ppermute | solution.py:57
  339.3 51.1 %collective-permute-start.59 = (bf16[256,512]{1,0:T(8,128)(2,1)}, bf16[256,512]{1,0:T(8,128)(2,1)S(1)}, u32[]{:S(2)}, u32[]{:S(2)}) collective-permute-start(bf16[256,512]{1,0:T(8,128)(2,1)} %get-tuple-element.392), channel_id=1, source_target_pairs={{0,2},{1,3},{2,0},{3,1},{4,6},{5,7},{6,4},{7,5},{8,10},{9,11},{10,... | collective-permute-start | bytes 786440 | tf_op jit(solution)/shard_map/ppermute | solution.py:57
  372.6 20.2 %collective-permute-start.60 = (bf16[256,512]{1,0:T(8,128)(2,1)}, bf16[256,512]{1,0:T(8,128)(2,1)S(1)}, u32[]{:S(2)}, u32[]{:S(2)}) collective-permute-start(bf16[256,512]{1,0:T(8,128)(2,1)} %get-tuple-element.391), channel_id=1, source_target_pairs={{0,2},{1,3},{2,0},{3,1},{4,6},{5,7},{6,4},{7,5},{8,10},{9,11},{10,... | collective-permute-start | bytes 786440 | tf_op jit(solution)/shard_map/ppermute | solution.py:57
  373.6 21.4 %collective-permute-start.61 = (bf16[256,512]{1,0:T(8,128)(2,1)}, bf16[256,512]{1,0:T(8,128)(2,1)S(1)}, u32[]{:S(2)}, u32[]{:S(2)}) collective-permute-start(bf16[256,512]{1,0:T(8,128)(2,1)} %get-tuple-element.390), channel_id=1, source_target_pairs={{0,4},{1,5},{2,6},{3,7},{4,0},{5,1},{6,2},{7,3},{8,12},{9,13},{10,... | collective-permute-start | bytes 786440 | tf_op jit(solution)/shard_map/ppermute | solution.py:57
  375.0 20.0 %collective-permute-start.62 = (bf16[256,512]{1,0:T(8,128)(2,1)}, bf16[256,512]{1,0:T(8,128)(2,1)S(1)}, u32[]{:S(2)}, u32[]{:S(2)}) collective-permute-start(bf16[256,512]{1,0:T(8,128)(2,1)} %get-tuple-element.389), channel_id=1, source_target_pairs={{0,4},{1,5},{2,6},{3,7},{4,0},{5,1},{6,2},{7,3},{8,12},{9,13},{10,... | collective-permute-start | bytes 786440 | tf_op jit(solution)/shard_map/ppermute | solution.py:57
  378.0 17.0 %collective-permute-start.63 = (bf16[64,1536]{1,0:T(8,128)(2,1)S(1)}, bf16[64,1536]{1,0:T(8,128)(2,1)S(1)}, u32[]{:S(2)}, u32[]{:S(2)}) collective-permute-start(bf16[64,1536]{1,0:T(8,128)(2,1)S(1)} %get-tuple-element.404), channel_id=1, source_target_pairs={{0,24},{1,25},{2,26},{3,27},{4,28},{5,29},{6,30},{7,31},{8,0},{9,1... | collective-permute-start | bytes 589832 | tf_op jit(solution)/shard_map/ppermute | solution.py:61
  422.0 36.9 %collective-permute-start.73 = (bf16[64,3072]{1,0:T(8,128)(2,1)S(1)}, bf16[64,3072]{1,0:T(8,128)(2,1)S(1)}, u32[]{:S(2)}, u32[]{:S(2)}) collective-permute-start(bf16[64,3072]{1,0:T(8,128)(2,1)S(1)} %get-tuple-element.396), channel_id=1, source_target_pairs={{0,16},{1,17},{2,18},{3,19},{4,20},{5,21},{6,22},{7,23},{8,24},{9,... | collective-permute-start | bytes 1179656 | tf_op jit(solution)/shard_map/ppermute | solution.py:61
  424.2 34.8 %collective-permute-start.74 = (bf16[64,3072]{1,0:T(8,128)(2,1)S(1)}, bf16[64,3072]{1,0:T(8,128)(2,1)S(1)}, u32[]{:S(2)}, u32[]{:S(2)}) collective-permute-start(bf16[64,3072]{1,0:T(8,128)(2,1)S(1)} %get-tuple-element.393), channel_id=1, source_target_pairs={{0,8},{1,9},{2,10},{3,11},{4,12},{5,13},{6,14},{7,15},{8,16},{9,17... | collective-permute-start | bytes 1179656 | tf_op jit(solution)/shard_map/ppermute | solution.py:61
  426.1 34.9 %collective-permute-start.70 = (bf16[256,512]{1,0:T(8,128)(2,1)S(1)}, bf16[256,512]{1,0:T(8,128)(2,1)S(1)}, u32[]{:S(2)}, u32[]{:S(2)}) collective-permute-start(bf16[256,512]{1,0:T(8,128)(2,1)S(1)} %get-tuple-element.384), channel_id=1, source_target_pairs={{0,4},{1,5},{2,6},{3,7},{4,0},{5,1},{6,2},{7,3},{8,12},{9,13},{10,... | collective-permute-start | bytes 786440 | tf_op jit(solution)/shard_map/ppermute | solution.py:57
  428.3 36.7 %collective-permute-start.71 = (bf16[256,512]{1,0:T(8,128)(2,1)S(1)}, bf16[256,512]{1,0:T(8,128)(2,1)S(1)}, u32[]{:S(2)}, u32[]{:S(2)}) collective-permute-start(bf16[256,512]{1,0:T(8,128)(2,1)S(1)} %get-tuple-element.383), channel_id=1, source_target_pairs={{0,2},{1,3},{2,0},{3,1},{4,6},{5,7},{6,4},{7,5},{8,10},{9,11},{10,... | collective-permute-start | bytes 786440 | tf_op jit(solution)/shard_map/ppermute | solution.py:57
  433.4 31.6 %collective-permute-start.66 = (bf16[256,1024]{1,0:T(8,128)(2,1)S(1)}, bf16[256,1024]{1,0:T(8,128)(2,1)S(1)}, u32[]{:S(2)}, u32[]{:S(2)}) collective-permute-start(bf16[256,1024]{1,0:T(8,128)(2,1)S(1)} %get-tuple-element.388), channel_id=1, source_target_pairs={{0,2},{1,3},{2,0},{3,1},{4,6},{5,7},{6,4},{7,5},{8,10},{9,11},{10,... | collective-permute-start | bytes 1572872 | tf_op jit(solution)/shard_map/ppermute | solution.py:57
  461.0 23.0 %collective-permute-start.69 = (bf16[256,1024]{1,0:T(8,128)(2,1)S(1)}, bf16[256,1024]{1,0:T(8,128)(2,1)S(1)}, u32[]{:S(2)}, u32[]{:S(2)}) collective-permute-start(bf16[256,1024]{1,0:T(8,128)(2,1)S(1)} %get-tuple-element.385), channel_id=1, source_target_pairs={{0,4},{1,5},{2,6},{3,7},{4,0},{5,1},{6,2},{7,3},{8,12},{9,13},{10,... | collective-permute-start | bytes 1572872 | tf_op jit(solution)/shard_map/ppermute | solution.py:57
  522.6 24.2 %collective-permute-start.94 = (bf16[64,2048]{1,0:T(8,128)(2,1)S(1)}, bf16[64,2048]{1,0:T(8,128)(2,1)S(1)}, u32[]{:S(2)}, u32[]{:S(2)}) collective-permute-start(bf16[64,2048]{1,0:T(8,128)(2,1)S(1)} %get-tuple-element.399), channel_id=1, source_target_pairs={{0,16},{1,17},{2,18},{3,19},{4,20},{5,21},{6,22},{7,23},{8,24},{9,... | collective-permute-start | bytes 786440 | tf_op jit(solution)/shard_map/ppermute | solution.py:61
  523.1 23.7 %collective-permute-start.95 = (bf16[64,2048]{1,0:T(8,128)(2,1)S(1)}, bf16[64,2048]{1,0:T(8,128)(2,1)S(1)}, u32[]{:S(2)}, u32[]{:S(2)}) collective-permute-start(bf16[64,2048]{1,0:T(8,128)(2,1)S(1)} %get-tuple-element.398), channel_id=1, source_target_pairs={{0,8},{1,9},{2,10},{3,11},{4,12},{5,13},{6,14},{7,15},{8,16},{9,17... | collective-permute-start | bytes 786440 | tf_op jit(solution)/shard_map/ppermute | solution.py:61
  (176 other events, 2344.8 us)

commit v3 on v2

v3 whole, which is shorter than its diff:
```python
import functools
import math

import jax
import jax.numpy as jnp
from jax import lax
from jax.experimental import pallas as pl
from jax.experimental.pallas import tpu as pltpu
from jax.sharding import PartitionSpec as P

epsilon = 1e-06
rope_base = 1000000.0
low = jnp.bfloat16
full = jnp.float32
barrier = lax.optimization_barrier


def dot(left_side, right_side, left_dim=1, right_dim=0, kind=full):
    return lax.dot_general(
        left_side,
        right_side,
        (((left_dim,), (right_dim,)), ((), ())),
        preferred_element_type=kind,
    )


def inverse_rms(values):
    return lax.rsqrt(jnp.mean(values * values, axis=-1, keepdims=True) + epsilon)


def rotate(values, cosines, sines):
    half_size = values.shape[-1] // 2
    first_half = values[..., :half_size]
    second = values[..., half_size:]
    return jnp.concatenate(
        [first_half * cosines - second * sines, second * cosines + first_half * sines], axis=-1
    )


def norm_back(gradient, normed, scales):
    return scales * (gradient - normed * jnp.mean(gradient * normed, axis=-1, keepdims=True))


class Slice:
    def __init__(self):
        self.count = lax.axis_size("dp")
        self.chips = self.count // 2
        self.side = 1
        while 4 * self.side * self.side < self.chips:
            self.side *= 2
        self.device = lax.axis_index("dp")
        self.core = self.device % 2
        self.chip = self.device // 2

    def ring(self, array, by):
        step = 2 * self.side * self.side * by
        return lax.ppermute(
            array, "dp", [(i, (i + step) % self.count) for i in range(self.count)]
        )

    def chip_along(self, array, by):
        pairs = [(i, i + 2 * by) for i in range(self.count) if 0 <= i + 2 * by < self.count]
        return lax.ppermute(array, "dp", pairs)

    def last_core_along(self, array, by):
        pairs = [(i, i + 2 * by) for i in range(1, self.count, 2) if 0 <= i + 2 * by < self.count]
        return lax.ppermute(array, "dp", pairs)

    def pair(self, array):
        return lax.ppermute(array, "dp", [(i, i ^ 1) for i in range(self.count)])

    def plane(self, array, stage, amount):
        pairs = []
        for i in range(self.count):
            along_x = i % 2 != stage % 2
            pairs.append((i, i ^ (2 * amount * (1 if along_x else self.side))))
        return lax.ppermute(array, "dp", pairs)

    def by_core(self, mine, other, axis=0):
        return jnp.where(
            self.core == 0,
            jnp.concatenate([mine, other], axis=axis),
            jnp.concatenate([other, mine], axis=axis),
        )

    def places(self, chip, unit):
        side = self.side
        entry = jnp.arange(self.chips * unit, dtype=jnp.int32)
        inner, block = entry % unit, entry // unit
        along_z, first, second = block % 4, block // 4 % side, block // (4 * side)
        along_x = jnp.where(self.core == 0, second, first)
        along_y = jnp.where(self.core == 0, first, second)
        own_x, own_y, own_z = chip % side, chip // side % side, chip // (side * side)
        source = (
            ((own_z - along_z + 4) % 4) * side * side + (own_y ^ along_y) * side + (own_x ^ along_x)
        )
        return source * unit + inner

    def swapped(self, array):
        size = array.shape[1] // (self.side * self.side)
        starts = [
            (second * self.side + first) * size
            for first in range(self.side)
            for second in range(self.side)
        ]
        return jnp.concatenate([array[:, start : start + size] for start in starts], 1)

    def pair_in(self, array, count):
        return jnp.concatenate([self.pair(part) for part in jnp.split(array, count)])

    def scatter_z(self, blocks):
        return [blocks[0], blocks[1], self.ring(blocks[2], -1), self.ring(blocks[3], 1)]

    def scatter_z_last(self, terms):
        own, one, two, three = terms
        sent = (one.astype(full) + two.astype(full)).astype(one.dtype)
        return [own, three, self.ring(sent, -1)]

    def gather_plane(self, array, stage):
        return [array] + [self.plane(array, stage, m) for m in range(1, self.side)]

    def scatter_plane(self, parts, stage):
        return [self.plane(part, stage, m + 1) for m, part in enumerate(parts[1:])]


def place_kernel(core_ref, mine_ref, other_ref, out_ref):
    at_mine = pl.program_id(0) == core_ref[0]

    @pl.when(at_mine)
    def _():
        out_ref[...] = mine_ref[...]

    @pl.when(jnp.logical_not(at_mine))
    def _():
        out_ref[...] = other_ref[...]


def place(which, mine, other):
    rows, columns = mine.shape
    return call(
        place_kernel,
        "place",
        (2,),
        [whole_block(mine), whole_block(other)],
        [((2 * rows, columns), mine.dtype, mine.shape, lambda i, core: (i, 0))],
        0,
        8 * mine.size,
        scalars=(which,),
    )[0]


def fold_kernel(counts, core_ref, *refs):
    ins, (mine_ref, other_ref) = refs[:-2], refs[-2:]
    rows = mine_ref.shape[0]
    first = core_ref[0] == 0
    start, at = 0, 0
    for count in counts:
        terms = [ref[...].astype(full) for ref in ins[at : at + count]]
        total = sum(terms[1:], terms[0])
        here = slice(start, start + total.shape[1])
        mine_ref[:, here] = jnp.where(first, total[:rows], total[rows:])
        other_ref[:, here] = jnp.where(first, total[rows:], total[:rows])
        start += total.shape[1]
        at += count


def fold(which, *groups):
    rows = groups[0][0].shape[0] // 2
    columns = sum([group[0].shape[1] for group in groups])
    terms = [term for group in groups for term in group]
    fixed = lambda i, core: (0, 0)
    return call(
        functools.partial(fold_kernel, tuple([len(group) for group in groups])),
        "fold",
        (1,),
        [whole_block(term) for term in terms],
        [((rows, columns), full, (rows, columns), fixed)] * 2,
        0,
        20 * rows * columns,
        scalars=(which,),
    )


def join_kernel(ranges, core_ref, mine_ref, other_ref, *outs):
    def write(first, second):
        for out, spans in zip(outs, ranges):
            at = 0
            for ref in (first, second):
                for start, end in spans:
                    out[:, at : at + end - start] = ref[:, start:end]
                    at += end - start

    pl.when(core_ref[0] == 0)(lambda: write(mine_ref, other_ref))
    pl.when(core_ref[0] != 0)(lambda: write(other_ref, mine_ref))


def join(which, mine, other, *ranges):
    rows = mine.shape[0]
    widths = [2 * sum([end - start for start, end in spans]) for spans in ranges]
    fixed = lambda i, core: (0, 0)
    return call(
        functools.partial(join_kernel, ranges),
        "join",
        (1,),
        [whole_block(mine), whole_block(other)],
        [((rows, columns), mine.dtype, (rows, columns), fixed) for columns in widths],
        0,
        16 * mine.size,
        scalars=(which,),
    )


def cut_kernel(cuts, blocks, *refs):
    ins, outs = refs[:blocks], refs[blocks:]
    rows = ins[0].shape[0]
    for at, block in enumerate(ins):
        for out, start, end in zip(outs, cuts[:-1], cuts[1:]):
            out[at * rows : (at + 1) * rows, :] = block[:, start:end]


def stack_cut(blocks, cuts):
    rows, columns = blocks[0].shape
    cuts = (0,) + tuple(cuts) + (columns,)
    shapes = [
        (len(blocks) * rows, end - start) for start, end in zip(cuts[:-1], cuts[1:])
    ]
    return call(
        functools.partial(cut_kernel, cuts, len(blocks)),
        "stack_cut",
        (1,),
        [whole_block(block) for block in blocks],
        [(shape, low, shape, lambda i: (0, 0)) for shape in shapes],
        0,
        4 * len(blocks) * rows * columns,
    )


def score_bias(query_segments, key_segments, rows, halo):
    key_count, query_count = key_segments.shape[0], query_segments.shape[1]
    key_place = lax.broadcasted_iota(jnp.int32, (key_count, query_count), 0) - halo
    query_place = lax.broadcasted_iota(jnp.int32, (key_count, query_count), 1)
    seen = (key_segments == query_segments) & (key_place <= query_place)
    return jnp.where(seen, 0.0, -1e30).astype(full)


def parts_of(rows, halo):
    return (((0, halo), 2 * halo), ((halo, rows), halo + rows))


def reorder(refs, part, parts, unit):
    size = refs[0].shape[0] // parts
    return jnp.concatenate(
        [
            ref[row : row + unit, :]
            for row in range(part * size, (part + 1) * size, unit)
            for ref in refs
        ],
        axis=0,
    )


def write_parts(out_ref, parts, swap=False):
    side = parts.side
    for second in range(side):
        found = parts(second).astype(out_ref.dtype)
        width = found.shape[1]
        if not swap:
            out_ref[:, second * width : (second + 1) * width] = found
            continue
        size = width // side
        for first in range(side):
            start = (first * side + second) * size
            out_ref[:, start : start + size] = found[:, first * size : (first + 1) * size]


class Parts:
    def __init__(self, side, find):
        self.side = side
        self.find = find

    def __call__(self, part):
        return self.find(part)


def contract(value, refs, columns=slice(None)):
    size = refs[0].shape[0]
    total = None
    for at, ref in enumerate(refs):
        term = dot(value[:, at * size : (at + 1) * size], ref[:, columns])
        total = term if total is None else total + term
    return total


def turn(values, cosines, sines):
    return values * cosines + pltpu.roll(values, values.shape[1] // 2, 1) * sines


def row_rms(values):
    return lax.rsqrt(jnp.mean(values * values, axis=1, keepdims=True) + epsilon)


def call(
    kernel, name, grid, ins, outs, flops, bytes_accessed, scratch=(), transcendentals=0, scalars=(),
    least=0,
):
    size = sum([2 * math.prod(block) * array.dtype.itemsize for array, block, _ in ins])
    size += sum([2 * math.prod(block) * jnp.dtype(kind).itemsize for _, kind, block, _ in outs])
    size += sum([math.prod(part.shape) * jnp.dtype(part.dtype).itemsize for part in scratch])
    return pl.pallas_call(
        kernel,
        grid_spec=pltpu.PrefetchScalarGridSpec(
            num_scalar_prefetch=len(scalars),
            grid=grid,
            in_specs=[pl.BlockSpec(block, index) for _, block, index in ins],
            out_specs=[pl.BlockSpec(block, index) for _, _, block, index in outs],
            scratch_shapes=list(scratch),
        ),
        out_shape=[jax.ShapeDtypeStruct(shape, kind) for shape, kind, _, _ in outs],
        compiler_params=pltpu.CompilerParams(vmem_limit_bytes=max(size + (10 << 20), least)),
        cost_estimate=pl.CostEstimate(
            flops=flops, bytes_accessed=bytes_accessed, transcendentals=transcendentals
        ),
        name=name,
    )(*scalars, *[array for array, _, _ in ins])


def tile_of(columns):
    return next(tile for tile in (768, 512, 256, 128, columns) if columns % tile == 0)


def whole_block(array):
    return (array, array.shape, lambda *at: (0,) * array.ndim)


def project_kernel(q_cols, k_cols, x_ref, cos_ref, sin_ref, pick_ref, *refs):
    parts = refs[:-8]
    in_ref, q_ref, k_ref, v_ref, qp_ref, kp_ref, rows_ref, heads_ref = refs[-8:]
    head_size = heads_ref.shape[1]
    k_at = q_cols + 128
    step = pl.program_id(0)

    @pl.when(step == 0)
    def _():
        found = [ref[:, q_cols:k_at].astype(full).T[:8] for ref in parts]
        rows = jnp.concatenate(found, axis=1)
        rows_ref[...] = rows
        heads_ref[...] = dot(rows.astype(low), pick_ref[...])

    x = x_ref[...].astype(full)
    attn_in = (x * row_rms(x) * rows_ref[0:1, :]).astype(low)
    in_ref[...] = attn_in
    cosines, sines = cos_ref[...], sin_ref[...]

    def heads_of(projected, gain, proj_ref, out_ref, start):
        proj_ref[:, start : start + projected.shape[1]] = projected.astype(low)
        for column in range(0, projected.shape[1], head_size):
            head = projected[:, column : column + head_size]
            head = turn(head * row_rms(head) * gain, cosines, sines)
            out_ref[:, start + column : start + column + head_size] = head.astype(low)

    heads_of(contract(attn_in, parts, slice(k_at, k_at + k_cols)), heads_ref[3:4, :], kp_ref, k_ref, 0)
    v_ref[...] = contract(attn_in, parts, slice(k_at + k_cols, k_at + 2 * k_cols)).astype(low)

    @pl.when(step > 0)
    def _():
        for start in range(0, q_cols, 512):
            heads_of(
                contract(attn_in, parts, slice(start, start + 512)),
                heads_ref[2:3, :], qp_ref, q_ref, start,
            )


def project(ordered, cosines, sines, pick, parts, q_cols, k_cols, halo):
    row_count, width = ordered.shape
    own = row_count - halo
    head_size = cosines.shape[1]
    tile = lambda i: (i, 0)
    later = lambda i: (jnp.maximum(i - 1, 0), 0)
    fixed = lambda i: (0, 0)
    return call(
        functools.partial(project_kernel, q_cols, k_cols),
        "project",
        (row_count // halo,),
        [
            (ordered, (halo, width), tile),
            (cosines, (halo, head_size), tile),
            (sines, (halo, head_size), tile),
            whole_block(pick),
        ]
        + [whole_block(part) for part in parts],
        [
            ((row_count, width), low, (halo, width), tile),
            ((own, q_cols), low, (halo, q_cols), later),
            ((row_count, k_cols), low, (halo, k_cols), tile),
            ((row_count, k_cols), low, (halo, k_cols), tile),
            ((own, q_cols), low, (halo, q_cols), later),
            ((row_count, k_cols), low, (halo, k_cols), tile),
            ((8, width), full, (8, width), fixed),
            ((8, head_size), full, (8, head_size), fixed),
        ],
        2 * row_count * width * (q_cols + 2 * k_cols),
        20 << 20,
    )


def gate_kernel(side, xm_ref, xo_ref, *refs):
    gate_refs, up_refs = refs[:side], refs[side : 2 * side]
    act_ref, to_gate_ref, to_up_ref = refs[2 * side :]
    half = xm_ref.shape[0]
    for at, ref in enumerate((xm_ref, xo_ref)):
        rows = slice(at * half, (at + 1) * half)
        gate = contract(ref, gate_refs)
        up = contract(ref, up_refs)
        sigma = 1.0 / (1.0 + jnp.exp(-gate))
        silu = gate * sigma
        act_ref[rows, :] = (silu * up).astype(low)
        to_gate_ref[rows, :] = (up * sigma * (1.0 + gate * (1.0 - sigma))).astype(low)
        to_up_ref[rows, :] = silu.astype(low)


def gate_forward(mine, other, parts):
    half, width = mine.shape
    columns = parts[0].shape[1] // 2
    tile = tile_of(columns)
    wide = lambda j: (0, j)
    after = lambda j: (0, j + columns // tile)
    block = (parts[0].shape[0], tile)
    return call(
        functools.partial(gate_kernel, len(parts)),
        "gate_forward",
        (columns // tile,),
        [whole_block(mine), whole_block(other)]
        + [(part, block, wide) for part in parts]
        + [(part, block, after) for part in parts],
        [((2 * half, columns), low, (2 * half, tile), wide)] * 3,
        8 * half * width * columns,
        16 << 20,
        transcendentals=2 * half * columns,
    )


def act_back_kernel(unit, gb_ref, to_gate_ref, to_up_ref, *refs):
    down_refs, (gate_out, up_out) = refs[:4], refs[4:]
    act_grad = dot(gb_ref[...], reorder(down_refs, 0, 1, unit))
    gate_out[...] = (act_grad * to_gate_ref[...].astype(full)).astype(low)
    up_out[...] = (act_grad * to_up_ref[...].astype(full)).astype(low)


def act_backward(both, to_gate, to_up, down_parts, unit):
    rows, columns = to_gate.shape
    tile = min(tile_of(columns), 512)
    wide = lambda j: (0, j)
    return call(
        functools.partial(act_back_kernel, unit),
        "act_backward",
        (columns // tile,),
        [whole_block(both)]
        + [(factor, (rows, tile), wide) for factor in (to_gate, to_up)]
        + [(part, (part.shape[0], tile), wide) for part in down_parts],
        [((rows, columns), low, (rows, tile), wide)] * 2,
        2 * both.size * columns,
        16 << 20,
    )


def mlp_back_kernel(side, steps, gate_ref, up_ref, *refs):
    parts, (other_ref, mine_ref) = refs[:side], refs[side:]
    columns = gate_ref.shape[1]
    found = Parts(
        side,
        lambda part: dot(gate_ref[...], parts[part][:, :columns], 1, 1)
        + dot(up_ref[...], parts[part][:, columns:], 1, 1),
    )
    pl.when(pl.program_id(0) < steps)(lambda: write_parts(other_ref, found, swap=True))
    pl.when(pl.program_id(0) >= steps)(lambda: write_parts(mine_ref, found))


def mlp_backward(gate_grad, up_grad, parts, tile=256):
    rows, columns = gate_grad.shape[0] // 2, gate_grad.shape[1]
    width = len(parts) * parts[0].shape[0]
    steps = rows // tile
    rows_of = lambda i: ((i + steps) % (2 * steps), 0)
    return call(
        functools.partial(mlp_back_kernel, len(parts), steps),
        "mlp_backward",
        (2 * steps,),
        [(grad, (tile, columns), rows_of) for grad in (gate_grad, up_grad)]
        + [whole_block(part) for part in parts],
        [
            ((rows, width), full, (tile, width), lambda i: (jnp.minimum(i, steps - 1), 0)),
            ((rows, width), full, (tile, width), lambda i: (jnp.maximum(i - steps, 0), 0)),
        ],
        8 * rows * columns * width,
        16 << 20,
    )


def down_kernel(side, unit, steps, act_ref, *refs):
    down_refs, (other_ref, mine_ref) = refs[:4], refs[4:]
    parts = Parts(
        side, lambda part: dot(act_ref[...], reorder(down_refs, part, side, unit), 1, 1)
    )
    pl.when(pl.program_id(0) < steps)(lambda: write_parts(other_ref, parts, swap=True))
    pl.when(pl.program_id(0) >= steps)(lambda: write_parts(mine_ref, parts))


def down_forward(activated, down_parts, side, unit, tile=256):
    rows, columns = activated.shape[0] // 2, activated.shape[1]
    width = 4 * down_parts[0].shape[0]
    steps = rows // tile
    return call(
        functools.partial(down_kernel, side, unit, steps),
        "down_forward",
        (2 * steps,),
        [(activated, (tile, columns), lambda i: ((i + steps) % (2 * steps), 0))]
        + [whole_block(part) for part in down_parts],
        [
            ((rows, width), full, (tile, width), lambda i: (jnp.minimum(i, steps - 1), 0)),
            ((rows, width), full, (tile, width), lambda i: (jnp.maximum(i - steps, 0), 0)),
        ],
        4 * rows * columns * width,
        12 << 20,
    )


def back_kernel(side, q_cols, steps, core_ref, q_ref, k_ref, v_ref, halo_ref, *refs):
    parts, (other_ref, mine_ref) = refs[:side], refs[side:]
    step = pl.program_id(0)
    k_cols = k_ref.shape[1]
    k_at = q_cols + 128
    v_at = k_at + k_cols
    half = jnp.where(step < steps, 1 - core_ref[0], core_ref[0])
    last = (half == 1) & (step % steps == steps - 1)
    later = jnp.where(last, halo_ref[...].astype(full), 0.0)
    keys = (k_ref[...].astype(full) + later[:, :k_cols]).astype(low)
    values = (v_ref[...].astype(full) + later[:, k_cols:]).astype(low)

    def terms(part):
        return (
            dot(q_ref[...], parts[part][:, :q_cols], 1, 1)
            + dot(keys, parts[part][:, k_at:v_at], 1, 1)
            + dot(values, parts[part][:, v_at : v_at + k_cols], 1, 1)
        )

    pl.when(step < steps)(lambda: write_parts(other_ref, Parts(side, terms), swap=True))
    pl.when(step >= steps)(lambda: write_parts(mine_ref, Parts(side, terms)))


def input_backward(which, query_low, key_low, value_low, later, parts):
    own, q_cols = query_low.shape
    k_cols = key_low.shape[1]
    tile = later.shape[0]
    halo_steps = (key_low.shape[0] - own) // tile
    steps = own // 2 // tile
    width = len(parts) * parts[0].shape[0]

    def own_rows(i, core):
        half = jnp.where(i < steps, 1 - core[0], core[0])
        return half * steps + i % steps

    return call(
        functools.partial(back_kernel, len(parts), q_cols, steps),
        "input_backward",
        (2 * steps,),
        [(query_low, (tile, q_cols), lambda i, core: (own_rows(i, core), 0))]
        + [
            (part, (tile, k_cols), lambda i, core: (halo_steps + own_rows(i, core), 0))
            for part in (key_low, value_low)
        ]
        + [whole_block(part) for part in [later] + parts],
        [
            ((own // 2, width), full, (tile, width), lambda i, core: (jnp.minimum(i, steps - 1), 0)),
            ((own // 2, width), full, (tile, width), lambda i, core: (jnp.maximum(i - steps, 0), 0)),
        ],
        2 * own * width * (q_cols + 2 * k_cols),
        16 << 20,
        scalars=(which,),
    )


def finish_kernel(mine_ref, sent_ref, x_ref, hidden_ref, gain_ref, out_ref, sum_ref):
    grad = mine_ref[...] + sent_ref[...]
    x = x_ref[...].astype(full)
    scales = row_rms(x)
    normed = x * scales

    @pl.when(pl.program_id(0) == 0)
    def _():
        sum_ref[...] = jnp.zeros_like(sum_ref)

    sum_ref[0:1, :] += jnp.sum(grad * normed, axis=0, keepdims=True)
    back = grad * gain_ref[0:1, :]
    mean = jnp.mean(back * normed, axis=1, keepdims=True)
    out_ref[...] = (hidden_ref[...] + scales * (back - normed * mean)).astype(low)


def finish_tokens(mine, sent, inputs, hidden_grad, gains, tile=128):
    rows, width = mine.shape
    rows_of = lambda i: (i, 0)
    fixed = lambda i: (0, 0)
    return call(
        finish_kernel,
        "finish_tokens",
        (rows // tile,),
        [(array, (tile, width), rows_of) for array in (mine, sent, inputs, hidden_grad)]
        + [whole_block(gains)],
        [((rows, width), low, (tile, width), rows_of), ((8, width), full, (8, width), fixed)],
        12 * rows * width,
        18 * rows * width,
    )


def sums_kernel(side, tokens, segments, *refs):
    outs, turned = refs[-1 - side : -1], refs[-1]
    right_refs = refs[-1 - side - len(segments) : -1 - side]
    left_refs = refs[: -1 - side - len(segments)]
    step = pl.program_id(0)
    size = turned.shape[0] // side

    @pl.when(step == 0)
    def _():
        start = 0
        for ref in left_refs:
            turned[:, start : start + ref.shape[0]] = ref[...].T
            start += ref.shape[0]

    for ref, (first, steps, row) in zip(right_refs, segments):

        @pl.when((step >= first) & (step < first + steps))
        def _(ref=ref, row=row):
            for part, out in enumerate(outs):
                out[...] = dot(turned[part * size : (part + 1) * size, row:], ref[...]).astype(low)


def token_sums(side, lefts, rights):
    width = lefts[0].shape[1]
    tokens = sum([left.shape[0] for left in lefts])
    tile = min([tile_of(array.shape[1]) for array, _ in rights])
    segments, step = [], 0
    for array, row in rights:
        steps = array.shape[1] // tile
        segments.append((step, steps, row))
        step += steps

    def clip(first, steps):
        return lambda j: (0, jnp.clip(j - first, 0, steps - 1))

    ins = [whole_block(left) for left in lefts]
    for (array, _), (first, steps, _) in zip(rights, segments):
        ins.append((array, (array.shape[0], tile), clip(first, steps)))
    found = call(
        functools.partial(sums_kernel, side, tokens, tuple(segments)),
        "token_sums",
        (step,),
        ins,
        [((width // side, step * tile), low, (width // side, tile), lambda j: (0, j))] * side,
        2 * tokens * width * step * tile,
        12 << 20,
        scratch=[pltpu.VMEM((width, tokens), low)],
    )
    return list(found)


def mix_kernel(side, steps, core_ref, att_left, att_right, *refs):
    weights, (other_ref, mine_ref) = refs[:side], refs[side:]
    cut = att_left.shape[1]
    parts = Parts(
        side,
        lambda part: dot(att_left[...], weights[part][:, :cut], 1, 1)
        + dot(att_right[...], weights[part][:, cut:], 1, 1),
    )
    pl.when(pl.program_id(0) < steps)(lambda: write_parts(other_ref, parts, swap=True))
    pl.when(pl.program_id(0) >= steps)(lambda: write_parts(mine_ref, parts))


def mix_forward(which, att_left, att_right, weights, tile=256):
    rows, columns = att_left.shape[0] // 2, att_left.shape[1]
    width = len(weights) * weights[0].shape[0]
    steps = rows // tile

    def rows_of(i, core):
        half = jnp.where(i < steps, 1 - core[0], core[0])
        return (half * steps + i % steps, 0)

    return call(
        functools.partial(mix_kernel, len(weights), steps),
        "mix_forward",
        (2 * steps,),
        [(part, (tile, columns), rows_of) for part in (att_left, att_right)]
        + [whole_block(part) for part in weights],
        [
            ((rows, width), full, (tile, width), lambda i, core: (jnp.minimum(i, steps - 1), 0)),
            ((rows, width), full, (tile, width), lambda i, core: (jnp.maximum(i - steps, 0), 0)),
        ],
        8 * rows * columns * width,
        12 << 20,
        scalars=(which,),
    )


def mix_back_kernel(branch_ref, *refs):
    weights, out_ref = refs[:-1], refs[-1]
    out_ref[...] = contract(branch_ref, weights).astype(low)


def mix_backward(branch, weights, tile=256):
    rows, width = branch.shape
    columns = weights[0].shape[1]
    rows_of = lambda i: (i, 0)
    return call(
        mix_back_kernel,
        "mix_backward",
        (rows // tile,),
        [(branch, (tile, width), rows_of)] + [whole_block(part) for part in weights],
        [((rows, columns), low, (tile, columns), rows_of)],
        2 * rows * columns * width,
        6 << 20,
    )[0]


def forward_kernel(scale, rows, halo, q_ref, k_ref, v_ref, qs_ref, ks_ref, out_ref, bias_ref):
    block = pl.program_id(1)
    start = pl.multiple_of(block * rows, rows)
    window = halo + rows
    head_size = k_ref.shape[1]

    @pl.when(pl.program_id(0) == 0)
    def _():
        bias_ref[block] = score_bias(
            qs_ref[...], ks_ref[pl.ds(start, window), :], rows, halo
        )

    for (low_row, high_row), key_count in parts_of(rows, halo):
        keys = k_ref[pl.ds(start, key_count), :]
        values = v_ref[pl.ds(start, key_count), :]
        bias = bias_ref[block, :key_count, low_row:high_row]
        for group in range(q_ref.shape[1] // head_size):
            lanes = slice(group * head_size, (group + 1) * head_size)
            query = q_ref[low_row:high_row, lanes]
            scores = dot(keys, query, 1, 1) * scale + bias
            weights = jnp.exp2(scores)
            total = jnp.sum(weights, axis=0, keepdims=True)
            probs = (weights * (1.0 / total)).astype(low)
            mixed = dot(values, probs, 0, 0)
            out_ref[low_row:high_row, lanes] = mixed.T.astype(low)


def head_back(gradient, projected, gain, cosines, sines):
    scales = row_rms(projected)
    normed = projected * scales
    back = turn(gradient, cosines, -sines)
    gain_grad = jnp.sum(back * normed, axis=0, keepdims=True)
    back = back * gain
    mean = jnp.mean(back * normed, axis=1, keepdims=True)
    return scales * (back - normed * mean), gain_grad


def backward_kernel(
    scale, rows, halo, *refs
):
    q_ref, k_ref, v_ref, g_ref, qp_ref, kp_ref, cos_ref, sin_ref, heads_ref, qs_ref, ks_ref = refs[
        :11
    ]
    dq_ref, dk_ref, dv_ref, gains_ref, bias_ref, key_ref, value_ref = refs[11:]
    head = pl.program_id(0)
    block = pl.program_id(1)
    start = pl.multiple_of(block * rows, rows)
    window = halo + rows
    head_size = k_ref.shape[1]
    factor = head_size ** (-0.5)

    @pl.when(head == 0)
    def _():
        bias_ref[block] = score_bias(
            qs_ref[...], ks_ref[pl.ds(start, window), :], rows, halo
        )

    @pl.when((head == 0) & (block == 0))
    def _():
        gains_ref[...] = jnp.zeros_like(gains_ref)

    @pl.when(block == 0)
    def _():
        key_ref[...] = jnp.zeros_like(key_ref)
        value_ref[...] = jnp.zeros_like(value_ref)

    for (low_row, high_row), key_count in parts_of(rows, halo):
        keys = k_ref[pl.ds(start, key_count), :]
        values = v_ref[pl.ds(start, key_count), :]
        bias = bias_ref[block, :key_count, low_row:high_row]
        here = pl.ds(start + (halo + low_row), high_row - low_row)
        cosines, sines = cos_ref[here, :], sin_ref[here, :]
        key_sum = None
        value_sum = None
        for group in range(q_ref.shape[1] // head_size):
            lanes = slice(group * head_size, (group + 1) * head_size)
            query = q_ref[low_row:high_row, lanes]
            grad = g_ref[low_row:high_row, lanes]
            weights = jnp.exp2(dot(keys, query, 1, 1) * scale + bias)
            total = jnp.sum(weights, axis=0, keepdims=True)
            softmax = weights * (1.0 / total)
            prob_grad = dot(values, grad, 1, 1)
            product = softmax * prob_grad
            mean = jnp.sum(product, axis=0, keepdims=True)
            score_grad = (product - softmax * mean).astype(low)
            value_term = dot(softmax.astype(low), grad)
            key_term = dot(score_grad, query)
            value_sum = value_term if value_sum is None else value_sum + value_term
            key_sum = key_term if key_sum is None else key_sum + key_term
            query_grad = dot(keys, score_grad, 0, 0).T * factor
            query_grad, gain_grad = head_back(
                query_grad,
                qp_ref[low_row:high_row, lanes].astype(full),
                heads_ref[2:3, :],
                cosines,
                sines,
            )
            dq_ref[low_row:high_row, lanes] = query_grad.astype(low)
            gains_ref[0:1, :] += gain_grad
        key_ref[pl.ds(start, key_count), :] += key_sum * factor
        value_ref[pl.ds(start, key_count), :] += value_sum

    @pl.when(block == pl.num_programs(1) - 1)
    def _():
        dv_ref[...] = value_ref[...].astype(low)
        for row in range(0, k_ref.shape[0], halo):
            here = slice(row, row + halo)
            key_grad, gain_grad = head_back(
                key_ref[here, :],
                kp_ref[here, :].astype(full),
                heads_ref[3:4, :],
                cos_ref[here, :],
                sin_ref[here, :],
            )
            dk_ref[here, :] = key_grad.astype(low)
            gains_ref[1:2, :] += gain_grad


def attention_forward(
    queries, keys, values, query_segments, key_segments, rows, halo, head_size, first, heads
):
    token_count = queries.shape[0]
    lanes = queries.shape[1] // (keys.shape[1] // head_size)
    window = halo + token_count
    scale = head_size ** (-0.5) / math.log(2.0)
    q_at, k_at = lambda h, b: (b, first + h), lambda h, b: (0, first + h)
    shape = (token_count, heads * lanes)
    return call(
        functools.partial(forward_kernel, scale, rows, halo),
        "attention_forward",
        (heads, token_count // rows),
        [
            (queries, (rows, lanes), q_at),
            (keys, (window, head_size), k_at),
            (values, (window, head_size), k_at),
            (query_segments, (1, rows), lambda h, b: (0, b)),
            whole_block(key_segments),
        ],
        [(shape, low, (rows, lanes), lambda h, b: (b, h))],
        4 * token_count * heads * lanes * (halo + rows),
        4 << 20,
        scratch=[pltpu.VMEM((token_count // rows, halo + rows, rows), full)],
        transcendentals=token_count * heads * lanes // head_size * (halo + rows),
    )[0]


def attention_backward(
    queries, keys, values, grads, query_proj, key_proj, cosines, sines, heads_gain,
    query_segments, key_segments, rows, halo, head_size,
):
    token_count = queries.shape[0]
    heads = keys.shape[1] // head_size
    lanes = queries.shape[1] // heads
    window = halo + token_count
    scale = head_size ** (-0.5) / math.log(2.0)
    q_at, k_at, fixed = lambda h, b: (b, h), lambda h, b: (0, h), lambda h, b: (0, 0)
    return call(
        functools.partial(backward_kernel, scale, rows, halo),
        "attention_backward",
        (heads, token_count // rows),
        [
            (queries, (rows, lanes), q_at),
            (keys, (window, head_size), k_at),
            (values, (window, head_size), k_at),
            (grads, (rows, lanes), q_at),
            (query_proj, (rows, lanes), q_at),
            (key_proj, (window, head_size), k_at),
            whole_block(cosines),
            whole_block(sines),
            whole_block(heads_gain),
            (query_segments, (1, rows), lambda h, b: (0, b)),
            whole_block(key_segments),
        ],
        [
            (queries.shape, low, (rows, lanes), q_at),
            (keys.shape, low, (window, head_size), k_at),
            (keys.shape, low, (window, head_size), k_at),
            ((8, head_size), full, (8, head_size), fixed),
        ],
        10 * queries.size * (halo + rows),
        24 << 20,
        scratch=[
            pltpu.VMEM((token_count // rows, halo + rows, rows), full),
            pltpu.VMEM((window, head_size), full),
            pltpu.VMEM((window, head_size), full),
        ],
        least=48 << 20,
        transcendentals=queries.size // head_size * (halo + rows),
    )


def per_device(
    tokens,
    segments,
    norm_gain,
    q_weight,
    k_weight,
    v_weight,
    o_weight,
    q_gain,
    k_gain,
    mlp_gain,
    gate_weight,
    up_weight,
    down_weight,
    cotangent,
):
    net = Slice()
    row_count, width = tokens.shape
    halo = row_count // 2
    chip_rows = 2 * row_count
    weight_rows = q_weight.shape[0]
    head_size = q_gain.shape[0] * net.count
    gain_rows = q_gain.shape[0]

    q_cols, k_cols, o_cols, ff_cols = (
        weight.shape[1] // 2 for weight in (q_weight, k_weight, o_weight, gate_weight)
    )
    unit = 2 * weight_rows
    side = net.side
    which = net.core.astype(jnp.int32).reshape(1)

    column = lax.broadcasted_iota(jnp.int32, (weight_rows, 128), 1)
    extras = jnp.zeros((weight_rows, 128), low)
    for at, gain in enumerate((norm_gain, mlp_gain, q_gain, k_gain)):
        gain = jnp.pad(gain, (0, weight_rows - gain.shape[0]))
        extras = jnp.where(column == at, gain[:, None], extras)

    def chip_block(*parts):
        mine, other = [], []
        for weight, start, end in parts:
            half = weight.shape[1] // 2 if end is not None else 0
            for to, core in ((mine, net.core), (other, 1 - net.core)):
                if end is None:
                    to.append(weight)
                else:
                    to.append(
                        lax.dynamic_slice_in_dim(weight, core * half + start, end - start, 1)
                    )
        return net.by_core(jnp.concatenate(mine, 1), net.pair(jnp.concatenate(other, 1)))

    block_qkv = chip_block(
        (q_weight, 0, q_cols), (extras, 0, None), (k_weight, 0, k_cols), (v_weight, 0, k_cols)
    )
    z_qkv = [block_qkv, net.ring(block_qkv, 1), net.ring(block_qkv, -1)]
    z_one, z_three, tokens, segments, o_weight, gate_weight, up_weight, down_weight = barrier(
        (
            z_qkv[1], z_qkv[2], tokens, segments, o_weight, gate_weight, up_weight, down_weight
        )
    )
    z_qkv = [block_qkv, z_one, net.ring(z_one, 1), z_three]
    block_rest = chip_block(
        (down_weight, 0, ff_cols), (o_weight, 0, o_cols), (gate_weight, 0, ff_cols),
        (up_weight, 0, ff_cols),
    )
    block_down, block_mlp = block_rest[:, :ff_cols], block_rest[:, ff_cols:]
    z_mlp = [block_mlp, net.ring(block_mlp, 1)]
    numbers = jnp.broadcast_to(segments.astype(low)[:, None], (row_count, 128))
    own_tokens = jnp.concatenate([tokens, numbers], 1)
    before = net.last_core_along(own_tokens[row_count - halo :], 1)
    places = net.places(net.chip, unit)
    order = (jnp.arange(width, dtype=jnp.int32)[:, None] == places[None, :]).astype(low)
    head_places = net.places(net.chip, 2 * gain_rows)
    head_order = (
        jnp.arange(head_size, dtype=jnp.int32)[:, None] == head_places[None, :]
    ).astype(full)
    entry = jnp.arange(width, dtype=jnp.int32)
    gain_place = places // weight_rows * gain_rows + entry % weight_rows
    pick = (
        (entry % weight_rows < gain_rows)[:, None]
        & (gain_place[:, None] == jnp.arange(head_size, dtype=jnp.int32)[None, :])
    ).astype(low)
    plane_down = jnp.stack(net.gather_plane(block_down, 0))
    z_qkv, plane_down, own_tokens, before, order, pick, z_mlp, cotangent = barrier(
        (z_qkv, plane_down, own_tokens, before, order, pick, z_mlp, cotangent)
    )

    (qkv,) = stack_cut(z_qkv, ())
    qkv = net.gather_plane(qkv, 0)
    z_mlp.append(net.ring(z_mlp[-1], 1))
    plane_down = jnp.stack(net.gather_plane(plane_down, 1))
    plane_down = plane_down.reshape(side * side * unit, ff_cols)
    both = place(which, own_tokens, net.pair(own_tokens))
    before = jnp.where(net.core == 0, net.pair(before), before)
    qkv, z_mlp, plane_down, both, before = barrier((qkv, z_mlp, plane_down, both, before))

    (qkv,) = stack_cut(qkv, ())
    qkv = net.gather_plane(qkv, 1)
    z_mlp.append(net.ring(z_mlp[-1], 1))
    chip_tokens, before_tokens = both[:, :width], before[:, :width]
    chip_segments = both[:, width].astype(jnp.int32)
    before_segments = jnp.where(net.chip > 0, before[:, width].astype(jnp.int32), -1)
    window_tokens = jnp.concatenate([before_tokens, chip_tokens])
    window_segments = jnp.concatenate([before_segments, chip_segments])
    counter = jnp.arange(halo + chip_rows, dtype=jnp.int32)
    changes = jnp.concatenate([jnp.ones((1,), bool), window_segments[1:] != window_segments[:-1]])
    starts = lax.cummax(jnp.where(changes, counter, 0), axis=0)
    offsets = (counter - starts).astype(full)
    frequency = jnp.exp(
        (jnp.arange(head_size, dtype=jnp.int32) % (head_size // 2)).astype(full)
        * (-2.0 * math.log(rope_base) / head_size)
    )
    angles = offsets[:, None] * frequency[None, :]
    cosines = jnp.cos(angles)
    sines = jnp.sin(angles) * jnp.where(jnp.arange(head_size) < head_size // 2, -1.0, 1.0)
    query_segments = chip_segments[None, :]
    key_segments = window_segments[:, None]
    ordered = dot(window_tokens, order, kind=low)
    qkv, z_mlp, plane_down, ordered, cosines, sines = barrier(
        (qkv, z_mlp, plane_down, ordered, cosines, sines)
    )

    own_cotangent = dot(cotangent, order, kind=low)
    (mlp,) = stack_cut(z_mlp, ())
    mlp = net.gather_plane(mlp, 0)
    z_down = [plane_down, net.ring(plane_down, 1)]
    attn_in, queries, keys, values, query_proj, key_proj, gain_rows_full, heads_gain = project(
        ordered, cosines, sines, pick, qkv, q_cols, k_cols, halo
    )
    gain_one, gain_two = gain_rows_full[0], gain_rows_full[1]
    kv_heads = k_cols // head_size

    def attend(first):
        return attention_forward(
            queries, keys, values, query_segments, key_segments, row_count, halo, head_size,
            first, kv_heads // 2,
        )

    att_left = attend(0)
    att_left, mlp, z_down, queries, keys, values, own_cotangent = barrier(
        (att_left, mlp, z_down, queries, keys, values, own_cotangent)
    )

    other_cotangent = net.pair(net.swapped(own_cotangent))
    cotangents = jnp.concatenate([own_cotangent, other_cotangent])
    mix, mlp = stack_cut(mlp, (o_cols,))
    mix = net.gather_plane(mix, 1)
    att_right = attend(kv_heads // 2)
    z_down.append(net.ring(z_down[-1], 1))
    att_left, att_right, mix, mlp, cotangents, z_down = barrier(
        (att_left, att_right, mix, mlp, cotangents, z_down)
    )

    mlp = net.gather_plane(mlp, 1)
    z_down.append(net.ring(z_down[-1], 1))
    own_inputs = lax.dynamic_slice_in_dim(ordered, halo + net.core * row_count, row_count).astype(
        full
    )
    branch_other, branch_mine = mix_forward(which, att_left, att_right, mix)
    hidden_state = own_inputs + (branch_mine + net.pair_in(branch_other, 4))
    scale_two = inverse_rms(hidden_state)
    normed_two = hidden_state * scale_two
    mlp_own = (normed_two * gain_two).astype(low)
    mlp_other = net.pair_in(net.swapped(mlp_own), 2)
    mlp_own, mlp_other, mlp, z_down = barrier((mlp_own, mlp_other, mlp, z_down))

    activated, to_gate, to_up = gate_forward(mlp_own, mlp_other, mlp)
    down_sums = token_sums(side, [cotangents], [(activated, 0)])
    activated, to_gate, to_up, down_sums, z_down = barrier(
        (activated, to_gate, to_up, down_sums, z_down)
    )

    def plus(array, *terms):
        return sum([term.astype(full) for term in terms], array.astype(full)).astype(array.dtype)

    def inner(terms):
        size = terms[0].shape[0] // side
        sent = [
            plus(*[term[at * size : (at + 1) * size] for term in terms]) for at in range(1, side)
        ]
        return [term[:size] for term in terms], [None] + sent

    down_in = net.scatter_plane(down_sums, 1)
    gate_grad, up_grad = act_backward(cotangents, to_gate, to_up, z_down, unit)
    mlp_sums = token_sums(side, [mlp_own, mlp_other], [(gate_grad, 0), (up_grad, 0)])
    gate_grad, up_grad, mlp_sums, down_sum, activated = barrier(
        (gate_grad, up_grad, mlp_sums, down_sums[:1] + down_in, activated)
    )

    mlp_in = net.scatter_plane(mlp_sums, 1)
    z_down_sum = plus(*down_sum).reshape(side, 4, unit, ff_cols)
    z_down_sum = net.scatter_z([z_down_sum[:, m] for m in range(4)])
    mlp_grad_other, mlp_grad_mine = mlp_backward(gate_grad, up_grad, mlp)
    mlp_in_grad = mlp_grad_mine + net.pair_in(mlp_grad_other, 4)
    hidden_grad = own_cotangent.astype(full) + norm_back(
        mlp_in_grad * gain_two, normed_two, scale_two
    )
    branch_own = hidden_grad.astype(low)
    branch_low = place(which, branch_own, net.pair_in(net.swapped(branch_own), 2))
    attended_grad = mix_backward(branch_low, mix)
    mix_sums = token_sums(side, [branch_low], [(att_left, 0), (att_right, 0)])
    out_other, out_mine = down_forward(activated, z_down, side, unit)
    mixed_out = hidden_state + (out_mine + net.pair_in(out_other, 4))
    mixed_out = dot(mixed_out.astype(low), order, 1, 1, low)
    attended_grad, mix_sums, mlp_in_grad, mlp_sum, mixed_out, z_down_sum = barrier(
        (attended_grad, mix_sums, mlp_in_grad, mlp_sums[:1] + mlp_in, mixed_out, z_down_sum)
    )

    mlp_sum, mlp_sent = inner(mlp_sum)
    mlp_in = net.scatter_plane(mlp_sent, 0)
    mix_in = net.scatter_plane(mix_sums, 1)
    z_down_sum = net.scatter_z_last(z_down_sum)
    query_low, key_low, value_low, gain_grads = attention_backward(
        queries, keys, values, attended_grad, query_proj, key_proj, cosines, sines, heads_gain,
        query_segments, key_segments, row_count, halo, head_size,
    )
    query_low, key_low, value_low, mlp_sum, mix_sum, z_down_sum = barrier(
        (query_low, key_low, value_low, mlp_sum + mlp_in, mix_sums[:1] + mix_in, z_down_sum)
    )

    mix_sum, mix_sent = inner(mix_sum)
    mix_in = net.scatter_plane(mix_sent, 0)
    z_mlp = jnp.split(plus(*mlp_sum), 4)
    down_sum = plus(*z_down_sum)
    down_in = net.scatter_plane([down_sum[m] for m in range(side)], 0)
    later = net.chip_along(jnp.concatenate([key_low[:halo], value_low[:halo]], 1), -1)
    qkv_sums = token_sums(side, [attn_in], [(query_low, halo), (key_low, 0), (value_low, 0)])
    qkv_sums, query_low, mlp_in_grad, mix_sum, z_mlp, down_sum, later = barrier(
        (
            qkv_sums, query_low, mlp_in_grad, mix_sum + mix_in, z_mlp, [down_sum[0]] + down_in,
            later,
        )
    )

    qkv_in = net.scatter_plane(qkv_sums, 1)
    z_mlp = net.scatter_z(z_mlp)
    gain_two_grad = jnp.sum(mlp_in_grad * normed_two, axis=0, keepdims=True)
    head_gains = dot(gain_grads[:2], head_order)
    z_mix = jnp.split(plus(*mix_sum), 4)
    grad_other, grad_mine = input_backward(which, query_low, key_low, value_low, later, qkv)
    qkv_sum, z_mlp, grad_other, grad_mine, z_mix, gain_two_grad, head_gains = barrier(
        (
            qkv_sums[:1] + qkv_in, z_mlp, grad_other, grad_mine, z_mix, gain_two_grad, head_gains,
        )
    )

    qkv_sum, qkv_sent = inner(qkv_sum)
    qkv_in = net.scatter_plane(qkv_sent, 0)
    z_mlp = net.scatter_z_last(z_mlp)
    z_mix = net.scatter_z(z_mix)
    grad_sent = net.pair(grad_other)
    qkv_sum, z_mlp, z_mix, grad_mine, grad_sent = barrier(
        (qkv_sum + qkv_in, z_mlp, z_mix, grad_mine, grad_sent)
    )

    z_qkv = jnp.split(plus(*qkv_sum), 4)
    z_qkv = [z_qkv[0]] + [net.ring(z_qkv[m], -m) for m in range(1, 4)]
    z_mix = net.scatter_z_last(z_mix)
    input_grad, gain_one_grad = finish_tokens(
        grad_mine, grad_sent, own_inputs, hidden_grad, gain_rows_full
    )
    gains = jnp.concatenate([gain_one_grad[:1], gain_two_grad])

    def gain_parts(gains, heads):
        count = side if gains.shape[1] > width // (side * side) else 4
        return [
            jnp.concatenate(both, 1)
            for both in zip(jnp.split(gains, count, 1), jnp.split(heads, count, 1))
        ]

    def gain_cut(array):
        at = array.shape[1] * width // (width + head_size)
        return array[:, :at], array[:, at:]

    gains = gain_parts(gains, head_gains)
    gains = plus(gains[0], *net.scatter_plane(gains, 1))
    gains = gain_parts(*gain_cut(gains))
    gains = plus(gains[0], *net.scatter_plane(gains, 0))
    rest_mine, rest_other = fold(which, z_mlp, down_sum)
    rest_other = net.pair(rest_other)
    z_qkv, gains, rest_mine, rest_other, input_grad, z_mix = barrier(
        (z_qkv, gains, rest_mine, rest_other, input_grad, z_mix)
    )

    input_grad = dot(input_grad, order, 1, 1, low)
    z_mine, z_other = fold(which, z_qkv, z_mix)
    z_other = net.pair(z_other)
    gains = gain_parts(*gain_cut(gains))
    gains = sum([net.ring(gains[m], -m) for m in range(1, 4)], gains[0])
    gains, heads = gain_cut(gains)
    gains = jnp.concatenate(
        [gains[:1, :weight_rows], gains[1:, :weight_rows], heads[:1, :gain_rows],
         heads[1:, :gain_rows], gains[:1, weight_rows:], gains[1:, weight_rows:],
         heads[:1, gain_rows:], heads[1:, gain_rows:]], 1,
    ).reshape(2, -1)
    gain_mine = jnp.where(net.core == 0, gains[0], gains[1])
    gain_other = jnp.where(net.core == 0, gains[1], gains[0])
    gain_sum = gain_mine + net.pair(gain_other)
    ends = [0]
    for size in (ff_cols, ff_cols, ff_cols):
        ends.append(ends[-1] + size)
    gate_out, up_out, down_out = join(
        which, rest_mine, rest_other, *[((start, end),) for start, end in zip(ends[:-1], ends[1:])]
    )
    v_at = q_cols + k_cols
    o_at = v_at + k_cols
    q_out, k_out, v_out, o_out = join(
        which, z_mine, z_other, ((0, q_cols),), ((q_cols, v_at),), ((v_at, o_at),),
        ((o_at, o_at + o_cols),),
    )
    return (
        mixed_out,
        input_grad,
        gain_sum[:weight_rows],
        q_out,
        k_out,
        v_out,
        o_out,
        gain_sum[2 * weight_rows : 2 * weight_rows + gain_rows],
        gain_sum[2 * weight_rows + gain_rows :],
        gain_sum[weight_rows : 2 * weight_rows],
        gate_out,
        up_out,
        down_out,
    )


def solution(mesh):
    rows = P("dp", None)
    line = P("dp")
    return jax.shard_map(
        per_device,
        mesh=mesh,
        in_specs=(
            rows, line, line, rows, rows, rows, rows, line, line, line, rows, rows, rows, rows,
        ),
        out_specs=(
            rows, rows, line, rows, rows, rows, rows, line, line, line, rows, rows, rows,
        ),
        check_vma=False,
    )
```

time: 561 us -> 442 us (0.79)
  waiting for transfers between devices: 207 us -> 158 us
  matrix products: 47.7 us -> 11.5 us
  Pallas kernels: 108 us -> 135 us
  other arithmetic: 51.7 us -> 26.2 us
  starting transfers between devices: 97.4 us -> 77.3 us
  local copies, waits for them, and re-layouts: 35.7 us -> 23.1 us
    ppermute x71 -> x43, waiting for transfers between devices: 101 us -> 57.4 us  [the longest x17 48.3 us: plane(): return lax.ppermute(array, 'dp', pairs)]
    dot_general x14 -> x5, matrix products: 47.7 us -> 11.5 us  [dot(): lax.dot_general(left_side, right_side, (((left_dim,), (right_dim,)), ((),...]
    pallas_call x10 -> x26, Pallas kernels: 108 us -> 135 us  [call(): pl.pallas_call(kernel, grid_spec=pltpu.PrefetchScalarGridSpec(num_scalar_...]
    ppermute x71 -> x43, starting transfers between devices: 62.6 us -> 40.4 us  [the longest x17 33.7 us: plane(): return lax.ppermute(array, 'dp', pairs)]
    select_n x13 -> x2, other arithmetic: 14.4 us -> 0.17 us  [by_core(): jnp.where(self.core == 0, jnp.concatenate([mine, other], axis=axis), jnp....]
    convert_element_type x13, other arithmetic: 18.7 us -> 12.1 us  [the longest x8 7.43 us: plus(): sum([term.astype(full) for term in terms], array.astype(full))]
    unnamed x248 -> x116, local copies, waits for them, and re-layouts: 14.9 us -> 8.72 us
    ppermute x27 -> x24, starting transfers between devices: 29.8 us -> 35.7 us  [ring(): lax.ppermute(array, 'dp', [(i, (i + step) % self.count) for i in range(se...]
  transfers between devices with their start and end apart: 100 -> 68, of which waited for: 33 -> 30; matrix products, arithmetic and copies ran while one was open for 18% -> 9% of each run, Pallas kernels for 17% -> 26%
where the time goes in v3:
time: 442 us; the launch traced here: 434 us
  waiting for transfers between devices  158 us (36%)
  Pallas kernels  135 us (31%)
  starting transfers between devices  77.3 us (17%)
  other arithmetic  26.2 us (6%)
  local copies, waits for them, and re-layouts  23.1 us (5%)
  matrix products  11.5 us (3%)
    pallas_call x26, Pallas kernels, call(): pl.pallas_call(kernel, grid_spec=pltpu.PrefetchScalarGridSpec(num_scalar_...  135 us
    ppermute x24, waiting for transfers between devices, ring(): lax.ppermute(array, 'dp', [(i, (i + step) % self.count) for i in range(se...  96.6 us
    ppermute x17, waiting for transfers between devices, plane(): return lax.ppermute(array, 'dp', pairs)  48.3 us
    ppermute x24, starting transfers between devices, ring(): lax.ppermute(array, 'dp', [(i, (i + step) % self.count) for i in range(se...  35.7 us
    ppermute x17, starting transfers between devices, plane(): return lax.ppermute(array, 'dp', pairs)  33.7 us
    dot_general x5, matrix products, dot(): lax.dot_general(left_side, right_side, (((left_dim,), (right_dim,)), ((),...  11.5 us
    ppermute x25, waiting for transfers between devices, pair(): return lax.ppermute(array, 'dp', [(i, i ^ 1) for i in range(self.count)])  9.06 us
  transfers between devices with their start and end apart: 68, of which 30 were waited for; matrix products, arithmetic and copies ran while one was open for 9% of the time, Pallas kernels for 26%

profile of v3, /device:TPU:0, one launch (start us, length us, event | category | flops | bytes accessed | tf_op | source)
XLA Modules:
  0.0 434.2 jit_solution(703990133497036111)
XLA Ops:
  6.3 5.0 %collective-permute-start.2 = (bf16[64,2176]{1,0:T(8,128)(2,1)S(1)}, bf16[64,2176]{1,0:T(8,128)(2,1)S(1)}, u32[]{:S(2)}, u32[]{:S(2)}) collective-permute-start(bf16[64,2176]{1,0:T(8,128)(2,1)S(1)} %maximum_select_fusion.1.refs_0_), channel_id=1, source_target_pairs={{0,24},{1,25},{2,26},{3,27},{4,28},{5,29},{6,30},{7,31},{8,0},{9,1... | collective-permute-start | bytes 835592 | tf_op jit(solution)/shard_map/ppermute | solution.py:57
  11.4 2.2 fusion
  13.6 4.8 %collective-permute-done.2.refs_3_ = bf16[64,2176]{1,0:T(8,128)(2,1)S(1)} collective-permute-done((bf16[64,2176]{1,0:T(8,128)(2,1)S(1)}, bf16[64,2176]{1,0:T(8,128)(2,1)S(1)}, u32[]{:S(2)}, u32[]{:S(2)}) %collective-permute-start.2) | collective-permute-done | bytes 278560 | tf_op jit(solution)/shard_map/ppermute | solution.py:57
  18.4 6.0 %collective-permute-done.1.refs_1_ = bf16[64,2176]{1,0:T(8,128)(2,1)S(1)} collective-permute-done((bf16[64,2176]{1,0:T(8,128)(2,1)S(1)}, bf16[64,2176]{1,0:T(8,128)(2,1)S(1)}, u32[]{:S(2)}, u32[]{:S(2)}) %collective-permute-start.1) | collective-permute-done | bytes 278560 | tf_op jit(solution)/shard_map/ppermute | solution.py:57
  30.2 9.4 %collective-permute-done.5 = bf16[64,1536]{1,0:T(8,128)(2,1)S(1)} collective-permute-done((bf16[64,1536]{1,0:T(8,128)(2,1)S(1)}, bf16[64,1536]{1,0:T(8,128)(2,1)S(1)}, u32[]{:S(2)}, u32[]{:S(2)}) %collective-permute-start.5) | collective-permute-done | bytes 196640 | tf_op jit(solution)/shard_map/ppermute | solution.py:77
  39.7 8.1 %collective-permute-done.7.refs_1_ = bf16[64,4096]{1,0:T(8,128)(2,1)S(1)} collective-permute-done((bf16[64,4096]{1,0:T(8,128)(2,1)S(1)}, bf16[64,4096]{1,0:T(8,128)(2,1)S(1)}, u32[]{:S(2)}, u32[]{:S(2)}) %collective-permute-start.7) | collective-permute-done | bytes 524320 | tf_op jit(solution)/shard_map/ppermute | solution.py:57
  49.7 5.1 %collective-permute-start.8 = (bf16[256,2176]{1,0:T(8,128)(2,1)S(1)}, bf16[256,2176]{1,0:T(8,128)(2,1)S(1)}, u32[]{:S(2)}, u32[]{:S(2)}) collective-permute-start(bf16[256,2176]{1,0:T(8,128)(2,1)S(1)} %stack_cut.4.refs_0_), channel_id=1, source_target_pairs={{0,4},{1,3},{2,6},{3,1},{4,0},{5,7},{6,2},{7,5},{8,12},{9,11},{10,... | collective-permute-start | bytes 3342344 | tf_op jit(solution)/shard_map/ppermute | solution.py:77
  59.0 10.8 %collective-permute-done.9.refs_2_ = bf16[64,4096]{1,0:T(8,128)(2,1)S(1)} collective-permute-done((bf16[64,4096]{1,0:T(8,128)(2,1)S(1)}, bf16[64,4096]{1,0:T(8,128)(2,1)S(1)}, u32[]{:S(2)}, u32[]{:S(2)}) %collective-permute-start.9) | collective-permute-done | bytes 524320 | tf_op jit(solution)/shard_map/ppermute | solution.py:57
  78.4 2.2 collective-permute-start.14
  80.8 5.4 %fusion.1.x_ref = bf16[1280,1024]{1,0:T(8,128)(2,1)S(1)} fusion(bf16[1024,1024]{1,0:T(8,128)(2,1)} %fusion, bf16[1024,1024]{1,0:T(8,128)(2,1)} %slice.213, bf16[256,1024]{1,0:T(8,128)(2,1)} %slice.212), kind=kOutput, calls=%fused_computation.5 | convolution fusion | flops 2689597440 | bytes 7340032 | tf_op jit(solution)/shard_map/dot_general | solution.py:19
  86.3 2.4 fusion.10
  88.6 5.9 %collective-permute-done.14.refs_3_ = bf16[64,4096]{1,0:T(8,128)(2,1)S(1)} collective-permute-done((bf16[64,4096]{1,0:T(8,128)(2,1)}, bf16[64,4096]{1,0:T(8,128)(2,1)S(1)}, u32[]{:S(2)}, u32[]{:S(2)}) %collective-permute-start.14) | collective-permute-done | bytes 524320 | tf_op jit(solution)/shard_map/ppermute | solution.py:57
  94.5 5.4 %collective-permute-done.13.refs_1_ = bf16[512,2176]{1,0:T(8,128)(2,1)} collective-permute-done((bf16[512,2176]{1,0:T(8,128)(2,1)}, bf16[512,2176]{1,0:T(8,128)(2,1)}, u32[]{:S(2)}, u32[]{:S(2)}) %collective-permute-start.13) | collective-permute-done | bytes 2228256 | tf_op jit(solution)/shard_map/ppermute | solution.py:77
  104.8 11.0 %project.1 = (bf16[1280,1024]{1,0:T(8,128)(2,1)S(1)}, bf16[1024,1024]{1,0:T(8,128)(2,1)S(1)}, bf16[1280,512]{1,0:T(8,128)(2,1)S(1)}, bf16[1280,512]{1,0:T(8,128)...) custom-call(bf16[1280,1024]{1,0:T(8,128)(2,1)S(1)} %fusion.1.x_ref, ...), custom_call_target="tpu_custom_call" | custom-call | flops 5368709120 | bytes 20971520 | tf_op jit(solution)/shard_map/project/pallas_call | solution.py:309
  118.7 8.6 %attention_forward.2.att_left.refs_1_ = bf16[1024,512]{1,0:T(8,128)(2,1)S(1)} custom-call(bf16[1024,1024]{1,0:T(8,128)(2,1)S(1)} %get-tuple-element.257.q_ref.refs_0_, bf16[1280,512]{1,0:T(8,128)(2,1)S(1)} %get-tuple-element.258.k_ref.refs_1_, bf16[1280,512]{1,0:T(8,128)(2,1)S(1)} %get-tuple-element.259.v_ref.refs_2_, s32[1,1024]{1,0:T(1,128)S(1)} %bitcast.54, ...), custom_call_target="tpu_custom_call" | custom-call | flops 1610612736 | bytes 4194304 | tf_op jit(solution)/shard_map/attention_forward/pallas_call | solution.py:309
  132.0 8.7 %attention_forward.3.att_right.refs_2_ = bf16[1024,512]{1,0:T(8,128)(2,1)S(1)} custom-call(bf16[1024,1024]{1,0:T(8,128)(2,1)S(1)} %get-tuple-element.257.q_ref.refs_0_, bf16[1280,512]{1,0:T(8,128)(2,1)S(1)} %get-tuple-element.258.k_ref.refs_1_, bf16[1280,512]{1,0:T(8,128)(2,1)S(1)} %get-tuple-element.259.v_ref.refs_2_, s32[1,1024]{1,0:T(1,128)S(1)} %bitcast.55, ...), custom_call_target="tpu_custom_call" | custom-call | flops 1610612736 | bytes 4194304 | tf_op jit(solution)/shard_map/attention_forward/pallas_call | solution.py:309
  140.9 11.2 %collective-permute-done.19.refs_2_ = bf16[256,1536]{1,0:T(8,128)(2,1)S(1)} collective-permute-done((bf16[256,1536]{1,0:T(8,128)(2,1)S(1)}, bf16[256,1536]{1,0:T(8,128)(2,1)S(1)}, u32[]{:S(2)}, u32[]{:S(2)}) %collective-permute-start.19) | collective-permute-done | bytes 786464 | tf_op jit(solution)/shard_map/ppermute | solution.py:57
  154.0 3.1 mix_forward.1
  163.6 2.9 multiply_reduce_fusion.2
  170.9 12.0 %collective-permute-done.27.refs_3_ = bf16[256,1536]{1,0:T(8,128)(2,1)S(1)} collective-permute-done((bf16[256,1536]{1,0:T(8,128)(2,1)}, bf16[256,1536]{1,0:T(8,128)(2,1)S(1)}, u32[]{:S(2)}, u32[]{:S(2)}) %collective-permute-start.27) | collective-permute-done | bytes 786464 | tf_op jit(solution)/shard_map/ppermute | solution.py:57
  182.9 6.8 %collective-permute-done.26.refs_1_.refs_3_ = bf16[512,3072]{1,0:T(8,128)(2,1)} collective-permute-done((bf16[512,3072]{1,0:T(8,128)(2,1)}, bf16[512,3072]{1,0:T(8,128)(2,1)}, u32[]{:S(2)}, u32[]{:S(2)}) %collective-permute-start.26) | collective-permute-done | bytes 3145760 | tf_op jit(solution)/shard_map/ppermute | solution.py:77
  189.7 10.1 %gate_forward.1 = (bf16[1024,1536]{1,0:T(8,128)(2,1)S(1)}, bf16[1024,1536]{1,0:T(8,128)(2,1)S(1)}, bf16[1024,1536]{1,0:T(8,128)(2,1)S(1)}) custom-call(bf16[512,1024]{1,0:T(8,128)(2,1)S(1)} %multiply_convert_fusion.xm_ref.refs_0_, bf16[512,1024]{1,0:T(8,128)(2,1)S(1)} %pad_maximum_fusion.4.xo_ref.refs_1_, ...), custom_call_target="tpu_custom_call" | custom-call | flops 6442450944 | bytes 16777216 | tf_op jit(solution)/shard_map/gate_forward/pallas_call | solution.py:309
  199.9 4.7 %token_sums.4 = (bf16[512,1536]{1,0:T(8,128)(2,1)S(1)}, bf16[512,1536]{1,0:T(8,128)(2,1)S(1)}) custom-call(bf16[1024,1024]{1,0:T(8,128)(2,1)S(1)} %pad_maximum_fusion.refs_0_.gb_ref, bf16[1024,1536]{1,0:T(8,128)(2,1)S(1)} %get-tuple-element.312.refs_1_.act_ref), custom_call_target="tpu_custom_call" | custom-call | flops 3221225472 | bytes 12582912 | tf_op jit(solution)/shard_map/token_sums/pallas_call | solution.py:309
  206.5 5.1 %act_backward.1 = (bf16[1024,1536]{1,0:T(8,128)(2,1)S(1)}, bf16[1024,1536]{1,0:T(8,128)(2,1)S(1)}) custom-call(bf16[1024,1024]{1,0:T(8,128)(2,1)S(1)} %pad_maximum_fusion.refs_0_.gb_ref, bf16[1024,1536]{1,0:T(8,128)(2,1)S(1)} %get-tuple-element.291.to_gate_ref, bf16[1024,1536]{1,0:T(8,128)(2,1)S(1)} %get-tuple-element.292.to_up_ref, ...), custom_call_target="tpu_custom_call" | custom-call | flops 3221225472 | bytes 16777216 | tf_op jit(solution)/shard_map/act_backward/pallas_call | solution.py:309
  211.7 8.9 %token_sums.5 = (bf16[512,3072]{1,0:T(8,128)(2,1)S(1)}, bf16[512,3072]{1,0:T(8,128)(2,1)S(1)}) custom-call(bf16[512,1024]{1,0:T(8,128)(2,1)S(1)} %multiply_convert_fusion.xm_ref.refs_0_, bf16[512,1024]{1,0:T(8,128)(2,1)S(1)} %pad_maximum_fusion.4.xo_ref.refs_1_, bf16[1024,1536]{1,0:T(8,128)(2,1)S(1)} %get-tuple-element.304.refs_2_.gate_ref, ...), custom_call_target="tpu_custom_call" | custom-call | flops 6442450944 | bytes 12582912 | tf_op jit(solution)/shard_map/token_sums/pallas_call | solution.py:309
  220.6 4.5 %collective-permute-done.28 = bf16[512,1536]{1,0:T(8,128)(2,1)S(1)} collective-permute-done((bf16[512,1536]{1,0:T(8,128)(2,1)S(1)}, bf16[512,1536]{1,0:T(8,128)(2,1)S(1)}, u32[]{:S(2)}, u32[]{:S(2)}) %collective-permute-start.28) | collective-permute-done | bytes 1572896 | tf_op jit(solution)/shard_map/ppermute | solution.py:77
  225.1 4.1 down_forward.1
  230.5 10.4 %mlp_backward.1 = (f32[512,1024]{1,0:T(8,128)S(1)}, f32[512,1024]{1,0:T(8,128)S(1)}) custom-call(bf16[1024,1536]{1,0:T(8,128)(2,1)S(1)} %get-tuple-element.304.refs_2_.gate_ref, bf16[1024,1536]{1,0:T(8,128)(2,1)S(1)} %get-tuple-element.305.refs_3_.up_ref, bf16[512,3072]{1,0:T(8,128)(2,1)} %get-tuple-element.280.refs_0_.refs_2_, ...), custom_call_target="tpu_custom_call" | custom-call | flops 6442450944 | bytes 16777216 | tf_op jit(solution)/shard_map/mlp_backward/pallas_call | solution.py:309
  251.1 3.8 collective-permute-start.40
  254.9 2.4 fusion.8
  259.0 2.9 mix_backward.1.refs_3_
  263.3 3.3 token_sums.6
  266.6 4.1 collective-permute-done.40
  270.7 12.8 %collective-permute-done.35 = bf16[512,3072]{1,0:T(8,128)(2,1)S(1)} collective-permute-done((bf16[512,3072]{1,0:T(8,128)(2,1)S(1)}, bf16[512,3072]{1,0:T(8,128)(2,1)S(1)}, u32[]{:S(2)}, u32[]{:S(2)}) %collective-permute-start.35) | collective-permute-done | bytes 3145760 | tf_op jit(solution)/shard_map/ppermute | solution.py:77
  289.9 30.5 %attention_backward.1 = (bf16[1024,1024]{1,0:T(8,128)(2,1)}, bf16[1280,512]{1,0:T(8,128)(2,1)S(1)}, bf16[1280,512]{1,0:T(8,128)(2,1)S(1)}, f32[8,128]{1,0:T(8,128)S(1)}) custom-call(bf16[1024,1024]{1,0:T(8,128)(2,1)} %copy-done.2, bf16[1280,512]{1,0:T(8,128)(2,1)S(1)} %copy-done.4, bf16[1280,512]{1,0:T(8,128)(2,1)} %copy-done.5, ...), custom_call_target="tpu_custom_call" | custom-call | flops 8053063680 | bytes 25165824 | tf_op jit(solution)/shard_map/attention_backward/pallas_call | solution.py:309
  320.4 2.2 add_convert_fusion
  326.6 2.9 collective-permute-start.46
  329.5 6.9 %token_sums.7 = (bf16[512,2048]{1,0:T(8,128)(2,1)S(1)}, bf16[512,2048]{1,0:T(8,128)(2,1)S(1)}) custom-call(bf16[1280,1024]{1,0:T(8,128)(2,1)S(1)} %copy-done.36, bf16[1024,1024]{1,0:T(8,128)(2,1)S(1)} %copy-done.34, bf16[1280,512]{1,0:T(8,128)(2,1)S(1)} %get-tuple-element.335.refs_2_.k_ref, bf16[1280,512]{1,0:T(8,128)(2,1)S(1)} %get-tuple-element.336.refs_3_.v_ref), custom_call_target="tpu_custom_call" | custom-call | flops 5368709120 | bytes 12582912 | tf_op jit(solution)/shard_map/token_sums/pallas_call | solution.py:309
  337.7 4.2 collective-permute-done.47.halo_ref
  341.8 5.7 %collective-permute-start.48 = (bf16[512,2048]{1,0:T(8,128)(2,1)S(1)}, bf16[512,2048]{1,0:T(8,128)(2,1)S(1)}, u32[]{:S(2)}, u32[]{:S(2)}) collective-permute-start(bf16[512,2048]{1,0:T(8,128)(2,1)S(1)} %get-tuple-element.349), channel_id=1, source_target_pairs={{0,2},{1,5},{2,0},{3,7},{4,6},{5,1},{6,4},{7,3},{8,10},{9,13},{10,... | collective-permute-start | bytes 6291464 | tf_op jit(solution)/shard_map/ppermute | solution.py:77
  350.4 8.8 %input_backward.1 = (f32[512,1024]{1,0:T(8,128)S(1)}, f32[512,1024]{1,0:T(8,128)S(1)}) custom-call(s32[1]{0:T(128)} %bitcast.core_ref, bf16[1024,1024]{1,0:T(8,128)(2,1)S(1)} %copy-done.34, bf16[1280,512]{1,0:T(8,128)(2,1)S(1)} %get-tuple-element.335.refs_2_.k_ref, bf16[1280,512]{1,0:T(8,128)(2,1)S(1)} %get-tuple-element.336.refs_3_.v_ref, ...), custom_call_target="tpu_custom_call" | custom-call | flops 4294967296 | bytes 16777216 | tf_op jit(solution)/shard_map/input_backward/pallas_call | solution.py:309
  359.2 5.8 %collective-permute-done.49 = bf16[64,3072]{1,0:T(8,128)(2,1)S(1)} collective-permute-done((bf16[64,3072]{1,0:T(8,128)(2,1)S(1)}, bf16[64,3072]{1,0:T(8,128)(2,1)S(1)}, u32[]{:S(2)}, u32[]{:S(2)}) %collective-permute-start.49) | collective-permute-done | bytes 393248 | tf_op jit(solution)/shard_map/ppermute | solution.py:57
  365.0 6.6 %collective-permute-done.48 = bf16[512,2048]{1,0:T(8,128)(2,1)S(1)} collective-permute-done((bf16[512,2048]{1,0:T(8,128)(2,1)S(1)}, bf16[512,2048]{1,0:T(8,128)(2,1)S(1)}, u32[]{:S(2)}, u32[]{:S(2)}) %collective-permute-start.48) | collective-permute-done | bytes 2097184 | tf_op jit(solution)/shard_map/ppermute | solution.py:77
  376.7 13.4 %collective-permute-done.53 = bf16[64,1024]{1,0:T(8,128)(2,1)S(1)} collective-permute-done((bf16[64,1024]{1,0:T(8,128)(2,1)S(1)}, bf16[64,1024]{1,0:T(8,128)(2,1)S(1)}, u32[]{:S(2)}, u32[]{:S(2)}) %collective-permute-start.53) | collective-permute-done | bytes 131104 | tf_op jit(solution)/shard_map/ppermute | solution.py:57
  399.3 2.8 collective-permute-done.60
  403.6 14.6 %collective-permute-done.62.refs_6_ = bf16[64,1024]{1,0:T(8,128)(2,1)S(1)} collective-permute-done((bf16[64,1024]{1,0:T(8,128)(2,1)S(1)}, bf16[64,1024]{1,0:T(8,128)(2,1)S(1)}, u32[]{:S(2)}, u32[]{:S(2)}) %collective-permute-start.62) | collective-permute-done | bytes 131104 | tf_op jit(solution)/shard_map/ppermute | solution.py:57
  418.4 6.3 %collective-permute-start.65 = (f32[2,72]{1,0:T(2,128)S(1)}, f32[2,72]{1,0:T(2,128)S(1)}, u32[]{:S(2)}, u32[]{:S(2)}) collective-permute-start(f32[2,72]{1,0:T(2,128)S(1)} %pad_maximum_fusion.16), channel_id=1, source_target_pairs={{0,8},{1,9},{2,10},{3,11},{4,12},{5,13},{6,14},{7,15},{8,16},{9,17... | collective-permute-start | bytes 1736 | tf_op jit(solution)/shard_map/ppermute | solution.py:57
  427.2 2.3 fusion.96
  (350 shorter events, 104.8 us)
Async XLA Ops:
  6.3 12.1 %collective-permute-start.2 = (bf16[64,2176]{1,0:T(8,128)(2,1)S(1)}, bf16[64,2176]{1,0:T(8,128)(2,1)S(1)}, u32[]{:S(2)}, u32[]{:S(2)}) collective-permute-start(bf16[64,2176]{1,0:T(8,128)(2,1)S(1)} %maximum_select_fusion.1.refs_0_), channel_id=1, source_target_pairs={{0,24},{1,25},{2,26},{3,27},{4,28},{5,29},{6,30},{7,31},{8,0},{9,1... | collective-permute-start | bytes 835592 | tf_op jit(solution)/shard_map/ppermute | solution.py:57
  11.3 13.1 %collective-permute-start.1 = (bf16[64,2176]{1,0:T(8,128)(2,1)S(1)}, bf16[64,2176]{1,0:T(8,128)(2,1)S(1)}, u32[]{:S(2)}, u32[]{:S(2)}) collective-permute-start(bf16[64,2176]{1,0:T(8,128)(2,1)S(1)} %maximum_select_fusion.1.refs_0_), channel_id=1, source_target_pairs={{0,8},{1,9},{2,10},{3,11},{4,12},{5,13},{6,14},{7,15},{8,16},{9,17... | collective-permute-start | bytes 835592 | tf_op jit(solution)/shard_map/ppermute | solution.py:57
  25.7 14.0 %collective-permute-start.3 = (bf16[64,2176]{1,0:T(8,128)(2,1)S(1)}, bf16[64,2176]{1,0:T(8,128)(2,1)S(1)}, u32[]{:S(2)}, u32[]{:S(2)}) collective-permute-start(bf16[64,2176]{1,0:T(8,128)(2,1)S(1)} %collective-permute-done.1.refs_1_), channel_id=1, source_target_pairs={{0,8},{1,9},{2,10},{3,11},{4,12},{5,13},{6,14},{7,15},{8,16},{9,17... | collective-permute-start | bytes 835592 | tf_op jit(solution)/shard_map/ppermute | solution.py:57
  27.6 12.2 %collective-permute-start.6 = (bf16[256,1152]{1,0:T(8,128)(2,1)S(1)}, bf16[256,1152]{1,0:T(8,128)(2,1)S(1)}, u32[]{:S(2)}, u32[]{:S(2)}) collective-permute-start(bf16[256,1152]{1,0:T(8,128)(2,1)S(1)} %fusion.11), channel_id=1, source_target_pairs={{1,3},{3,5},{5,7},{7,9},{9,11},{11,13},{13,15},{15,17},{17,19},{19... | collective-permute-start | bytes 1769480 | tf_op jit(solution)/shard_map/ppermute | solution.py:67
  28.5 19.4 %collective-permute-start.7 = (bf16[64,4096]{1,0:T(8,128)(2,1)S(1)}, bf16[64,4096]{1,0:T(8,128)(2,1)S(1)}, u32[]{:S(2)}, u32[]{:S(2)}) collective-permute-start(bf16[64,4096]{1,0:T(8,128)(2,1)S(1)} %slice.270.refs_0_), channel_id=1, source_target_pairs={{0,8},{1,9},{2,10},{3,11},{4,12},{5,13},{6,14},{7,15},{8,16},{9,17... | collective-permute-start | bytes 1572872 | tf_op jit(solution)/shard_map/ppermute | solution.py:57
  28.6 11.1 %collective-permute-start.5 = (bf16[64,1536]{1,0:T(8,128)(2,1)S(1)}, bf16[64,1536]{1,0:T(8,128)(2,1)S(1)}, u32[]{:S(2)}, u32[]{:S(2)}) collective-permute-start(bf16[64,1536]{1,0:T(8,128)(2,1)S(1)} %get-tuple-element.465), channel_id=1, source_target_pairs={{0,4},{1,3},{2,6},{3,1},{4,0},{5,7},{6,2},{7,5},{8,12},{9,11},{10,... | collective-permute-start | bytes 589832 | tf_op jit(solution)/shard_map/ppermute | solution.py:77
  47.8 11.0 %collective-permute-start.11 = (bf16[512,1152]{1,0:T(8,128)(2,1)S(1)}, bf16[512,1152]{1,0:T(8,128)(2,1)S(1)}, u32[]{:S(2)}, u32[]{:S(2)}) collective-permute-start(bf16[512,1152]{1,0:T(8,128)(2,1)S(1)} %pad_maximum_fusion.1.mine_ref), channel_id=1, source_target_pairs={{0,1},{1,0},{2,3},{3,2},{4,5},{5,4},{6,7},{7,6},{8,9},{9,8},{10,11... | collective-permute-start | bytes 3538952 | tf_op jit(solution)/shard_map/ppermute | solution.py:70
  47.8 9.1 %collective-permute-start.10 = (bf16[2,64,1536]{2,1,0:T(8,128)(2,1)S(1)}, bf16[2,64,1536]{2,1,0:T(8,128)(2,1)S(1)}, u32[]{:S(2)}, u32[]{:S(2)}) collective-permute-start(bf16[2,64,1536]{2,1,0:T(8,128)(2,1)S(1)} %pad_maximum_fusion.9), channel_id=1, source_target_pairs={{0,2},{1,5},{2,0},{3,7},{4,6},{5,1},{6,4},{7,3},{8,10},{9,13},{10,... | collective-permute-start | bytes 1179656 | tf_op jit(solution)/shard_map/ppermute | solution.py:77
  49.3 8.6 %collective-permute-start.12 = (bf16[256,1152]{1,0:T(8,128)(2,1)S(1)}, bf16[256,1152]{1,0:T(8,128)(2,1)S(1)}, u32[]{:S(2)}, u32[]{:S(2)}) collective-permute-start(bf16[256,1152]{1,0:T(8,128)(2,1)S(1)} %collective-permute-done.6), channel_id=1, source_target_pairs={{0,1},{1,0},{2,3},{3,2},{4,5},{5,4},{6,7},{7,6},{8,9},{9,8},{10,11... | collective-permute-start | bytes 1769480 | tf_op jit(solution)/shard_map/ppermute | solution.py:70
  49.7 20.2 %collective-permute-start.8 = (bf16[256,2176]{1,0:T(8,128)(2,1)S(1)}, bf16[256,2176]{1,0:T(8,128)(2,1)S(1)}, u32[]{:S(2)}, u32[]{:S(2)}) collective-permute-start(bf16[256,2176]{1,0:T(8,128)(2,1)S(1)} %stack_cut.4.refs_0_), channel_id=1, source_target_pairs={{0,4},{1,3},{2,6},{3,1},{4,0},{5,7},{6,2},{7,5},{8,12},{9,11},{10,... | collective-permute-start | bytes 3342344 | tf_op jit(solution)/shard_map/ppermute | solution.py:77
  54.8 15.1 %collective-permute-start.9 = (bf16[64,4096]{1,0:T(8,128)(2,1)S(1)}, bf16[64,4096]{1,0:T(8,128)(2,1)S(1)}, u32[]{:S(2)}, u32[]{:S(2)}) collective-permute-start(bf16[64,4096]{1,0:T(8,128)(2,1)S(1)} %collective-permute-done.7.refs_1_), channel_id=1, source_target_pairs={{0,8},{1,9},{2,10},{3,11},{4,12},{5,13},{6,14},{7,15},{8,16},{9,17... | collective-permute-start | bytes 1572872 | tf_op jit(solution)/shard_map/ppermute | solution.py:57
  72.2 27.8 %collective-permute-start.13 = (bf16[512,2176]{1,0:T(8,128)(2,1)}, bf16[512,2176]{1,0:T(8,128)(2,1)}, u32[]{:S(2)}, u32[]{:S(2)}) collective-permute-start(bf16[512,2176]{1,0:T(8,128)(2,1)} %stack_cut.5.refs_0_), channel_id=1, source_target_pairs={{0,2},{1,5},{2,0},{3,7},{4,6},{5,1},{6,4},{7,3},{8,10},{9,13},{10,... | collective-permute-start | bytes 6684680 | tf_op jit(solution)/shard_map/ppermute | solution.py:77
  78.4 16.1 %collective-permute-start.14 = (bf16[64,4096]{1,0:T(8,128)(2,1)}, bf16[64,4096]{1,0:T(8,128)(2,1)S(1)}, u32[]{:S(2)}, u32[]{:S(2)}) collective-permute-start(bf16[64,4096]{1,0:T(8,128)(2,1)} %copy-done.22), channel_id=1, source_target_pairs={{0,8},{1,9},{2,10},{3,11},{4,12},{5,13},{6,14},{7,15},{8,16},{9,17... | collective-permute-start | bytes 1572872 | tf_op jit(solution)/shard_map/ppermute | solution.py:57
  100.1 27.3 %collective-permute-start.15 = (bf16[256,4096]{1,0:T(8,128)(2,1)S(1)}, bf16[256,4096]{1,0:T(8,128)(2,1)S(1)}, u32[]{:S(2)}, u32[]{:S(2)}) collective-permute-start(bf16[256,4096]{1,0:T(8,128)(2,1)S(1)} %stack_cut.6.refs_0_), channel_id=1, source_target_pairs={{0,4},{1,3},{2,6},{3,1},{4,0},{5,7},{6,2},{7,5},{8,12},{9,11},{10,... | collective-permute-start | bytes 6291464 | tf_op jit(solution)/shard_map/ppermute | solution.py:77
  101.3 26.1 %collective-permute-start.16 = (bf16[256,1536]{1,0:T(8,128)(2,1)S(1)}, bf16[256,1536]{1,0:T(8,128)(2,1)S(1)}, u32[]{:S(2)}, u32[]{:S(2)}) collective-permute-start(bf16[256,1536]{1,0:T(8,128)(2,1)S(1)} %bitcast.51), channel_id=1, source_target_pairs={{0,8},{1,9},{2,10},{3,11},{4,12},{5,13},{6,14},{7,15},{8,16},{9,17... | collective-permute-start | bytes 2359304 | tf_op jit(solution)/shard_map/ppermute | solution.py:57
  127.6 13.1 %collective-permute-start.18 = (bf16[512,1024]{1,0:T(8,128)(2,1)S(1)}, bf16[512,1024]{1,0:T(8,128)(2,1)S(1)}, u32[]{:S(2)}, u32[]{:S(2)}) collective-permute-start(bf16[512,1024]{1,0:T(8,128)(2,1)S(1)} %pad_maximum_fusion.2), channel_id=1, source_target_pairs={{0,1},{1,0},{2,3},{3,2},{4,5},{5,4},{6,7},{7,6},{8,9},{9,8},{10,11... | collective-permute-start | bytes 3145736 | tf_op jit(solution)/shard_map/ppermute | solution.py:70
  129.7 22.4 %collective-permute-start.17 = (bf16[512,1024]{1,0:T(8,128)(2,1)S(1)}, bf16[512,1024]{1,0:T(8,128)(2,1)S(1)}, u32[]{:S(2)}, u32[]{:S(2)}) collective-permute-start(bf16[512,1024]{1,0:T(8,128)(2,1)S(1)} %get-tuple-element.268.refs_0_), channel_id=1, source_target_pairs={{0,2},{1,5},{2,0},{3,7},{4,6},{5,1},{6,4},{7,3},{8,10},{9,13},{10,... | collective-permute-start | bytes 3145736 | tf_op jit(solution)/shard_map/ppermute | solution.py:77
  131.7 20.3 %collective-permute-start.19 = (bf16[256,1536]{1,0:T(8,128)(2,1)S(1)}, bf16[256,1536]{1,0:T(8,128)(2,1)S(1)}, u32[]{:S(2)}, u32[]{:S(2)}) collective-permute-start(bf16[256,1536]{1,0:T(8,128)(2,1)S(1)} %collective-permute-done.16.refs_1_), channel_id=1, source_target_pairs={{0,8},{1,9},{2,10},{3,11},{4,12},{5,13},{6,14},{7,15},{8,16},{9,17... | collective-permute-start | bytes 2359304 | tf_op jit(solution)/shard_map/ppermute | solution.py:57
  152.1 37.6 %collective-permute-start.26 = (bf16[512,3072]{1,0:T(8,128)(2,1)}, bf16[512,3072]{1,0:T(8,128)(2,1)}, u32[]{:S(2)}, u32[]{:S(2)}) collective-permute-start(bf16[512,3072]{1,0:T(8,128)(2,1)} %get-tuple-element.280.refs_0_.refs_2_), channel_id=1, source_target_pairs={{0,2},{1,5},{2,0},{3,7},{4,6},{5,1},{6,4},{7,3},{8,10},{9,13},{10,... | collective-permute-start | bytes 9437192 | tf_op jit(solution)/shard_map/ppermute | solution.py:77
  161.3 21.6 %collective-permute-start.27 = (bf16[256,1536]{1,0:T(8,128)(2,1)}, bf16[256,1536]{1,0:T(8,128)(2,1)S(1)}, u32[]{:S(2)}, u32[]{:S(2)}) collective-permute-start(bf16[256,1536]{1,0:T(8,128)(2,1)} %copy-done.31), channel_id=1, source_target_pairs={{0,8},{1,9},{2,10},{3,11},{4,12},{5,13},{6,14},{7,15},{8,16},{9,17... | collective-permute-start | bytes 2359304 | tf_op jit(solution)/shard_map/ppermute | solution.py:57
  204.6 20.5 %collective-permute-start.28 = (bf16[512,1536]{1,0:T(8,128)(2,1)S(1)}, bf16[512,1536]{1,0:T(8,128)(2,1)S(1)}, u32[]{:S(2)}, u32[]{:S(2)}) collective-permute-start(bf16[512,1536]{1,0:T(8,128)(2,1)S(1)} %get-tuple-element.302), channel_id=1, source_target_pairs={{0,2},{1,5},{2,0},{3,7},{4,6},{5,1},{6,4},{7,3},{8,10},{9,13},{10,... | collective-permute-start | bytes 4718600 | tf_op jit(solution)/shard_map/ppermute | solution.py:77
  230.5 19.8 %collective-permute-start.36 = (f32[128,1024]{1,0:T(8,128)}, f32[128,1024]{1,0:T(8,128)S(1)}, u32[]{:S(2)}, u32[]{:S(2)}) collective-permute-start(f32[128,1024]{1,0:T(8,128)} %get-tuple-element.424), channel_id=1, source_target_pairs={{0,1},{1,0},{2,3},{3,2},{4,5},{5,4},{6,7},{7,6},{8,9},{9,8},{10,11... | collective-permute-start | bytes 1572872 | tf_op jit(solution)/shard_map/ppermute | solution.py:70
  243.2 7.2 %collective-permute-start.39 = (f32[128,1024]{1,0:T(8,128)}, f32[128,1024]{1,0:T(8,128)S(1)}, u32[]{:S(2)}, u32[]{:S(2)}) collective-permute-start(f32[128,1024]{1,0:T(8,128)} %get-tuple-element.425), channel_id=1, source_target_pairs={{0,1},{1,0},{2,3},{3,2},{4,5},{5,4},{6,7},{7,6},{8,9},{9,8},{10,11... | collective-permute-start | bytes 1572872 | tf_op jit(solution)/shard_map/ppermute | solution.py:70
  244.0 7.1 %collective-permute-start.38 = (f32[128,1024]{1,0:T(8,128)}, f32[128,1024]{1,0:T(8,128)S(1)}, u32[]{:S(2)}, u32[]{:S(2)}) collective-permute-start(f32[128,1024]{1,0:T(8,128)} %get-tuple-element.426), channel_id=1, source_target_pairs={{0,1},{1,0},{2,3},{3,2},{4,5},{5,4},{6,7},{7,6},{8,9},{9,8},{10,11... | collective-permute-start | bytes 1572872 | tf_op jit(solution)/shard_map/ppermute | solution.py:70
  246.2 37.3 %collective-permute-start.35 = (bf16[512,3072]{1,0:T(8,128)(2,1)S(1)}, bf16[512,3072]{1,0:T(8,128)(2,1)S(1)}, u32[]{:S(2)}, u32[]{:S(2)}) collective-permute-start(bf16[512,3072]{1,0:T(8,128)(2,1)S(1)} %get-tuple-element.311), channel_id=1, source_target_pairs={{0,2},{1,5},{2,0},{3,7},{4,6},{5,1},{6,4},{7,3},{8,10},{9,13},{10,... | collective-permute-start | bytes 9437192 | tf_op jit(solution)/shard_map/ppermute | solution.py:77
  250.4 7.0 %collective-permute-start.33 = (bf16[256,1024]{1,0:T(8,128)(2,1)S(1)}, bf16[256,1024]{1,0:T(8,128)(2,1)S(1)}, u32[]{:S(2)}, u32[]{:S(2)}) collective-permute-start(bf16[256,1024]{1,0:T(8,128)(2,1)S(1)} %get-tuple-element.448), channel_id=1, source_target_pairs={{0,1},{1,0},{2,3},{3,2},{4,5},{5,4},{6,7},{7,6},{8,9},{9,8},{10,11... | collective-permute-start | bytes 1572872 | tf_op jit(solution)/shard_map/ppermute | solution.py:70
  251.0 15.6 %collective-permute-start.41 = (bf16[2,64,1536]{2,1,0:T(8,128)(2,1)S(1)}, bf16[2,64,1536]{2,1,0:T(8,128)(2,1)S(1)}, u32[]{:S(2)}, u32[]{:S(2)}) collective-permute-start(bf16[2,64,1536]{2,1,0:T(8,128)(2,1)S(1)} %get-tuple-element.440), channel_id=1, source_target_pairs={{0,8},{1,9},{2,10},{3,11},{4,12},{5,13},{6,14},{7,15},{8,16},{9,17... | collective-permute-start | bytes 1179656 | tf_op jit(solution)/shard_map/ppermute | solution.py:57
  251.1 19.6 %collective-permute-start.40 = (bf16[2,64,1536]{2,1,0:T(8,128)(2,1)S(1)}, bf16[2,64,1536]{2,1,0:T(8,128)(2,1)S(1)}, u32[]{:S(2)}, u32[]{:S(2)}) collective-permute-start(bf16[2,64,1536]{2,1,0:T(8,128)(2,1)S(1)} %get-tuple-element.441), channel_id=1, source_target_pairs={{0,24},{1,25},{2,26},{3,27},{4,28},{5,29},{6,30},{7,31},{8,0},{9,1... | collective-permute-start | bytes 1179656 | tf_op jit(solution)/shard_map/ppermute | solution.py:57
  285.6 34.7 %collective-permute-start.42 = (bf16[256,3072]{1,0:T(8,128)(2,1)}, bf16[256,3072]{1,0:T(8,128)(2,1)}, u32[]{:S(2)}, u32[]{:S(2)}) collective-permute-start(bf16[256,3072]{1,0:T(8,128)(2,1)} %add_convert_fusion.1), channel_id=1, source_target_pairs={{0,4},{1,3},{2,6},{3,1},{4,0},{5,7},{6,2},{7,5},{8,12},{9,11},{10,... | collective-permute-start | bytes 4718600 | tf_op jit(solution)/shard_map/ppermute | solution.py:77
  286.9 33.5 %collective-permute-start.43 = (bf16[512,1024]{1,0:T(8,128)(2,1)S(1)}, bf16[512,1024]{1,0:T(8,128)(2,1)}, u32[]{:S(2)}, u32[]{:S(2)}) collective-permute-start(bf16[512,1024]{1,0:T(8,128)(2,1)S(1)} %get-tuple-element.329), channel_id=1, source_target_pairs={{0,2},{1,5},{2,0},{3,7},{4,6},{5,1},{6,4},{7,3},{8,10},{9,13},{10,... | collective-permute-start | bytes 3145736 | tf_op jit(solution)/shard_map/ppermute | solution.py:77
  289.8 30.5 %collective-permute-start.44 = (bf16[2,64,1536]{2,1,0:T(8,128)(2,1)}, bf16[2,64,1536]{2,1,0:T(8,128)(2,1)S(1)}, u32[]{:S(2)}, u32[]{:S(2)}) collective-permute-start(bf16[2,64,1536]{2,1,0:T(8,128)(2,1)} %add_convert_fusion.9), channel_id=1, source_target_pairs={{0,24},{1,25},{2,26},{3,27},{4,28},{5,29},{6,30},{7,31},{8,0},{9,1... | collective-permute-start | bytes 1179656 | tf_op jit(solution)/shard_map/ppermute | solution.py:57
  324.2 13.5 %collective-permute-start.45 = (bf16[256,1024]{1,0:T(8,128)(2,1)S(1)}, bf16[256,1024]{1,0:T(8,128)(2,1)S(1)}, u32[]{:S(2)}, u32[]{:S(2)}) collective-permute-start(bf16[256,1024]{1,0:T(8,128)(2,1)S(1)} %add_convert_fusion.6), channel_id=1, source_target_pairs={{0,4},{1,3},{2,6},{3,1},{4,0},{5,7},{6,2},{7,5},{8,12},{9,11},{10,... | collective-permute-start | bytes 1572872 | tf_op jit(solution)/shard_map/ppermute | solution.py:77
  325.1 16.8 %collective-permute-start.47 = (bf16[256,1024]{1,0:T(8,128)(2,1)S(1)}, bf16[256,1024]{1,0:T(8,128)(2,1)S(1)}, u32[]{:S(2)}, u32[]{:S(2)}) collective-permute-start(bf16[256,1024]{1,0:T(8,128)(2,1)S(1)} %pad_maximum_fusion.8), channel_id=1, source_target_pairs={{2,0},{3,1},{4,2},{5,3},{6,4},{7,5},{8,6},{9,7},{10,8},{11,9},{12,... | collective-permute-start | bytes 1572872 | tf_op jit(solution)/shard_map/ppermute | solution.py:63
  326.6 11.1 %collective-permute-start.46 = (bf16[64,1536]{1,0:T(8,128)(2,1)S(1)}, bf16[64,1536]{1,0:T(8,128)(2,1)S(1)}, u32[]{:S(2)}, u32[]{:S(2)}) collective-permute-start(bf16[64,1536]{1,0:T(8,128)(2,1)S(1)} %get-tuple-element.470), channel_id=1, source_target_pairs={{0,4},{1,3},{2,6},{3,1},{4,0},{5,7},{6,2},{7,5},{8,12},{9,11},{10,... | collective-permute-start | bytes 589832 | tf_op jit(solution)/shard_map/ppermute | solution.py:77
  341.8 29.7 %collective-permute-start.48 = (bf16[512,2048]{1,0:T(8,128)(2,1)S(1)}, bf16[512,2048]{1,0:T(8,128)(2,1)S(1)}, u32[]{:S(2)}, u32[]{:S(2)}) collective-permute-start(bf16[512,2048]{1,0:T(8,128)(2,1)S(1)} %get-tuple-element.349), channel_id=1, source_target_pairs={{0,2},{1,5},{2,0},{3,7},{4,6},{5,1},{6,4},{7,3},{8,10},{9,13},{10,... | collective-permute-start | bytes 6291464 | tf_op jit(solution)/shard_map/ppermute | solution.py:77
  347.7 17.3 %collective-permute-start.49 = (bf16[64,3072]{1,0:T(8,128)(2,1)S(1)}, bf16[64,3072]{1,0:T(8,128)(2,1)S(1)}, u32[]{:S(2)}, u32[]{:S(2)}) collective-permute-start(bf16[64,3072]{1,0:T(8,128)(2,1)S(1)} %get-tuple-element.352), channel_id=1, source_target_pairs={{0,24},{1,25},{2,26},{3,27},{4,28},{5,29},{6,30},{7,31},{8,0},{9,1... | collective-permute-start | bytes 1179656 | tf_op jit(solution)/shard_map/ppermute | solution.py:57
  348.0 17.0 %collective-permute-start.50 = (bf16[64,3072]{1,0:T(8,128)(2,1)S(1)}, bf16[64,3072]{1,0:T(8,128)(2,1)S(1)}, u32[]{:S(2)}, u32[]{:S(2)}) collective-permute-start(bf16[64,3072]{1,0:T(8,128)(2,1)S(1)} %get-tuple-element.353), channel_id=1, source_target_pairs={{0,8},{1,9},{2,10},{3,11},{4,12},{5,13},{6,14},{7,15},{8,16},{9,17... | collective-permute-start | bytes 1179656 | tf_op jit(solution)/shard_map/ppermute | solution.py:57
  371.6 18.5 %collective-permute-start.55 = (f32[512,1024]{1,0:T(8,128)S(1)}, f32[512,1024]{1,0:T(8,128)S(1)}, u32[]{:S(2)}, u32[]{:S(2)}) collective-permute-start(f32[512,1024]{1,0:T(8,128)S(1)} %get-tuple-element.374), channel_id=1, source_target_pairs={{0,1},{1,0},{2,3},{3,2},{4,5},{5,4},{6,7},{7,6},{8,9},{9,8},{10,11... | collective-permute-start | bytes 6291464 | tf_op jit(solution)/shard_map/ppermute | solution.py:70
  372.0 18.1 %collective-permute-start.51 = (bf16[256,2048]{1,0:T(8,128)(2,1)S(1)}, bf16[256,2048]{1,0:T(8,128)(2,1)S(1)}, u32[]{:S(2)}, u32[]{:S(2)}) collective-permute-start(bf16[256,2048]{1,0:T(8,128)(2,1)S(1)} %add_convert_fusion.4), channel_id=1, source_target_pairs={{0,4},{1,3},{2,6},{3,1},{4,0},{5,7},{6,2},{7,5},{8,12},{9,11},{10,... | collective-permute-start | bytes 3145736 | tf_op jit(solution)/shard_map/ppermute | solution.py:77
  372.9 17.2 %collective-permute-start.52 = (bf16[64,3072]{1,0:T(8,128)(2,1)S(1)}, bf16[64,3072]{1,0:T(8,128)(2,1)S(1)}, u32[]{:S(2)}, u32[]{:S(2)}) collective-permute-start(bf16[64,3072]{1,0:T(8,128)(2,1)S(1)} %add_convert_fusion.7), channel_id=1, source_target_pairs={{0,24},{1,25},{2,26},{3,27},{4,28},{5,29},{6,30},{7,31},{8,0},{9,1... | collective-permute-start | bytes 1179656 | tf_op jit(solution)/shard_map/ppermute | solution.py:57
  374.5 15.5 %collective-permute-start.53 = (bf16[64,1024]{1,0:T(8,128)(2,1)S(1)}, bf16[64,1024]{1,0:T(8,128)(2,1)S(1)}, u32[]{:S(2)}, u32[]{:S(2)}) collective-permute-start(bf16[64,1024]{1,0:T(8,128)(2,1)S(1)} %get-tuple-element.371), channel_id=1, source_target_pairs={{0,24},{1,25},{2,26},{3,27},{4,28},{5,29},{6,30},{7,31},{8,0},{9,1... | collective-permute-start | bytes 393224 | tf_op jit(solution)/shard_map/ppermute | solution.py:57
  375.8 14.3 %collective-permute-start.54 = (bf16[64,1024]{1,0:T(8,128)(2,1)S(1)}, bf16[64,1024]{1,0:T(8,128)(2,1)S(1)}, u32[]{:S(2)}, u32[]{:S(2)}) collective-permute-start(bf16[64,1024]{1,0:T(8,128)(2,1)S(1)} %get-tuple-element.372), channel_id=1, source_target_pairs={{0,8},{1,9},{2,10},{3,11},{4,12},{5,13},{6,14},{7,15},{8,16},{9,17... | collective-permute-start | bytes 393224 | tf_op jit(solution)/shard_map/ppermute | solution.py:57
  393.9 24.3 %collective-permute-start.58 = (bf16[64,2048]{1,0:T(8,128)(2,1)S(1)}, bf16[64,2048]{1,0:T(8,128)(2,1)S(1)}, u32[]{:S(2)}, u32[]{:S(2)}) collective-permute-start(bf16[64,2048]{1,0:T(8,128)(2,1)S(1)} %get-tuple-element.444), channel_id=1, source_target_pairs={{0,8},{1,9},{2,10},{3,11},{4,12},{5,13},{6,14},{7,15},{8,16},{9,17... | collective-permute-start | bytes 786440 | tf_op jit(solution)/shard_map/ppermute | solution.py:57
  395.2 23.0 %collective-permute-start.57 = (bf16[64,2048]{1,0:T(8,128)(2,1)S(1)}, bf16[64,2048]{1,0:T(8,128)(2,1)S(1)}, u32[]{:S(2)}, u32[]{:S(2)}) collective-permute-start(bf16[64,2048]{1,0:T(8,128)(2,1)S(1)} %get-tuple-element.445), channel_id=1, source_target_pairs={{0,16},{1,17},{2,18},{3,19},{4,20},{5,21},{6,22},{7,23},{8,24},{9,... | collective-permute-start | bytes 786440 | tf_op jit(solution)/shard_map/ppermute | solution.py:57
  396.6 21.6 %collective-permute-start.56 = (bf16[64,2048]{1,0:T(8,128)(2,1)S(1)}, bf16[64,2048]{1,0:T(8,128)(2,1)S(1)}, u32[]{:S(2)}, u32[]{:S(2)}) collective-permute-start(bf16[64,2048]{1,0:T(8,128)(2,1)S(1)} %get-tuple-element.446), channel_id=1, source_target_pairs={{0,24},{1,25},{2,26},{3,27},{4,28},{5,29},{6,30},{7,31},{8,0},{9,1... | collective-permute-start | bytes 786440 | tf_op jit(solution)/shard_map/ppermute | solution.py:57
  398.3 19.9 %collective-permute-start.61 = (f32[32,4608]{1,0:T(8,128)S(1)}, f32[32,4608]{1,0:T(8,128)S(1)}, u32[]{:S(2)}, u32[]{:S(2)}) collective-permute-start(f32[32,4608]{1,0:T(8,128)S(1)} %get-tuple-element.389), channel_id=1, source_target_pairs={{0,1},{1,0},{2,3},{3,2},{4,5},{5,4},{6,7},{7,6},{8,9},{9,8},{10,11... | collective-permute-start | bytes 1769480 | tf_op jit(solution)/shard_map/ppermute | solution.py:70
  402.1 16.1 %collective-permute-start.62 = (bf16[64,1024]{1,0:T(8,128)(2,1)S(1)}, bf16[64,1024]{1,0:T(8,128)(2,1)S(1)}, u32[]{:S(2)}, u32[]{:S(2)}) collective-permute-start(bf16[64,1024]{1,0:T(8,128)(2,1)S(1)} %add_convert_fusion.10), channel_id=1, source_target_pairs={{0,24},{1,25},{2,26},{3,27},{4,28},{5,29},{6,30},{7,31},{8,0},{9,1... | collective-permute-start | bytes 393224 | tf_op jit(solution)/shard_map/ppermute | solution.py:57
  418.4 11.3 %collective-permute-start.65 = (f32[2,72]{1,0:T(2,128)S(1)}, f32[2,72]{1,0:T(2,128)S(1)}, u32[]{:S(2)}, u32[]{:S(2)}) collective-permute-start(f32[2,72]{1,0:T(2,128)S(1)} %pad_maximum_fusion.16), channel_id=1, source_target_pairs={{0,8},{1,9},{2,10},{3,11},{4,12},{5,13},{6,14},{7,15},{8,16},{9,17... | collective-permute-start | bytes 1736 | tf_op jit(solution)/shard_map/ppermute | solution.py:57
  (80 other events, 797.1 us)

commit v4 on v3

--- a/solution.py
+++ b/solution.py
@@ -404,38 +404,41 @@
 
 
 def gate_kernel(side, xm_ref, xo_ref, *refs):
-    gate_refs, up_refs = refs[:side], refs[side : 2 * side]
-    act_ref, to_gate_ref, to_up_ref = refs[2 * side :]
+    first_refs, gate_refs, up_refs = refs[:side], refs[side : 2 * side], refs[2 * side : 3 * side]
+    act_ref, to_gate_ref, to_up_ref = refs[3 * side :]
     half = xm_ref.shape[0]
-    for at, ref in enumerate((xm_ref, xo_ref)):
-        rows = slice(at * half, (at + 1) * half)
-        gate = contract(ref, gate_refs)
-        up = contract(ref, up_refs)
-        sigma = 1.0 / (1.0 + jnp.exp(-gate))
-        silu = gate * sigma
-        act_ref[rows, :] = (silu * up).astype(low)
-        to_gate_ref[rows, :] = (up * sigma * (1.0 + gate * (1.0 - sigma))).astype(low)
-        to_up_ref[rows, :] = silu.astype(low)
-
-
-def gate_forward(mine, other, parts):
+
+    def write(gate_refs):
+        for at, ref in enumerate((xm_ref, xo_ref)):
+            rows = slice(at * half, (at + 1) * half)
+            gate = contract(ref, gate_refs)
+            up = contract(ref, up_refs)
+            sigma = 1.0 / (1.0 + jnp.exp(-gate))
+            silu = gate * sigma
+            act_ref[rows, :] = (silu * up).astype(low)
+            to_gate_ref[rows, :] = (up * sigma * (1.0 + gate * (1.0 - sigma))).astype(low)
+            to_up_ref[rows, :] = silu.astype(low)
+
+    pl.when(pl.program_id(0) == 0)(lambda: write(first_refs))
+    pl.when(pl.program_id(0) == 1)(lambda: write(gate_refs))
+
+
+def gate_forward(mine, other, mix, gate, up):
     half, width = mine.shape
-    columns = parts[0].shape[1] // 2
-    tile = tile_of(columns)
+    size, tile = gate[0].shape
     wide = lambda j: (0, j)
-    after = lambda j: (0, j + columns // tile)
-    block = (parts[0].shape[0], tile)
-    return call(
-        functools.partial(gate_kernel, len(parts)),
+    fixed = lambda j: (0, 0)
+    return call(
+        functools.partial(gate_kernel, len(gate)),
         "gate_forward",
-        (columns // tile,),
+        (2,),
         [whole_block(mine), whole_block(other)]
-        + [(part, block, wide) for part in parts]
-        + [(part, block, after) for part in parts],
-        [((2 * half, columns), low, (2 * half, tile), wide)] * 3,
-        8 * half * width * columns,
+        + [(part, (size, tile), fixed) for part in mix + gate]
+        + [(part, (size, tile), wide) for part in up],
+        [((2 * half, 2 * tile), low, (2 * half, tile), wide)] * 3,
+        16 * half * width * tile,
         16 << 20,
-        transcendentals=2 * half * columns,
+        transcendentals=4 * half * tile,
     )
 
 
@@ -464,34 +467,38 @@
 
 
 def mlp_back_kernel(side, steps, gate_ref, up_ref, *refs):
-    parts, (other_ref, mine_ref) = refs[:side], refs[side:]
-    columns = gate_ref.shape[1]
+    firsts, gates, ups = (refs[at * side : (at + 1) * side] for at in range(3))
+    other_ref, mine_ref = refs[3 * side :]
+    cut = gate_ref.shape[1] // 2
     found = Parts(
         side,
-        lambda part: dot(gate_ref[...], parts[part][:, :columns], 1, 1)
-        + dot(up_ref[...], parts[part][:, columns:], 1, 1),
+        lambda part: dot(gate_ref[:, :cut], firsts[part][...], 1, 1)
+        + dot(gate_ref[:, cut:], gates[part][...], 1, 1)
+        + dot(up_ref[...], ups[part][...], 1, 1),
     )
     pl.when(pl.program_id(0) < steps)(lambda: write_parts(other_ref, found, swap=True))
     pl.when(pl.program_id(0) >= steps)(lambda: write_parts(mine_ref, found))
 
 
-def mlp_backward(gate_grad, up_grad, parts, tile=256):
+def mlp_backward(gate_grad, up_grad, mix, gate, up, tile=256):
     rows, columns = gate_grad.shape[0] // 2, gate_grad.shape[1]
-    width = len(parts) * parts[0].shape[0]
+    size = gate[0].shape[0]
+    width = len(gate) * size
     steps = rows // tile
     rows_of = lambda i: ((i + steps) % (2 * steps), 0)
     return call(
-        functools.partial(mlp_back_kernel, len(parts), steps),
+        functools.partial(mlp_back_kernel, len(gate), steps),
         "mlp_backward",
         (2 * steps,),
         [(grad, (tile, columns), rows_of) for grad in (gate_grad, up_grad)]
-        + [whole_block(part) for part in parts],
+        + [(part, (size, columns // 2), lambda i: (0, 0)) for part in mix]
+        + [whole_block(part) for part in gate + up],
         [
             ((rows, width), full, (tile, width), lambda i: (jnp.minimum(i, steps - 1), 0)),
             ((rows, width), full, (tile, width), lambda i: (jnp.maximum(i - steps, 0), 0)),
         ],
-        8 * rows * columns * width,
-        16 << 20,
+        1,
+        1,
     )
 
 
@@ -518,8 +525,8 @@
             ((rows, width), full, (tile, width), lambda i: (jnp.minimum(i, steps - 1), 0)),
             ((rows, width), full, (tile, width), lambda i: (jnp.maximum(i - steps, 0), 0)),
         ],
-        4 * rows * columns * width,
-        12 << 20,
+        1,
+        1,
     )
 
 
@@ -572,13 +579,13 @@
             ((own // 2, width), full, (tile, width), lambda i, core: (jnp.minimum(i, steps - 1), 0)),
             ((own // 2, width), full, (tile, width), lambda i, core: (jnp.maximum(i - steps, 0), 0)),
         ],
-        2 * own * width * (q_cols + 2 * k_cols),
-        16 << 20,
+        1,
+        1,
         scalars=(which,),
     )
 
 
-def finish_kernel(mine_ref, sent_ref, x_ref, hidden_ref, gain_ref, out_ref, sum_ref):
+def finish_kernel(core_ref, mine_ref, sent_ref, x_ref, hidden_ref, gain_ref, out_ref, sum_ref):
     grad = mine_ref[...] + sent_ref[...]
     x = x_ref[...].astype(full)
     scales = row_rms(x)
@@ -594,26 +601,30 @@
     out_ref[...] = (hidden_ref[...] + scales * (back - normed * mean)).astype(low)
 
 
-def finish_tokens(mine, sent, inputs, hidden_grad, gains, tile=128):
+def finish_tokens(which, mine, sent, inputs, hidden_grad, gains, tile=128):
     rows, width = mine.shape
-    rows_of = lambda i: (i, 0)
-    fixed = lambda i: (0, 0)
+    rows_of = lambda i, core: (i, 0)
+    fixed = lambda i, core: (0, 0)
+    before = (inputs.shape[0] - 2 * rows) // tile
+    later = lambda i, core: (before + core[0] * (rows // tile) + i, 0)
+    block = (tile, width)
     return call(
         finish_kernel,
         "finish_tokens",
         (rows // tile,),
-        [(array, (tile, width), rows_of) for array in (mine, sent, inputs, hidden_grad)]
-        + [whole_block(gains)],
-        [((rows, width), low, (tile, width), rows_of), ((8, width), full, (8, width), fixed)],
-        12 * rows * width,
-        18 * rows * width,
-    )
-
-
-def sums_kernel(side, tokens, segments, *refs):
-    outs, turned = refs[-1 - side : -1], refs[-1]
-    right_refs = refs[-1 - side - len(segments) : -1 - side]
-    left_refs = refs[: -1 - side - len(segments)]
+        [(mine, block, rows_of), (sent, block, rows_of), (inputs, block, later)]
+        + [(hidden_grad, block, rows_of), whole_block(gains)],
+        [((rows, width), low, block, rows_of), ((8, width), full, (8, width), fixed)],
+        1,
+        1,
+        scalars=(which,),
+    )
+
+
+def sums_kernel(side, groups, segments, *refs):
+    outs, turned = refs[-1 - side * groups : -1], refs[-1]
+    right_refs = refs[-1 - side * groups - len(segments) : -1 - side * groups]
+    left_refs = refs[: -1 - side * groups - len(segments)]
     step = pl.program_id(0)
     size = turned.shape[0] // side
 
@@ -624,50 +635,54 @@
             turned[:, start : start + ref.shape[0]] = ref[...].T
             start += ref.shape[0]
 
-    for ref, (first, steps, row) in zip(right_refs, segments):
+    for ref, (first, steps, row, group) in zip(right_refs, segments):
 
         @pl.when((step >= first) & (step < first + steps))
-        def _(ref=ref, row=row):
-            for part, out in enumerate(outs):
+        def _(ref=ref, row=row, group=group):
+            for part, out in enumerate(outs[group * side : (group + 1) * side]):
                 out[...] = dot(turned[part * size : (part + 1) * size, row:], ref[...]).astype(low)
 
 
-def token_sums(side, lefts, rights):
+def token_sums(side, lefts, *groups):
     width = lefts[0].shape[1]
     tokens = sum([left.shape[0] for left in lefts])
-    tile = min([tile_of(array.shape[1]) for array, _ in rights])
-    segments, step = [], 0
-    for array, row in rights:
-        steps = array.shape[1] // tile
-        segments.append((step, steps, row))
-        step += steps
+    tile = min([tile_of(array.shape[1]) for group in groups for array, _ in group])
+    segments, step, ins, outs = [], 0, [], []
 
     def clip(first, steps):
         return lambda j: (0, jnp.clip(j - first, 0, steps - 1))
 
-    ins = [whole_block(left) for left in lefts]
-    for (array, _), (first, steps, _) in zip(rights, segments):
-        ins.append((array, (array.shape[0], tile), clip(first, steps)))
+    for at, group in enumerate(groups):
+        begin = step
+        for array, row in group:
+            steps = array.shape[1] // tile
+            segments.append((step, steps, row, at))
+            ins.append((array, (array.shape[0], tile), clip(step, steps)))
+            step += steps
+        block = (width // side, tile)
+        shape = (width // side, (step - begin) * tile)
+        outs += [(shape, low, block, clip(begin, step - begin))] * side
     found = call(
-        functools.partial(sums_kernel, side, tokens, tuple(segments)),
+        functools.partial(sums_kernel, side, len(groups), tuple(segments)),
         "token_sums",
         (step,),
-        ins,
-        [((width // side, step * tile), low, (width // side, tile), lambda j: (0, j))] * side,
-        2 * tokens * width * step * tile,
-        12 << 20,
+        [whole_block(left) for left in lefts] + ins,
+        outs,
+        1,
+        1,
         scratch=[pltpu.VMEM((width, tokens), low)],
     )
-    return list(found)
+    return [list(found[at * side : (at + 1) * side]) for at in range(len(groups))]
 
 
 def mix_kernel(side, steps, core_ref, att_left, att_right, *refs):
     weights, (other_ref, mine_ref) = refs[:side], refs[side:]
     cut = att_left.shape[1]
+    start = weights[0].shape[1] - 2 * cut
     parts = Parts(
         side,
-        lambda part: dot(att_left[...], weights[part][:, :cut], 1, 1)
-        + dot(att_right[...], weights[part][:, cut:], 1, 1),
+        lambda part: dot(att_left[...], weights[part][:, start : start + cut], 1, 1)
+        + dot(att_right[...], weights[part][:, start + cut :], 1, 1),
     )
     pl.when(pl.program_id(0) < steps)(lambda: write_parts(other_ref, parts, swap=True))
     pl.when(pl.program_id(0) >= steps)(lambda: write_parts(mine_ref, parts))
@@ -692,20 +707,20 @@
             ((rows, width), full, (tile, width), lambda i, core: (jnp.minimum(i, steps - 1), 0)),
             ((rows, width), full, (tile, width), lambda i, core: (jnp.maximum(i - steps, 0), 0)),
         ],
-        8 * rows * columns * width,
-        12 << 20,
+        1,
+        1,
         scalars=(which,),
     )
 
 
 def mix_back_kernel(branch_ref, *refs):
     weights, out_ref = refs[:-1], refs[-1]
-    out_ref[...] = contract(branch_ref, weights).astype(low)
-
-
-def mix_backward(branch, weights, tile=256):
+    start = weights[0].shape[1] - out_ref.shape[1]
+    out_ref[...] = contract(branch_ref, weights, slice(start, None)).astype(low)
+
+
+def mix_backward(branch, weights, columns, tile=256):
     rows, width = branch.shape
-    columns = weights[0].shape[1]
     rows_of = lambda i: (i, 0)
     return call(
         mix_back_kernel,
@@ -713,8 +728,8 @@
         (rows // tile,),
         [(branch, (tile, width), rows_of)] + [whole_block(part) for part in weights],
         [((rows, columns), low, (tile, columns), rows_of)],
-        2 * rows * columns * width,
-        6 << 20,
+        1,
+        1,
     )[0]
 
 
@@ -936,6 +951,7 @@
     q_cols, k_cols, o_cols, ff_cols = (
         weight.shape[1] // 2 for weight in (q_weight, k_weight, o_weight, gate_weight)
     )
+    ff_cut = ff_cols // 2
     unit = 2 * weight_rows
     side = net.side
     which = net.core.astype(jnp.int32).reshape(1)
@@ -962,22 +978,25 @@
     block_qkv = chip_block(
         (q_weight, 0, q_cols), (extras, 0, None), (k_weight, 0, k_cols), (v_weight, 0, k_cols)
     )
-    z_qkv = [block_qkv, net.ring(block_qkv, 1), net.ring(block_qkv, -1)]
-    z_one, z_three, tokens, segments, o_weight, gate_weight, up_weight, down_weight = barrier(
-        (
-            z_qkv[1], z_qkv[2], tokens, segments, o_weight, gate_weight, up_weight, down_weight
-        )
-    )
-    z_qkv = [block_qkv, z_one, net.ring(z_one, 1), z_three]
-    block_rest = chip_block(
-        (down_weight, 0, ff_cols), (o_weight, 0, o_cols), (gate_weight, 0, ff_cols),
-        (up_weight, 0, ff_cols),
-    )
-    block_down, block_mlp = block_rest[:, :ff_cols], block_rest[:, ff_cols:]
-    z_mlp = [block_mlp, net.ring(block_mlp, 1)]
+    z_qkv = [block_qkv] + [net.ring(block_qkv, m) for m in range(1, 4)]
     numbers = jnp.broadcast_to(segments.astype(low)[:, None], (row_count, 128))
     own_tokens = jnp.concatenate([tokens, numbers], 1)
     before = net.last_core_along(own_tokens[row_count - halo :], 1)
+    z_qkv, own_tokens, before, o_weight, gate_weight, up_weight, down_weight = barrier(
+        (z_qkv, own_tokens, before, o_weight, gate_weight, up_weight, down_weight)
+    )
+
+    (qkv,) = stack_cut(z_qkv, ())
+    qkv = net.gather_plane(qkv, 0)
+    block_rest = chip_block(
+        (down_weight, 0, ff_cols), (gate_weight, 0, ff_cut), (o_weight, 0, o_cols),
+        (gate_weight, ff_cut, ff_cols), (up_weight, 0, ff_cols),
+    )
+    mix_end = ff_cols + ff_cut + o_cols
+    block_down, block_mix, block_mlp = (
+        block_rest[:, :ff_cols], block_rest[:, ff_cols:mix_end], block_rest[:, mix_end:]
+    )
+    z_mix = [block_mix, net.ring(block_mix, 1)]
     places = net.places(net.chip, unit)
     order = (jnp.arange(width, dtype=jnp.int32)[:, None] == places[None, :]).astype(low)
     head_places = net.places(net.chip, 2 * gain_rows)
@@ -991,22 +1010,21 @@
         & (gain_place[:, None] == jnp.arange(head_size, dtype=jnp.int32)[None, :])
     ).astype(low)
     plane_down = jnp.stack(net.gather_plane(block_down, 0))
-    z_qkv, plane_down, own_tokens, before, order, pick, z_mlp, cotangent = barrier(
-        (z_qkv, plane_down, own_tokens, before, order, pick, z_mlp, cotangent)
-    )
-
-    (qkv,) = stack_cut(z_qkv, ())
-    qkv = net.gather_plane(qkv, 0)
-    z_mlp.append(net.ring(z_mlp[-1], 1))
+    qkv, plane_down, own_tokens, before, order, pick, z_mix, block_mlp, cotangent = barrier(
+        (qkv, plane_down, own_tokens, before, order, pick, z_mix, block_mlp, cotangent)
+    )
+
+    (qkv,) = stack_cut(qkv, ())
+    qkv = net.gather_plane(qkv, 1)
+    z_mix.append(net.ring(z_mix[-1], 1))
+    z_mix.append(net.ring(z_mix[-1], 1))
+    z_mlp = [block_mlp]
+    for _ in range(3):
+        z_mlp.append(net.ring(z_mlp[-1], 1))
     plane_down = jnp.stack(net.gather_plane(plane_down, 1))
     plane_down = plane_down.reshape(side * side * unit, ff_cols)
     both = place(which, own_tokens, net.pair(own_tokens))
     before = jnp.where(net.core == 0, net.pair(before), before)
-    qkv, z_mlp, plane_down, both, before = barrier((qkv, z_mlp, plane_down, both, before))
-
-    (qkv,) = stack_cut(qkv, ())
-    qkv = net.gather_plane(qkv, 1)
-    z_mlp.append(net.ring(z_mlp[-1], 1))
     chip_tokens, before_tokens = both[:, :width], before[:, :width]
     chip_segments = both[:, width].astype(jnp.int32)
     before_segments = jnp.where(net.chip > 0, before[:, width].astype(jnp.int32), -1)
@@ -1026,11 +1044,13 @@
     query_segments = chip_segments[None, :]
     key_segments = window_segments[:, None]
     ordered = dot(window_tokens, order, kind=low)
-    qkv, z_mlp, plane_down, ordered, cosines, sines = barrier(
-        (qkv, z_mlp, plane_down, ordered, cosines, sines)
+    qkv, z_mix, z_mlp, plane_down, ordered, cosines, sines = barrier(
+        (qkv, z_mix, z_mlp, plane_down, ordered, cosines, sines)
     )
 
     own_cotangent = dot(cotangent, order, kind=low)
+    (mix,) = stack_cut(z_mix, ())
+    mix = net.gather_plane(mix, 0)
     (mlp,) = stack_cut(z_mlp, ())
     mlp = net.gather_plane(mlp, 0)
     z_down = [plane_down, net.ring(plane_down, 1)]
@@ -1047,35 +1067,38 @@
         )
 
     att_left = attend(0)
-    att_left, mlp, z_down, queries, keys, values, own_cotangent = barrier(
-        (att_left, mlp, z_down, queries, keys, values, own_cotangent)
+    att_left, mix, mlp, z_down, queries, keys, values, own_cotangent = barrier(
+        (att_left, mix, mlp, z_down, queries, keys, values, own_cotangent)
     )
 
     other_cotangent = net.pair(net.swapped(own_cotangent))
     cotangents = jnp.concatenate([own_cotangent, other_cotangent])
-    mix, mlp = stack_cut(mlp, (o_cols,))
+    (mix,) = stack_cut(mix, ())
     mix = net.gather_plane(mix, 1)
+    gate, up = stack_cut(mlp, (ff_cut,))
     att_right = attend(kv_heads // 2)
     z_down.append(net.ring(z_down[-1], 1))
-    att_left, att_right, mix, mlp, cotangents, z_down = barrier(
-        (att_left, att_right, mix, mlp, cotangents, z_down)
-    )
-
-    mlp = net.gather_plane(mlp, 1)
+    att_left, att_right, mix, gate, up, cotangents, z_down = barrier(
+        (att_left, att_right, mix, gate, up, cotangents, z_down)
+    )
+
+    gate = net.gather_plane(gate, 1)
+    branch_other, branch_mine = mix_forward(which, att_left, att_right, mix)
+    branch_sent = net.pair_in(branch_other, 4)
+    branch_mine, branch_sent, gate, up = barrier((branch_mine, branch_sent, gate, up))
+
+    up = net.gather_plane(up, 1)
     z_down.append(net.ring(z_down[-1], 1))
-    own_inputs = lax.dynamic_slice_in_dim(ordered, halo + net.core * row_count, row_count).astype(
-        full
-    )
-    branch_other, branch_mine = mix_forward(which, att_left, att_right, mix)
-    hidden_state = own_inputs + (branch_mine + net.pair_in(branch_other, 4))
+    own_inputs = lax.dynamic_slice_in_dim(ordered, halo + net.core * row_count, row_count)
+    hidden_state = own_inputs.astype(full) + (branch_mine + branch_sent)
     scale_two = inverse_rms(hidden_state)
     normed_two = hidden_state * scale_two
     mlp_own = (normed_two * gain_two).astype(low)
     mlp_other = net.pair_in(net.swapped(mlp_own), 2)
-    mlp_own, mlp_other, mlp, z_down = barrier((mlp_own, mlp_other, mlp, z_down))
-
-    activated, to_gate, to_up = gate_forward(mlp_own, mlp_other, mlp)
-    down_sums = token_sums(side, [cotangents], [(activated, 0)])
+    mlp_own, mlp_other, up, z_down = barrier((mlp_own, mlp_other, up, z_down))
+
+    activated, to_gate, to_up = gate_forward(mlp_own, mlp_other, mix, gate, up)
+    (down_sums,) = token_sums(side, [cotangents], [(activated, 0)])
     activated, to_gate, to_up, down_sums, z_down = barrier(
         (activated, to_gate, to_up, down_sums, z_down)
     )
@@ -1088,116 +1111,153 @@
         sent = [
             plus(*[term[at * size : (at + 1) * size] for term in terms]) for at in range(1, side)
         ]
-        return [term[:size] for term in terms], [None] + sent
+        return terms, [None] + sent
+
+    def kept(terms, received):
+        size = received[0].shape[0]
+        return plus(*[term[:size] for term in terms], *received)
 
     down_in = net.scatter_plane(down_sums, 1)
     gate_grad, up_grad = act_backward(cotangents, to_gate, to_up, z_down, unit)
-    mlp_sums = token_sums(side, [mlp_own, mlp_other], [(gate_grad, 0), (up_grad, 0)])
-    gate_grad, up_grad, mlp_sums, down_sum, activated = barrier(
-        (gate_grad, up_grad, mlp_sums, down_sums[:1] + down_in, activated)
-    )
-
-    mlp_in = net.scatter_plane(mlp_sums, 1)
+    gate_sums, up_sums = token_sums(
+        side, [mlp_own, mlp_other], [(gate_grad, 0)], [(up_grad, 0)]
+    )
+    gate_grad, up_grad, gate_sums, up_sums, down_sum, activated = barrier(
+        (gate_grad, up_grad, gate_sums, up_sums, down_sums[:1] + down_in, activated)
+    )
+
+    gate_in = net.scatter_plane(gate_sums, 1)
     z_down_sum = plus(*down_sum).reshape(side, 4, unit, ff_cols)
-    z_down_sum = net.scatter_z([z_down_sum[:, m] for m in range(4)])
-    mlp_grad_other, mlp_grad_mine = mlp_backward(gate_grad, up_grad, mlp)
-    mlp_in_grad = mlp_grad_mine + net.pair_in(mlp_grad_other, 4)
+    z_down_sum = [z_down_sum[:, m] for m in range(4)]
+    mlp_grad_other, mlp_grad_mine = mlp_backward(gate_grad, up_grad, mix, gate, up)
+    mlp_grad_sent = net.pair_in(mlp_grad_other, 4)
+    out_other, out_mine = down_forward(activated, z_down, side, unit)
+    mlp_grad_mine, mlp_grad_sent, gate_sum, up_sums, out_other, out_mine = barrier(
+        (mlp_grad_mine, mlp_grad_sent, gate_sums[:1] + gate_in, up_sums, out_other, out_mine)
+    )
+
+    up_in = net.scatter_plane(up_sums, 1)
+    out_sent = net.pair_in(out_other, 4)
+    mixed_out = (hidden_state + (out_mine + out_sent)).astype(low)
+    mixed_out = dot(mixed_out, order, 1, 1, low)
+    gate_sum, gate_sent = inner(gate_sum)
+    mlp_in_grad = mlp_grad_mine + mlp_grad_sent
     hidden_grad = own_cotangent.astype(full) + norm_back(
         mlp_in_grad * gain_two, normed_two, scale_two
     )
     branch_own = hidden_grad.astype(low)
     branch_low = place(which, branch_own, net.pair_in(net.swapped(branch_own), 2))
-    attended_grad = mix_backward(branch_low, mix)
-    mix_sums = token_sums(side, [branch_low], [(att_left, 0), (att_right, 0)])
-    out_other, out_mine = down_forward(activated, z_down, side, unit)
-    mixed_out = hidden_state + (out_mine + net.pair_in(out_other, 4))
-    mixed_out = dot(mixed_out.astype(low), order, 1, 1, low)
-    attended_grad, mix_sums, mlp_in_grad, mlp_sum, mixed_out, z_down_sum = barrier(
-        (attended_grad, mix_sums, mlp_in_grad, mlp_sums[:1] + mlp_in, mixed_out, z_down_sum)
-    )
-
-    mlp_sum, mlp_sent = inner(mlp_sum)
+    attended_grad = mix_backward(branch_low, mix, o_cols)
+    (mix_sums,) = token_sums(side, [branch_low], [(att_left, 0), (att_right, 0)])
+    (
+        attended_grad, mix_sums, mlp_in_grad, gate_sum, gate_sent, up_sum, z_down_sum, mixed_out
+    ) = barrier(
+        (
+            attended_grad, mix_sums, mlp_in_grad, gate_sum, gate_sent, up_sums[:1] + up_in,
+            z_down_sum, mixed_out,
+        )
+    )
+    z_down_sum = net.scatter_z(z_down_sum)
+
+    up_sum, up_sent = inner(up_sum)
+    mlp_sent = [None] + [
+        jnp.concatenate(both, 1) for both in zip(gate_sent[1:], up_sent[1:])
+    ]
     mlp_in = net.scatter_plane(mlp_sent, 0)
     mix_in = net.scatter_plane(mix_sums, 1)
-    z_down_sum = net.scatter_z_last(z_down_sum)
     query_low, key_low, value_low, gain_grads = attention_backward(
         queries, keys, values, attended_grad, query_proj, key_proj, cosines, sines, heads_gain,
         query_segments, key_segments, row_count, halo, head_size,
     )
     query_low, key_low, value_low, mlp_sum, mix_sum, z_down_sum = barrier(
-        (query_low, key_low, value_low, mlp_sum + mlp_in, mix_sums[:1] + mix_in, z_down_sum)
+        (
+            query_low, key_low, value_low, (gate_sum, up_sum, mlp_in), mix_sums[:1] + mix_in,
+            z_down_sum,
+        )
     )
 
     mix_sum, mix_sent = inner(mix_sum)
     mix_in = net.scatter_plane(mix_sent, 0)
-    z_mlp = jnp.split(plus(*mlp_sum), 4)
-    down_sum = plus(*z_down_sum)
-    down_in = net.scatter_plane([down_sum[m] for m in range(side)], 0)
+    z_down_sum = net.scatter_z_last(z_down_sum)
     later = net.chip_along(jnp.concatenate([key_low[:halo], value_low[:halo]], 1), -1)
-    qkv_sums = token_sums(side, [attn_in], [(query_low, halo), (key_low, 0), (value_low, 0)])
-    qkv_sums, query_low, mlp_in_grad, mix_sum, z_mlp, down_sum, later = barrier(
-        (
-            qkv_sums, query_low, mlp_in_grad, mix_sum + mix_in, z_mlp, [down_sum[0]] + down_in,
-            later,
-        )
+    (qkv_sums,) = token_sums(
+        side, [attn_in], [(query_low, halo), (key_low, 0), (value_low, 0)]
+    )
+    qkv_sums, query_low, mlp_in_grad, mix_sum, mlp_sum, z_down_sum, later = barrier(
+        (qkv_sums, query_low, mlp_in_grad, (mix_sum, mix_in), mlp_sum, z_down_sum, later)
     )
 
     qkv_in = net.scatter_plane(qkv_sums, 1)
-    z_mlp = net.scatter_z(z_mlp)
+    gate_sum, up_sum, mlp_in = mlp_sum
+    mlp_sum = jnp.concatenate(
+        [
+            kept(gate_sum, [part[:, :ff_cols] for part in mlp_in]),
+            kept(up_sum, [part[:, ff_cols:] for part in mlp_in]),
+        ],
+        1,
+    )
+    z_mlp = net.scatter_z(jnp.split(mlp_sum, 4))
     gain_two_grad = jnp.sum(mlp_in_grad * normed_two, axis=0, keepdims=True)
     head_gains = dot(gain_grads[:2], head_order)
-    z_mix = jnp.split(plus(*mix_sum), 4)
+    z_mix = net.scatter_z(jnp.split(kept(*mix_sum), 4))
+    z_mlp, z_mix, query_low, later = barrier((z_mlp, z_mix, query_low, later))
     grad_other, grad_mine = input_backward(which, query_low, key_low, value_low, later, qkv)
-    qkv_sum, z_mlp, grad_other, grad_mine, z_mix, gain_two_grad, head_gains = barrier(
+    qkv_sum, z_mlp, z_mix, gain_two_grad, head_gains, grad_other, grad_mine = barrier(
         (
-            qkv_sums[:1] + qkv_in, z_mlp, grad_other, grad_mine, z_mix, gain_two_grad, head_gains,
+            qkv_sums[:1] + qkv_in, z_mlp, z_mix, gain_two_grad, head_gains, grad_other, grad_mine,
         )
     )
 
     qkv_sum, qkv_sent = inner(qkv_sum)
     qkv_in = net.scatter_plane(qkv_sent, 0)
     z_mlp = net.scatter_z_last(z_mlp)
-    z_mix = net.scatter_z(z_mix)
-    grad_sent = net.pair(grad_other)
-    qkv_sum, z_mlp, z_mix, grad_mine, grad_sent = barrier(
-        (qkv_sum + qkv_in, z_mlp, z_mix, grad_mine, grad_sent)
-    )
-
-    z_qkv = jnp.split(plus(*qkv_sum), 4)
-    z_qkv = [z_qkv[0]] + [net.ring(z_qkv[m], -m) for m in range(1, 4)]
     z_mix = net.scatter_z_last(z_mix)
+    down_sum = plus(*z_down_sum)
+    down_in = net.scatter_plane([down_sum[m] for m in range(side)], 0)
+    grad_sent = net.pair_in(grad_other, 4)
     input_grad, gain_one_grad = finish_tokens(
-        grad_mine, grad_sent, own_inputs, hidden_grad, gain_rows_full
-    )
-    gains = jnp.concatenate([gain_one_grad[:1], gain_two_grad])
-
-    def gain_parts(gains, heads):
-        count = side if gains.shape[1] > width // (side * side) else 4
+        which, grad_mine, grad_sent, ordered, hidden_grad, gain_rows_full
+    )
+    qkv_sum, z_mlp, z_mix, input_grad, gain_one_grad, down_sum = barrier(
+        (
+            (qkv_sum, qkv_in), z_mlp, z_mix, input_grad, gain_one_grad, [down_sum[0]] + down_in,
+        )
+    )
+
+    z_qkv = net.scatter_z(jnp.split(kept(*qkv_sum), 4))
+    input_grad = dot(input_grad, order, 1, 1, low)
+
+    def blocks_of(count):
         return [
             jnp.concatenate(both, 1)
             for both in zip(jnp.split(gains, count, 1), jnp.split(heads, count, 1))
         ]
 
-    def gain_cut(array):
+    def cut_gains(array):
         at = array.shape[1] * width // (width + head_size)
         return array[:, :at], array[:, at:]
 
-    gains = gain_parts(gains, head_gains)
-    gains = plus(gains[0], *net.scatter_plane(gains, 1))
-    gains = gain_parts(*gain_cut(gains))
-    gains = plus(gains[0], *net.scatter_plane(gains, 0))
-    rest_mine, rest_other = fold(which, z_mlp, down_sum)
+    gains, heads = jnp.concatenate([gain_one_grad[:1], gain_two_grad]), head_gains
+    gain_blocks = blocks_of(side)
+    gain_blocks = [gain_blocks[0]] + net.scatter_plane(gain_blocks, 1)
+    gains, heads = cut_gains(plus(*gain_blocks))
+    gain_blocks = blocks_of(side)
+    gain_blocks = [gain_blocks[0]] + net.scatter_plane(gain_blocks, 0)
+    rest_mine, rest_other = fold(which, z_mlp, z_mix, down_sum)
     rest_other = net.pair(rest_other)
-    z_qkv, gains, rest_mine, rest_other, input_grad, z_mix = barrier(
-        (z_qkv, gains, rest_mine, rest_other, input_grad, z_mix)
-    )
-
-    input_grad = dot(input_grad, order, 1, 1, low)
-    z_mine, z_other = fold(which, z_qkv, z_mix)
+    z_qkv, gain_blocks, input_grad, rest_mine, rest_other = barrier(
+        (z_qkv, gain_blocks, input_grad, rest_mine, rest_other)
+    )
+
+    z_qkv = net.scatter_z_last(z_qkv)
+    gains, heads = cut_gains(plus(*gain_blocks))
+    gain_blocks = blocks_of(4)
+    gain_blocks = [gain_blocks[0]] + [net.ring(gain_blocks[m], -m) for m in range(1, 4)]
+    z_qkv, gain_blocks = barrier((z_qkv, gain_blocks))
+
+    z_mine, z_other = fold(which, z_qkv)
     z_other = net.pair(z_other)
-    gains = gain_parts(*gain_cut(gains))
-    gains = sum([net.ring(gains[m], -m) for m in range(1, 4)], gains[0])
-    gains, heads = gain_cut(gains)
+    gains, heads = cut_gains(plus(*gain_blocks))
     gains = jnp.concatenate(
         [gains[:1, :weight_rows], gains[1:, :weight_rows], heads[:1, :gain_rows],
          heads[1:, :gain_rows], gains[:1, weight_rows:], gains[1:, weight_rows:],
@@ -1207,16 +1267,14 @@
     gain_other = jnp.where(net.core == 0, gains[1], gains[0])
     gain_sum = gain_mine + net.pair(gain_other)
     ends = [0]
-    for size in (ff_cols, ff_cols, ff_cols):
+    for size in (ff_cols, ff_cols, o_cols, ff_cols):
         ends.append(ends[-1] + size)
-    gate_out, up_out, down_out = join(
+    gate_out, up_out, o_out, down_out = join(
         which, rest_mine, rest_other, *[((start, end),) for start, end in zip(ends[:-1], ends[1:])]
     )
     v_at = q_cols + k_cols
-    o_at = v_at + k_cols
-    q_out, k_out, v_out, o_out = join(
-        which, z_mine, z_other, ((0, q_cols),), ((q_cols, v_at),), ((v_at, o_at),),
-        ((o_at, o_at + o_cols),),
+    q_out, k_out, v_out = join(
+        which, z_mine, z_other, ((0, q_cols),), ((q_cols, v_at),), ((v_at, v_at + k_cols),)
     )
     return (
         mixed_out,

time: 442 us -> 428 us (0.968)
  waiting for transfers between devices: 158 us -> 122 us
  starting transfers between devices: 77.3 us -> 87.2 us
  other arithmetic: 26.2 us -> 32.5 us
  local copies, waits for them, and re-layouts: 23.1 us -> 29.4 us
    ppermute x24 -> x27, waiting for transfers between devices: 96.6 us -> 75.2 us  [ring(): lax.ppermute(array, 'dp', [(i, (i + step) % self.count) for i in range(se...]
    ppermute x24 -> x27, starting transfers between devices: 35.7 us -> 52 us  [ring(): lax.ppermute(array, 'dp', [(i, (i + step) % self.count) for i in range(se...]
    ppermute x17 -> x20, starting transfers between devices: 33.7 us -> 23.7 us  [plane(): return lax.ppermute(array, 'dp', pairs)]
    unnamed x116 -> x168, local copies, waits for them, and re-layouts: 8.72 us -> 17.9 us
    ppermute x17 -> x20, waiting for transfers between devices: 48.3 us -> 39.6 us  [plane(): return lax.ppermute(array, 'dp', pairs)]
    ppermute x25 -> x28, waiting for transfers between devices: 9.06 us -> 6.9 us  [pair(): return lax.ppermute(array, 'dp', [(i, i ^ 1) for i in range(self.count)])]
    pallas_call x26 -> x28, Pallas kernels: 135 us -> 134 us  [call(): pl.pallas_call(kernel, grid_spec=pltpu.PrefetchScalarGridSpec(num_scalar_...]
  transfers between devices with their start and end apart: 68 -> 77, of which waited for: 30 -> 31; matrix products, arithmetic and copies ran while one was open for 9% -> 11% of each run, Pallas kernels for 26% -> 28%
where the time goes in v4:
time: 428 us; the launch traced here: 419 us
  Pallas kernels  134 us (31%)
  waiting for transfers between devices  122 us (29%)
  starting transfers between devices  87.2 us (20%)
  other arithmetic  32.5 us (8%)
  local copies, waits for them, and re-layouts  29.4 us (7%)
  matrix products  11.4 us (3%)
    pallas_call x28, Pallas kernels, call(): pl.pallas_call(kernel, grid_spec=pltpu.PrefetchScalarGridSpec(num_scalar_...  134 us
    ppermute x27, waiting for transfers between devices, ring(): lax.ppermute(array, 'dp', [(i, (i + step) % self.count) for i in range(se...  75.2 us
    ppermute x27, starting transfers between devices, ring(): lax.ppermute(array, 'dp', [(i, (i + step) % self.count) for i in range(se...  52 us
    ppermute x20, waiting for transfers between devices, plane(): return lax.ppermute(array, 'dp', pairs)  39.6 us
    ppermute x20, starting transfers between devices, plane(): return lax.ppermute(array, 'dp', pairs)  23.7 us
    unnamed x168, local copies, waits for them, and re-layouts  17.9 us
    dot_general x5, matrix products, dot(): lax.dot_general(left_side, right_side, (((left_dim,), (right_dim,)), ((),...  11.4 us
  transfers between devices with their start and end apart: 77, of which 31 were waited for; matrix products, arithmetic and copies ran while one was open for 11% of the time, Pallas kernels for 28%

profile of v4, /device:TPU:0, one launch (start us, length us, event | category | flops | bytes accessed | tf_op | source)
XLA Modules:
  0.0 419.4 jit_solution(14193618933771009436)
XLA Ops:
  9.5 4.7 %collective-permute-start.3 = (bf16[64,2176]{1,0:T(8,128)(2,1)S(1)}, bf16[64,2176]{1,0:T(8,128)(2,1)S(1)}, u32[]{:S(2)}, u32[]{:S(2)}) collective-permute-start(bf16[64,2176]{1,0:T(8,128)(2,1)S(1)} %maximum_select_fusion.1.refs_0_), channel_id=1, source_target_pairs={{0,24},{1,25},{2,26},{3,27},{4,28},{5,29},{6,30},{7,31},{8,0},{9,1... | collective-permute-start | bytes 835592 | tf_op jit(solution)/shard_map/ppermute | solution.py:57
  16.4 3.7 collective-permute-done.3.refs_3_
  20.1 17.7 %collective-permute-done.2.refs_2_ = bf16[64,2176]{1,0:T(8,128)(2,1)S(1)} collective-permute-done((bf16[64,2176]{1,0:T(8,128)(2,1)S(1)}, bf16[64,2176]{1,0:T(8,128)(2,1)S(1)}, u32[]{:S(2)}, u32[]{:S(2)}) %collective-permute-start.2) | collective-permute-done | bytes 278560 | tf_op jit(solution)/shard_map/ppermute | solution.py:57
  39.1 2.2 fusion
  47.4 11.7 %collective-permute-done.7 = bf16[64,1536]{1,0:T(8,128)(2,1)S(1)} collective-permute-done((bf16[64,1536]{1,0:T(8,128)(2,1)S(1)}, bf16[64,1536]{1,0:T(8,128)(2,1)S(1)}, u32[]{:S(2)}, u32[]{:S(2)}) %collective-permute-start.7) | collective-permute-done | bytes 196640 | tf_op jit(solution)/shard_map/ppermute | solution.py:77
  62.4 5.7 %collective-permute-start.15 = (bf16[2,64,1536]{2,1,0:T(8,128)(2,1)}, bf16[2,64,1536]{2,1,0:T(8,128)(2,1)}, u32[]{:S(2)}, u32[]{:S(2)}) collective-permute-start(bf16[2,64,1536]{2,1,0:T(8,128)(2,1)} %pad_maximum_fusion.14), channel_id=1, source_target_pairs={{0,2},{1,5},{2,0},{3,7},{4,6},{5,1},{6,4},{7,3},{8,10},{9,13},{10,... | collective-permute-start | bytes 1179656 | tf_op jit(solution)/shard_map/ppermute | solution.py:77
  68.6 2.2 collective-permute-start.10
  73.6 5.6 %collective-permute-done.10.refs_2_ = bf16[64,1792]{1,0:T(8,128)(2,1)} collective-permute-done((bf16[64,1792]{1,0:T(8,128)(2,1)}, bf16[64,1792]{1,0:T(8,128)(2,1)}, u32[]{:S(2)}, u32[]{:S(2)}) %collective-permute-start.10) | collective-permute-done | bytes 229408 | tf_op jit(solution)/shard_map/ppermute | solution.py:57
  79.8 2.6 collective-permute-start.11
  93.2 5.3 %fusion.1.x_ref = bf16[1280,1024]{1,0:T(8,128)(2,1)S(1)} fusion(bf16[1024,1024]{1,0:T(8,128)(2,1)} %fusion, bf16[1024,1024]{1,0:T(8,128)(2,1)} %slice.301, bf16[256,1024]{1,0:T(8,128)(2,1)} %slice.300), kind=kOutput, calls=%fused_computation.3 | convolution fusion | flops 2689597440 | bytes 7340032 | tf_op jit(solution)/shard_map/dot_general | solution.py:19
  98.6 2.4 fusion.9
  101.0 5.8 %collective-permute-done.9.refs_1_ = bf16[512,2176]{1,0:T(8,128)(2,1)} collective-permute-done((bf16[512,2176]{1,0:T(8,128)(2,1)S(1)}, bf16[512,2176]{1,0:T(8,128)(2,1)}, u32[]{:S(2)}, u32[]{:S(2)}) %collective-permute-start.9) | collective-permute-done | bytes 2228256 | tf_op jit(solution)/shard_map/ppermute | solution.py:77
  115.3 10.6 %project.1 = (bf16[1280,1024]{1,0:T(8,128)(2,1)S(1)}, bf16[1024,1024]{1,0:T(8,128)(2,1)S(1)}, bf16[1280,512]{1,0:T(8,128)(2,1)S(1)}, bf16[1280,512]{1,0:T(8,128)...) custom-call(bf16[1280,1024]{1,0:T(8,128)(2,1)S(1)} %fusion.1.x_ref, ...), custom_call_target="tpu_custom_call" | custom-call | flops 5368709120 | bytes 20971520 | tf_op jit(solution)/shard_map/project/pallas_call | solution.py:309
  128.7 8.6 %attention_forward.2.att_left.refs_1_ = bf16[1024,512]{1,0:T(8,128)(2,1)S(1)} custom-call(bf16[1024,1024]{1,0:T(8,128)(2,1)S(1)} %get-tuple-element.295.q_ref.refs_0_, bf16[1280,512]{1,0:T(8,128)(2,1)S(1)} %get-tuple-element.296.k_ref.refs_1_, bf16[1280,512]{1,0:T(8,128)(2,1)S(1)} %get-tuple-element.297.v_ref.refs_2_, s32[1,1024]{1,0:T(1,128)S(1)} %bitcast.54, ...), custom_call_target="tpu_custom_call" | custom-call | flops 1610612736 | bytes 4194304 | tf_op jit(solution)/shard_map/attention_forward/pallas_call | solution.py:309
  137.5 2.4 collective-permute-start.21
  140.2 2.2 collective-permute-start.23
  143.4 8.7 %attention_forward.3.att_right.refs_2_ = bf16[1024,512]{1,0:T(8,128)(2,1)S(1)} custom-call(bf16[1024,1024]{1,0:T(8,128)(2,1)S(1)} %get-tuple-element.295.q_ref.refs_0_, bf16[1280,512]{1,0:T(8,128)(2,1)S(1)} %get-tuple-element.296.k_ref.refs_1_, bf16[1280,512]{1,0:T(8,128)(2,1)S(1)} %get-tuple-element.297.v_ref.refs_2_, s32[1,1024]{1,0:T(1,128)S(1)} %bitcast.55, ...), custom_call_target="tpu_custom_call" | custom-call | flops 1610612736 | bytes 4194304 | tf_op jit(solution)/shard_map/attention_forward/pallas_call | solution.py:309
  153.7 8.1 %collective-permute-done.23.refs_2_ = bf16[256,1536]{1,0:T(8,128)(2,1)S(1)} collective-permute-done((bf16[256,1536]{1,0:T(8,128)(2,1)S(1)}, bf16[256,1536]{1,0:T(8,128)(2,1)S(1)}, u32[]{:S(2)}, u32[]{:S(2)}) %collective-permute-start.23) | collective-permute-done | bytes 786464 | tf_op jit(solution)/shard_map/ppermute | solution.py:57
  163.1 3.0 mix_forward.1
  170.3 2.5 collective-permute-start.32
  180.9 11.3 %collective-permute-done.32.refs_3_ = bf16[256,1536]{1,0:T(8,128)(2,1)S(1)} collective-permute-done((bf16[256,1536]{1,0:T(8,128)(2,1)}, bf16[256,1536]{1,0:T(8,128)(2,1)S(1)}, u32[]{:S(2)}, u32[]{:S(2)}) %collective-permute-start.32) | collective-permute-done | bytes 786464 | tf_op jit(solution)/shard_map/ppermute | solution.py:57
  192.3 4.6 %collective-permute-done.31.refs_5_ = bf16[512,1536]{1,0:T(8,128)(2,1)S(1)} collective-permute-done((bf16[512,1536]{1,0:T(8,128)(2,1)S(1)}, bf16[512,1536]{1,0:T(8,128)(2,1)S(1)}, u32[]{:S(2)}, u32[]{:S(2)}) %collective-permute-start.31) | collective-permute-done | bytes 1572896 | tf_op jit(solution)/shard_map/ppermute | solution.py:77
  196.9 9.8 %gate_forward.1 = (bf16[1024,1536]{1,0:T(8,128)(2,1)S(1)}, bf16[1024,1536]{1,0:T(8,128)(2,1)S(1)}, bf16[1024,1536]{1,0:T(8,128)(2,1)S(1)}) custom-call(bf16[512,1024]{1,0:T(8,128)(2,1)S(1)} %multiply_convert_fusion.xm_ref.refs_0_, bf16[512,1024]{1,0:T(8,128)(2,1)S(1)} %pad_maximum_fusion.8.xo_ref.refs_1_, bf16[512,1792]{1,0:T(8,128)(2,1)S(1)} %stack_cut.10.refs_0_, ...), custom_call_target="tpu_custom_call" | custom-call | flops 6442450944 | bytes 16777216 | tf_op jit(solution)/shard_map/gate_forward/pallas_call | solution.py:309
  206.7 4.7 %token_sums.4 = (bf16[512,1536]{1,0:T(8,128)(2,1)S(1)}, bf16[512,1536]{1,0:T(8,128)(2,1)S(1)}) custom-call(bf16[1024,1024]{1,0:T(8,128)(2,1)S(1)} %copy-done.9, bf16[1024,1536]{1,0:T(8,128)(2,1)S(1)} %get-tuple-element.360.refs_1_.act_ref), custom_call_target="tpu_custom_call" | custom-call | flops 1 | bytes 1 | tf_op jit(solution)/shard_map/token_sums/pallas_call | solution.py:309
  213.5 5.1 %act_backward.1 = (bf16[1024,1536]{1,0:T(8,128)(2,1)S(1)}, bf16[1024,1536]{1,0:T(8,128)(2,1)S(1)}) custom-call(bf16[1024,1024]{1,0:T(8,128)(2,1)S(1)} %copy-done.9, bf16[1024,1536]{1,0:T(8,128)(2,1)S(1)} %get-tuple-element.337.to_gate_ref, bf16[1024,1536]{1,0:T(8,128)(2,1)S(1)} %get-tuple-element.338.to_up_ref, bf16[256,1536]{1,0:T(8,128)(2,1)S(1)} %bitcast.52, ...), custom_call_target="tpu_custom_call" | custom-call | flops 3221225472 | bytes 16777216 | tf_op jit(solution)/shard_map/act_backward/pallas_call | solution.py:309
  218.6 9.1 %token_sums.5 = (bf16[512,1536]{1,0:T(8,128)(2,1)S(1)}, bf16[512,1536]{1,0:T(8,128)(2,1)S(1)}, bf16[512,1536]{1,0:T(8,128)(2,1)S(1)}, bf16[512,1536]{1,0:T(8,128)(2,1)S(1)}) custom-call(bf16[512,1024]{1,0:T(8,128)(2,1)S(1)} %multiply_convert_fusion.xm_ref.refs_0_, bf16[512,1024]{1,0:T(8,128)(2,1)S(1)} %pad_maximum_fusion.8.xo_ref.refs_1_, ...), custom_call_target="tpu_custom_call" | custom-call | flops 1 | bytes 1 | tf_op jit(solution)/shard_map/token_sums/pallas_call | solution.py:309
  228.9 4.2 %collective-permute-done.33 = bf16[512,1536]{1,0:T(8,128)(2,1)S(1)} collective-permute-done((bf16[512,1536]{1,0:T(8,128)(2,1)S(1)}, bf16[512,1536]{1,0:T(8,128)(2,1)S(1)}, u32[]{:S(2)}, u32[]{:S(2)}) %collective-permute-start.33) | collective-permute-done | bytes 1572896 | tf_op jit(solution)/shard_map/ppermute | solution.py:77
  235.0 4.1 down_forward.1
  239.1 8.9 %mlp_backward.1 = (f32[512,1024]{1,0:T(8,128)S(1)}, f32[512,1024]{1,0:T(8,128)S(1)}) custom-call(bf16[1024,1536]{1,0:T(8,128)(2,1)S(1)} %get-tuple-element.352.refs_2_.gate_ref, bf16[1024,1536]{1,0:T(8,128)(2,1)S(1)} %get-tuple-element.353.refs_3_.up_ref, bf16[512,1792]{1,0:T(8,128)(2,1)S(1)} %stack_cut.10.refs_0_, bf16[512,1792]{1,0:T(8,128)(2,1)S(1)} %copy-done.3, ...), custom_call_target="tpu_custom_call" | custom-call | flops 1 | bytes 1 | tf_op jit(solution)/shard_map/mlp_backward/pallas_call | solution.py:309
  264.9 2.9 mix_backward.1.refs_3_
  269.2 3.6 token_sums.6
  272.8 2.4 fusion.7
  282.9 30.2 %attention_backward.1 = (bf16[1024,1024]{1,0:T(8,128)(2,1)}, bf16[1280,512]{1,0:T(8,128)(2,1)S(1)}, bf16[1280,512]{1,0:T(8,128)(2,1)S(1)}, f32[8,128]{1,0:T(8,128)S(1)}) custom-call(bf16[1024,1024]{1,0:T(8,128)(2,1)} %copy-done.10, bf16[1280,512]{1,0:T(8,128)(2,1)S(1)} %copy-done.14, bf16[1280,512]{1,0:T(8,128)(2,1)} %copy-done.15, ...), custom_call_target="tpu_custom_call" | custom-call | flops 8053063680 | bytes 25165824 | tf_op jit(solution)/shard_map/attention_backward/pallas_call | solution.py:309
  317.9 5.2 %collective-permute-start.51 = (bf16[2,64,1536]{2,1,0:T(8,128)(2,1)S(1)}, bf16[2,64,1536]{2,1,0:T(8,128)(2,1)S(1)}, u32[]{:S(2)}, u32[]{:S(2)}) collective-permute-start(bf16[2,64,1536]{2,1,0:T(8,128)(2,1)S(1)} %add_convert_fusion.11), channel_id=1, source_target_pairs={{0,24},{1,25},{2,26},{3,27},{4,28},{5,29},{6,30},{7,31},{8,0},{9,1... | collective-permute-start | bytes 1179656 | tf_op jit(solution)/shard_map/ppermute | solution.py:57
  323.4 7.2 %token_sums.7 = (bf16[512,2048]{1,0:T(8,128)(2,1)S(1)}, bf16[512,2048]{1,0:T(8,128)(2,1)S(1)}) custom-call(bf16[1280,1024]{1,0:T(8,128)(2,1)S(1)} %copy-done.23, bf16[1024,1024]{1,0:T(8,128)(2,1)S(1)} %copy-done.8, bf16[1280,512]{1,0:T(8,128)(2,1)S(1)} %get-tuple-element.396.refs_2_.k_ref, bf16[1280,512]{1,0:T(8,128)(2,1)S(1)} %get-tuple-element.397.refs_3_.v_ref), custom_call_target="tpu_custom_call" | custom-call | flops 1 | bytes 1 | tf_op jit(solution)/shard_map/token_sums/pallas_call | solution.py:309
  330.6 7.7 %collective-permute-done.51 = bf16[2,64,1536]{2,1,0:T(8,128)(2,1)S(1)} collective-permute-done((bf16[2,64,1536]{2,1,0:T(8,128)(2,1)S(1)}, bf16[2,64,1536]{2,1,0:T(8,128)(2,1)S(1)}, u32[]{:S(2)}, u32[]{:S(2)}) %collective-permute-start.51) | collective-permute-done | bytes 393248 | tf_op jit(solution)/shard_map/ppermute | solution.py:57
  345.1 3.7 collective-permute-start.56
  349.1 11.8 %collective-permute-done.57.refs_4_ = bf16[64,1024]{1,0:T(8,128)(2,1)S(1)} collective-permute-done((bf16[64,1024]{1,0:T(8,128)(2,1)S(1)}, bf16[64,1024]{1,0:T(8,128)(2,1)S(1)}, u32[]{:S(2)}, u32[]{:S(2)}) %collective-permute-start.57) | collective-permute-done | bytes 131104 | tf_op jit(solution)/shard_map/ppermute | solution.py:57
  361.2 7.8 %input_backward.1 = (f32[512,1024]{1,0:T(8,128)S(1)}, f32[512,1024]{1,0:T(8,128)S(1)}) custom-call(s32[1]{0:T(128)} %bitcast.core_ref, bf16[1024,1024]{1,0:T(8,128)(2,1)S(1)} %copy-done.8, bf16[1280,512]{1,0:T(8,128)(2,1)S(1)} %get-tuple-element.396.refs_2_.k_ref, bf16[1280,512]{1,0:T(8,128)(2,1)S(1)} %get-tuple-element.397.refs_3_.v_ref, ...), custom_call_target="tpu_custom_call" | custom-call | flops 1 | bytes 1 | tf_op jit(solution)/shard_map/input_backward/pallas_call | solution.py:309
  373.5 2.2 collective-permute-start.59
  379.6 6.8 %collective-permute-done.65.refs_7_ = bf16[64,1536]{1,0:T(8,128)(2,1)S(1)} collective-permute-done((bf16[64,1536]{1,0:T(8,128)(2,1)S(1)}, bf16[64,1536]{1,0:T(8,128)(2,1)S(1)}, u32[]{:S(2)}, u32[]{:S(2)}) %collective-permute-start.65) | collective-permute-done | bytes 196640 | tf_op jit(solution)/shard_map/ppermute | solution.py:77
  387.4 2.3 fusion.95
  391.6 3.0 collective-permute-start.66
  396.0 2.8 collective-permute-done.69
  398.7 3.0 collective-permute-done.67.refs_1_
  401.8 3.1 collective-permute-done.66
  406.9 2.4 collective-permute-start.71
  409.5 3.8 collective-permute-start.72
  (419 shorter events, 127.2 us)
Async XLA Ops:
  8.0 29.8 %collective-permute-start.4 = (bf16[256,1152]{1,0:T(8,128)(2,1)}, bf16[256,1152]{1,0:T(8,128)(2,1)}, u32[]{:S(2)}, u32[]{:S(2)}) collective-permute-start(bf16[256,1152]{1,0:T(8,128)(2,1)} %fusion.10), channel_id=1, source_target_pairs={{1,3},{3,5},{5,7},{7,9},{9,11},{11,13},{13,15},{15,17},{17,19},{19... | collective-permute-start | bytes 1769480 | tf_op jit(solution)/shard_map/ppermute | solution.py:67
  9.5 10.6 %collective-permute-start.3 = (bf16[64,2176]{1,0:T(8,128)(2,1)S(1)}, bf16[64,2176]{1,0:T(8,128)(2,1)S(1)}, u32[]{:S(2)}, u32[]{:S(2)}) collective-permute-start(bf16[64,2176]{1,0:T(8,128)(2,1)S(1)} %maximum_select_fusion.1.refs_0_), channel_id=1, source_target_pairs={{0,24},{1,25},{2,26},{3,27},{4,28},{5,29},{6,30},{7,31},{8,0},{9,1... | collective-permute-start | bytes 835592 | tf_op jit(solution)/shard_map/ppermute | solution.py:57
  14.2 23.6 %collective-permute-start.2 = (bf16[64,2176]{1,0:T(8,128)(2,1)S(1)}, bf16[64,2176]{1,0:T(8,128)(2,1)S(1)}, u32[]{:S(2)}, u32[]{:S(2)}) collective-permute-start(bf16[64,2176]{1,0:T(8,128)(2,1)S(1)} %maximum_select_fusion.1.refs_0_), channel_id=1, source_target_pairs={{0,16},{1,17},{2,18},{3,19},{4,20},{5,21},{6,22},{7,23},{8,24},{9,... | collective-permute-start | bytes 835592 | tf_op jit(solution)/shard_map/ppermute | solution.py:57
  14.2 23.6 %collective-permute-start.1 = (bf16[64,2176]{1,0:T(8,128)(2,1)S(1)}, bf16[64,2176]{1,0:T(8,128)(2,1)S(1)}, u32[]{:S(2)}, u32[]{:S(2)}) collective-permute-start(bf16[64,2176]{1,0:T(8,128)(2,1)S(1)} %maximum_select_fusion.1.refs_0_), channel_id=1, source_target_pairs={{0,8},{1,9},{2,10},{3,11},{4,12},{5,13},{6,14},{7,15},{8,16},{9,17... | collective-permute-start | bytes 835592 | tf_op jit(solution)/shard_map/ppermute | solution.py:57
  41.4 18.5 %collective-permute-start.5 = (bf16[256,2176]{1,0:T(8,128)(2,1)S(1)}, bf16[256,2176]{1,0:T(8,128)(2,1)S(1)}, u32[]{:S(2)}, u32[]{:S(2)}) collective-permute-start(bf16[256,2176]{1,0:T(8,128)(2,1)S(1)} %stack_cut.6.refs_0_), channel_id=1, source_target_pairs={{0,4},{1,3},{2,6},{3,1},{4,0},{5,7},{6,2},{7,5},{8,12},{9,11},{10,... | collective-permute-start | bytes 3342344 | tf_op jit(solution)/shard_map/ppermute | solution.py:77
  44.2 14.9 %collective-permute-start.7 = (bf16[64,1536]{1,0:T(8,128)(2,1)S(1)}, bf16[64,1536]{1,0:T(8,128)(2,1)S(1)}, u32[]{:S(2)}, u32[]{:S(2)}) collective-permute-start(bf16[64,1536]{1,0:T(8,128)(2,1)S(1)} %get-tuple-element.553), channel_id=1, source_target_pairs={{0,4},{1,3},{2,6},{3,1},{4,0},{5,7},{6,2},{7,5},{8,12},{9,11},{10,... | collective-permute-start | bytes 589832 | tf_op jit(solution)/shard_map/ppermute | solution.py:77
  45.9 14.0 %collective-permute-start.8 = (bf16[64,1792]{1,0:T(8,128)(2,1)S(1)}, bf16[64,1792]{1,0:T(8,128)(2,1)}, u32[]{:S(2)}, u32[]{:S(2)}) collective-permute-start(bf16[64,1792]{1,0:T(8,128)(2,1)S(1)} %slice.298.refs_0_), channel_id=1, source_target_pairs={{0,8},{1,9},{2,10},{3,11},{4,12},{5,13},{6,14},{7,15},{8,16},{9,17... | collective-permute-start | bytes 688136 | tf_op jit(solution)/shard_map/ppermute | solution.py:57
  62.4 17.5 %collective-permute-start.15 = (bf16[2,64,1536]{2,1,0:T(8,128)(2,1)}, bf16[2,64,1536]{2,1,0:T(8,128)(2,1)}, u32[]{:S(2)}, u32[]{:S(2)}) collective-permute-start(bf16[2,64,1536]{2,1,0:T(8,128)(2,1)} %pad_maximum_fusion.14), channel_id=1, source_target_pairs={{0,2},{1,5},{2,0},{3,7},{4,6},{5,1},{6,4},{7,3},{8,10},{9,13},{10,... | collective-permute-start | bytes 1179656 | tf_op jit(solution)/shard_map/ppermute | solution.py:77
  68.1 18.6 %collective-permute-start.16 = (bf16[256,1152]{1,0:T(8,128)(2,1)}, bf16[256,1152]{1,0:T(8,128)(2,1)}, u32[]{:S(2)}, u32[]{:S(2)}) collective-permute-start(bf16[256,1152]{1,0:T(8,128)(2,1)} %collective-permute-done.4), channel_id=1, source_target_pairs={{0,1},{1,0},{2,3},{3,2},{4,5},{5,4},{6,7},{7,6},{8,9},{9,8},{10,11... | collective-permute-start | bytes 1769480 | tf_op jit(solution)/shard_map/ppermute | solution.py:70
  68.1 20.7 %collective-permute-start.17 = (bf16[512,1152]{1,0:T(8,128)(2,1)}, bf16[512,1152]{1,0:T(8,128)(2,1)}, u32[]{:S(2)}, u32[]{:S(2)}) collective-permute-start(bf16[512,1152]{1,0:T(8,128)(2,1)} %pad_maximum_fusion.4.mine_ref), channel_id=1, source_target_pairs={{0,1},{1,0},{2,3},{3,2},{4,5},{5,4},{6,7},{7,6},{8,9},{9,8},{10,11... | collective-permute-start | bytes 3538952 | tf_op jit(solution)/shard_map/ppermute | solution.py:70
  68.6 10.6 %collective-permute-start.10 = (bf16[64,1792]{1,0:T(8,128)(2,1)}, bf16[64,1792]{1,0:T(8,128)(2,1)}, u32[]{:S(2)}, u32[]{:S(2)}) collective-permute-start(bf16[64,1792]{1,0:T(8,128)(2,1)} %collective-permute-done.8.refs_1_), channel_id=1, source_target_pairs={{0,8},{1,9},{2,10},{3,11},{4,12},{5,13},{6,14},{7,15},{8,16},{9,17... | collective-permute-start | bytes 688136 | tf_op jit(solution)/shard_map/ppermute | solution.py:57
  70.9 14.3 %collective-permute-start.13 = (bf16[64,2304]{1,0:T(8,128)(2,1)}, bf16[64,2304]{1,0:T(8,128)(2,1)}, u32[]{:S(2)}, u32[]{:S(2)}) collective-permute-start(bf16[64,2304]{1,0:T(8,128)(2,1)} %collective-permute-done.12.refs_1_), channel_id=1, source_target_pairs={{0,8},{1,9},{2,10},{3,11},{4,12},{5,13},{6,14},{7,15},{8,16},{9,17... | collective-permute-start | bytes 884744 | tf_op jit(solution)/shard_map/ppermute | solution.py:57
  79.2 27.5 %collective-permute-start.9 = (bf16[512,2176]{1,0:T(8,128)(2,1)S(1)}, bf16[512,2176]{1,0:T(8,128)(2,1)}, u32[]{:S(2)}, u32[]{:S(2)}) collective-permute-start(bf16[512,2176]{1,0:T(8,128)(2,1)S(1)} %stack_cut.7.refs_0_), channel_id=1, source_target_pairs={{0,2},{1,5},{2,0},{3,7},{4,6},{5,1},{6,4},{7,3},{8,10},{9,13},{10,... | collective-permute-start | bytes 6684680 | tf_op jit(solution)/shard_map/ppermute | solution.py:77
  79.8 21.1 %collective-permute-start.11 = (bf16[64,1792]{1,0:T(8,128)(2,1)}, bf16[64,1792]{1,0:T(8,128)(2,1)}, u32[]{:S(2)}, u32[]{:S(2)}) collective-permute-start(bf16[64,1792]{1,0:T(8,128)(2,1)} %collective-permute-done.10.refs_2_), channel_id=1, source_target_pairs={{0,8},{1,9},{2,10},{3,11},{4,12},{5,13},{6,14},{7,15},{8,16},{9,17... | collective-permute-start | bytes 688136 | tf_op jit(solution)/shard_map/ppermute | solution.py:57
  85.2 15.8 %collective-permute-start.14 = (bf16[64,2304]{1,0:T(8,128)(2,1)}, bf16[64,2304]{1,0:T(8,128)(2,1)}, u32[]{:S(2)}, u32[]{:S(2)}) collective-permute-start(bf16[64,2304]{1,0:T(8,128)(2,1)} %collective-permute-done.13.refs_2_), channel_id=1, source_target_pairs={{0,8},{1,9},{2,10},{3,11},{4,12},{5,13},{6,14},{7,15},{8,16},{9,17... | collective-permute-start | bytes 884744 | tf_op jit(solution)/shard_map/ppermute | solution.py:57
  108.1 29.2 %collective-permute-start.19 = (bf16[256,2304]{1,0:T(8,128)(2,1)S(1)}, bf16[256,2304]{1,0:T(8,128)(2,1)S(1)}, u32[]{:S(2)}, u32[]{:S(2)}) collective-permute-start(bf16[256,2304]{1,0:T(8,128)(2,1)S(1)} %stack_cut.9.refs_0_), channel_id=1, source_target_pairs={{0,4},{1,3},{2,6},{3,1},{4,0},{5,7},{6,2},{7,5},{8,12},{9,11},{10,... | collective-permute-start | bytes 3538952 | tf_op jit(solution)/shard_map/ppermute | solution.py:77
  110.2 27.1 %collective-permute-start.20 = (bf16[256,1536]{1,0:T(8,128)(2,1)S(1)}, bf16[256,1536]{1,0:T(8,128)(2,1)S(1)}, u32[]{:S(2)}, u32[]{:S(2)}) collective-permute-start(bf16[256,1536]{1,0:T(8,128)(2,1)S(1)} %bitcast.51), channel_id=1, source_target_pairs={{0,8},{1,9},{2,10},{3,11},{4,12},{5,13},{6,14},{7,15},{8,16},{9,17... | collective-permute-start | bytes 2359304 | tf_op jit(solution)/shard_map/ppermute | solution.py:57
  113.5 23.8 %collective-permute-start.18 = (bf16[256,1792]{1,0:T(8,128)(2,1)S(1)}, bf16[256,1792]{1,0:T(8,128)(2,1)S(1)}, u32[]{:S(2)}, u32[]{:S(2)}) collective-permute-start(bf16[256,1792]{1,0:T(8,128)(2,1)S(1)} %stack_cut.8.refs_0_), channel_id=1, source_target_pairs={{0,4},{1,3},{2,6},{3,1},{4,0},{5,7},{6,2},{7,5},{8,12},{9,11},{10,... | collective-permute-start | bytes 2752520 | tf_op jit(solution)/shard_map/ppermute | solution.py:77
  137.5 24.4 %collective-permute-start.21 = (bf16[512,1792]{1,0:T(8,128)(2,1)S(1)}, bf16[512,1792]{1,0:T(8,128)(2,1)S(1)}, u32[]{:S(2)}, u32[]{:S(2)}) collective-permute-start(bf16[512,1792]{1,0:T(8,128)(2,1)S(1)} %stack_cut.10.refs_0_), channel_id=1, source_target_pairs={{0,2},{1,5},{2,0},{3,7},{4,6},{5,1},{6,4},{7,3},{8,10},{9,13},{10,... | collective-permute-start | bytes 5505032 | tf_op jit(solution)/shard_map/ppermute | solution.py:77
  140.1 12.0 %collective-permute-start.22 = (bf16[512,1024]{1,0:T(8,128)(2,1)S(1)}, bf16[512,1024]{1,0:T(8,128)(2,1)S(1)}, u32[]{:S(2)}, u32[]{:S(2)}) collective-permute-start(bf16[512,1024]{1,0:T(8,128)(2,1)S(1)} %pad_maximum_fusion.6), channel_id=1, source_target_pairs={{0,1},{1,0},{2,3},{3,2},{4,5},{5,4},{6,7},{7,6},{8,9},{9,8},{10,11... | collective-permute-start | bytes 3145736 | tf_op jit(solution)/shard_map/ppermute | solution.py:70
  140.2 21.7 %collective-permute-start.23 = (bf16[256,1536]{1,0:T(8,128)(2,1)S(1)}, bf16[256,1536]{1,0:T(8,128)(2,1)S(1)}, u32[]{:S(2)}, u32[]{:S(2)}) collective-permute-start(bf16[256,1536]{1,0:T(8,128)(2,1)S(1)} %collective-permute-done.20.refs_1_), channel_id=1, source_target_pairs={{0,8},{1,9},{2,10},{3,11},{4,12},{5,13},{6,14},{7,15},{8,16},{9,17... | collective-permute-start | bytes 2359304 | tf_op jit(solution)/shard_map/ppermute | solution.py:57
  161.9 12.7 %collective-permute-start.28 = (bf16[512,768]{1,0:T(8,128)(2,1)}, bf16[512,768]{1,0:T(8,128)(2,1)}, u32[]{:S(2)}, u32[]{:S(2)}) collective-permute-start(bf16[512,768]{1,0:T(8,128)(2,1)} %get-tuple-element.324.refs_2_), channel_id=1, source_target_pairs={{0,2},{1,5},{2,0},{3,7},{4,6},{5,1},{6,4},{7,3},{8,10},{9,13},{10,... | collective-permute-start | bytes 2359304 | tf_op jit(solution)/shard_map/ppermute | solution.py:77
  170.3 22.0 %collective-permute-start.32 = (bf16[256,1536]{1,0:T(8,128)(2,1)}, bf16[256,1536]{1,0:T(8,128)(2,1)S(1)}, u32[]{:S(2)}, u32[]{:S(2)}) collective-permute-start(bf16[256,1536]{1,0:T(8,128)(2,1)} %copy-done.44), channel_id=1, source_target_pairs={{0,8},{1,9},{2,10},{3,11},{4,12},{5,13},{6,14},{7,15},{8,16},{9,17... | collective-permute-start | bytes 2359304 | tf_op jit(solution)/shard_map/ppermute | solution.py:57
  176.4 20.5 %collective-permute-start.31 = (bf16[512,1536]{1,0:T(8,128)(2,1)S(1)}, bf16[512,1536]{1,0:T(8,128)(2,1)S(1)}, u32[]{:S(2)}, u32[]{:S(2)}) collective-permute-start(bf16[512,1536]{1,0:T(8,128)(2,1)S(1)} %copy-done.28), channel_id=1, source_target_pairs={{0,2},{1,5},{2,0},{3,7},{4,6},{5,1},{6,4},{7,3},{8,10},{9,13},{10,... | collective-permute-start | bytes 4718600 | tf_op jit(solution)/shard_map/ppermute | solution.py:77
  212.7 20.4 %collective-permute-start.33 = (bf16[512,1536]{1,0:T(8,128)(2,1)S(1)}, bf16[512,1536]{1,0:T(8,128)(2,1)S(1)}, u32[]{:S(2)}, u32[]{:S(2)}) collective-permute-start(bf16[512,1536]{1,0:T(8,128)(2,1)S(1)} %get-tuple-element.350), channel_id=1, source_target_pairs={{0,2},{1,5},{2,0},{3,7},{4,6},{5,1},{6,4},{7,3},{8,10},{9,13},{10,... | collective-permute-start | bytes 4718600 | tf_op jit(solution)/shard_map/ppermute | solution.py:77
  234.2 20.4 %collective-permute-start.38 = (bf16[512,1536]{1,0:T(8,128)(2,1)S(1)}, bf16[512,1536]{1,0:T(8,128)(2,1)S(1)}, u32[]{:S(2)}, u32[]{:S(2)}) collective-permute-start(bf16[512,1536]{1,0:T(8,128)(2,1)S(1)} %get-tuple-element.357), channel_id=1, source_target_pairs={{0,2},{1,5},{2,0},{3,7},{4,6},{5,1},{6,4},{7,3},{8,10},{9,13},{10,... | collective-permute-start | bytes 4718600 | tf_op jit(solution)/shard_map/ppermute | solution.py:77
  256.3 20.5 %collective-permute-start.41 = (bf16[512,1536]{1,0:T(8,128)(2,1)S(1)}, bf16[512,1536]{1,0:T(8,128)(2,1)S(1)}, u32[]{:S(2)}, u32[]{:S(2)}) collective-permute-start(bf16[512,1536]{1,0:T(8,128)(2,1)S(1)} %get-tuple-element.370), channel_id=1, source_target_pairs={{0,2},{1,5},{2,0},{3,7},{4,6},{5,1},{6,4},{7,3},{8,10},{9,13},{10,... | collective-permute-start | bytes 4718600 | tf_op jit(solution)/shard_map/ppermute | solution.py:77
  261.6 11.1 %collective-permute-start.42 = (f32[128,1024]{1,0:T(8,128)S(1)}, f32[128,1024]{1,0:T(8,128)S(1)}, u32[]{:S(2)}, u32[]{:S(2)}) collective-permute-start(f32[128,1024]{1,0:T(8,128)S(1)} %get-tuple-element.510), channel_id=1, source_target_pairs={{0,1},{1,0},{2,3},{3,2},{4,5},{5,4},{6,7},{7,6},{8,9},{9,8},{10,11... | collective-permute-start | bytes 1572872 | tf_op jit(solution)/shard_map/ppermute | solution.py:70
  261.8 11.0 %collective-permute-start.45 = (f32[128,1024]{1,0:T(8,128)S(1)}, f32[128,1024]{1,0:T(8,128)S(1)}, u32[]{:S(2)}, u32[]{:S(2)}) collective-permute-start(f32[128,1024]{1,0:T(8,128)S(1)} %get-tuple-element.511), channel_id=1, source_target_pairs={{0,1},{1,0},{2,3},{3,2},{4,5},{5,4},{6,7},{7,6},{8,9},{9,8},{10,11... | collective-permute-start | bytes 1572872 | tf_op jit(solution)/shard_map/ppermute | solution.py:70
  262.2 10.6 %collective-permute-start.44 = (f32[128,1024]{1,0:T(8,128)S(1)}, f32[128,1024]{1,0:T(8,128)S(1)}, u32[]{:S(2)}, u32[]{:S(2)}) collective-permute-start(f32[128,1024]{1,0:T(8,128)S(1)} %get-tuple-element.512), channel_id=1, source_target_pairs={{0,1},{1,0},{2,3},{3,2},{4,5},{5,4},{6,7},{7,6},{8,9},{9,8},{10,11... | collective-permute-start | bytes 1572872 | tf_op jit(solution)/shard_map/ppermute | solution.py:70
  278.0 35.2 %collective-permute-start.46 = (bf16[256,3072]{1,0:T(8,128)(2,1)S(1)}, bf16[256,3072]{1,0:T(8,128)(2,1)S(1)}, u32[]{:S(2)}, u32[]{:S(2)}) collective-permute-start(bf16[256,3072]{1,0:T(8,128)(2,1)S(1)} %pad_maximum_fusion.5), channel_id=1, source_target_pairs={{0,4},{1,3},{2,6},{3,1},{4,0},{5,7},{6,2},{7,5},{8,12},{9,11},{10,... | collective-permute-start | bytes 4718600 | tf_op jit(solution)/shard_map/ppermute | solution.py:77
  279.9 33.2 %collective-permute-start.47 = (bf16[512,1024]{1,0:T(8,128)(2,1)S(1)}, bf16[512,1024]{1,0:T(8,128)(2,1)}, u32[]{:S(2)}, u32[]{:S(2)}) collective-permute-start(bf16[512,1024]{1,0:T(8,128)(2,1)S(1)} %get-tuple-element.390), channel_id=1, source_target_pairs={{0,2},{1,5},{2,0},{3,7},{4,6},{5,1},{6,4},{7,3},{8,10},{9,13},{10,... | collective-permute-start | bytes 3145736 | tf_op jit(solution)/shard_map/ppermute | solution.py:77
  280.7 32.4 %collective-permute-start.48 = (bf16[2,64,1536]{2,1,0:T(8,128)(2,1)}, bf16[2,64,1536]{2,1,0:T(8,128)(2,1)S(1)}, u32[]{:S(2)}, u32[]{:S(2)}) collective-permute-start(bf16[2,64,1536]{2,1,0:T(8,128)(2,1)} %get-tuple-element.393), channel_id=1, source_target_pairs={{0,24},{1,25},{2,26},{3,27},{4,28},{5,29},{6,30},{7,31},{8,0},{9,1... | collective-permute-start | bytes 1179656 | tf_op jit(solution)/shard_map/ppermute | solution.py:57
  282.5 30.6 %collective-permute-start.49 = (bf16[2,64,1536]{2,1,0:T(8,128)(2,1)}, bf16[2,64,1536]{2,1,0:T(8,128)(2,1)S(1)}, u32[]{:S(2)}, u32[]{:S(2)}) collective-permute-start(bf16[2,64,1536]{2,1,0:T(8,128)(2,1)} %get-tuple-element.394), channel_id=1, source_target_pairs={{0,8},{1,9},{2,10},{3,11},{4,12},{5,13},{6,14},{7,15},{8,16},{9,17... | collective-permute-start | bytes 1179656 | tf_op jit(solution)/shard_map/ppermute | solution.py:57
  315.2 23.1 %collective-permute-start.50 = (bf16[256,1024]{1,0:T(8,128)(2,1)S(1)}, bf16[256,1024]{1,0:T(8,128)(2,1)S(1)}, u32[]{:S(2)}, u32[]{:S(2)}) collective-permute-start(bf16[256,1024]{1,0:T(8,128)(2,1)S(1)} %add_convert_fusion.8), channel_id=1, source_target_pairs={{0,4},{1,3},{2,6},{3,1},{4,0},{5,7},{6,2},{7,5},{8,12},{9,11},{10,... | collective-permute-start | bytes 1572872 | tf_op jit(solution)/shard_map/ppermute | solution.py:77
  315.4 22.9 %collective-permute-start.52 = (bf16[256,1024]{1,0:T(8,128)(2,1)S(1)}, bf16[256,1024]{1,0:T(8,128)(2,1)S(1)}, u32[]{:S(2)}, u32[]{:S(2)}) collective-permute-start(bf16[256,1024]{1,0:T(8,128)(2,1)S(1)} %pad_maximum_fusion.12), channel_id=1, source_target_pairs={{2,0},{3,1},{4,2},{5,3},{6,4},{7,5},{8,6},{9,7},{10,8},{11,9},{12,... | collective-permute-start | bytes 1572872 | tf_op jit(solution)/shard_map/ppermute | solution.py:63
  317.9 20.3 %collective-permute-start.51 = (bf16[2,64,1536]{2,1,0:T(8,128)(2,1)S(1)}, bf16[2,64,1536]{2,1,0:T(8,128)(2,1)S(1)}, u32[]{:S(2)}, u32[]{:S(2)}) collective-permute-start(bf16[2,64,1536]{2,1,0:T(8,128)(2,1)S(1)} %add_convert_fusion.11), channel_id=1, source_target_pairs={{0,24},{1,25},{2,26},{3,27},{4,28},{5,29},{6,30},{7,31},{8,0},{9,1... | collective-permute-start | bytes 1179656 | tf_op jit(solution)/shard_map/ppermute | solution.py:57
  338.3 30.8 %collective-permute-start.53 = (bf16[512,2048]{1,0:T(8,128)(2,1)S(1)}, bf16[512,2048]{1,0:T(8,128)(2,1)S(1)}, u32[]{:S(2)}, u32[]{:S(2)}) collective-permute-start(bf16[512,2048]{1,0:T(8,128)(2,1)S(1)} %get-tuple-element.413), channel_id=1, source_target_pairs={{0,2},{1,5},{2,0},{3,7},{4,6},{5,1},{6,4},{7,3},{8,10},{9,13},{10,... | collective-permute-start | bytes 6291464 | tf_op jit(solution)/shard_map/ppermute | solution.py:77
  339.2 22.0 %collective-permute-start.55 = (bf16[64,3072]{1,0:T(8,128)(2,1)S(1)}, bf16[64,3072]{1,0:T(8,128)(2,1)S(1)}, u32[]{:S(2)}, u32[]{:S(2)}) collective-permute-start(bf16[64,3072]{1,0:T(8,128)(2,1)S(1)} %get-tuple-element.522), channel_id=1, source_target_pairs={{0,8},{1,9},{2,10},{3,11},{4,12},{5,13},{6,14},{7,15},{8,16},{9,17... | collective-permute-start | bytes 1179656 | tf_op jit(solution)/shard_map/ppermute | solution.py:57
  341.3 19.9 %collective-permute-start.54 = (bf16[64,3072]{1,0:T(8,128)(2,1)S(1)}, bf16[64,3072]{1,0:T(8,128)(2,1)S(1)}, u32[]{:S(2)}, u32[]{:S(2)}) collective-permute-start(bf16[64,3072]{1,0:T(8,128)(2,1)S(1)} %get-tuple-element.525), channel_id=1, source_target_pairs={{0,24},{1,25},{2,26},{3,27},{4,28},{5,29},{6,30},{7,31},{8,0},{9,1... | collective-permute-start | bytes 1179656 | tf_op jit(solution)/shard_map/ppermute | solution.py:57
  344.9 16.0 %collective-permute-start.57 = (bf16[64,1024]{1,0:T(8,128)(2,1)S(1)}, bf16[64,1024]{1,0:T(8,128)(2,1)S(1)}, u32[]{:S(2)}, u32[]{:S(2)}) collective-permute-start(bf16[64,1024]{1,0:T(8,128)(2,1)S(1)} %get-tuple-element.554), channel_id=1, source_target_pairs={{0,8},{1,9},{2,10},{3,11},{4,12},{5,13},{6,14},{7,15},{8,16},{9,17... | collective-permute-start | bytes 393224 | tf_op jit(solution)/shard_map/ppermute | solution.py:57
  345.1 16.1 %collective-permute-start.56 = (bf16[64,1024]{1,0:T(8,128)(2,1)S(1)}, bf16[64,1024]{1,0:T(8,128)(2,1)S(1)}, u32[]{:S(2)}, u32[]{:S(2)}) collective-permute-start(bf16[64,1024]{1,0:T(8,128)(2,1)S(1)} %get-tuple-element.555), channel_id=1, source_target_pairs={{0,24},{1,25},{2,26},{3,27},{4,28},{5,29},{6,30},{7,31},{8,0},{9,1... | collective-permute-start | bytes 393224 | tf_op jit(solution)/shard_map/ppermute | solution.py:57
  369.5 18.0 %collective-permute-start.58 = (bf16[256,2048]{1,0:T(8,128)(2,1)S(1)}, bf16[256,2048]{1,0:T(8,128)(2,1)S(1)}, u32[]{:S(2)}, u32[]{:S(2)}) collective-permute-start(bf16[256,2048]{1,0:T(8,128)(2,1)S(1)} %add_convert_fusion.2), channel_id=1, source_target_pairs={{0,4},{1,3},{2,6},{3,1},{4,0},{5,7},{6,2},{7,5},{8,12},{9,11},{10,... | collective-permute-start | bytes 3145736 | tf_op jit(solution)/shard_map/ppermute | solution.py:77
  373.5 14.0 %collective-permute-start.59 = (bf16[64,3072]{1,0:T(8,128)(2,1)S(1)}, bf16[64,3072]{1,0:T(8,128)(2,1)S(1)}, u32[]{:S(2)}, u32[]{:S(2)}) collective-permute-start(bf16[64,3072]{1,0:T(8,128)(2,1)S(1)} %add_convert_fusion.10), channel_id=1, source_target_pairs={{0,24},{1,25},{2,26},{3,27},{4,28},{5,29},{6,30},{7,31},{8,0},{9,1... | collective-permute-start | bytes 1179656 | tf_op jit(solution)/shard_map/ppermute | solution.py:57
  375.7 10.8 %collective-permute-start.65 = (bf16[64,1536]{1,0:T(8,128)(2,1)S(1)}, bf16[64,1536]{1,0:T(8,128)(2,1)S(1)}, u32[]{:S(2)}, u32[]{:S(2)}) collective-permute-start(bf16[64,1536]{1,0:T(8,128)(2,1)S(1)} %get-tuple-element.558), channel_id=1, source_target_pairs={{0,4},{1,3},{2,6},{3,1},{4,0},{5,7},{6,2},{7,5},{8,12},{9,11},{10,... | collective-permute-start | bytes 589832 | tf_op jit(solution)/shard_map/ppermute | solution.py:77
  376.2 11.2 %collective-permute-start.60 = (bf16[64,1024]{1,0:T(8,128)(2,1)S(1)}, bf16[64,1024]{1,0:T(8,128)(2,1)S(1)}, u32[]{:S(2)}, u32[]{:S(2)}) collective-permute-start(bf16[64,1024]{1,0:T(8,128)(2,1)S(1)} %add_convert_fusion.13), channel_id=1, source_target_pairs={{0,24},{1,25},{2,26},{3,27},{4,28},{5,29},{6,30},{7,31},{8,0},{9,1... | collective-permute-start | bytes 393224 | tf_op jit(solution)/shard_map/ppermute | solution.py:57
  390.5 11.3 %collective-permute-start.67 = (bf16[64,2048]{1,0:T(8,128)(2,1)S(1)}, bf16[64,2048]{1,0:T(8,128)(2,1)S(1)}, u32[]{:S(2)}, u32[]{:S(2)}) collective-permute-start(bf16[64,2048]{1,0:T(8,128)(2,1)S(1)} %get-tuple-element.532), channel_id=1, source_target_pairs={{0,8},{1,9},{2,10},{3,11},{4,12},{5,13},{6,14},{7,15},{8,16},{9,17... | collective-permute-start | bytes 786440 | tf_op jit(solution)/shard_map/ppermute | solution.py:57
  391.6 13.3 %collective-permute-start.66 = (bf16[64,2048]{1,0:T(8,128)(2,1)S(1)}, bf16[64,2048]{1,0:T(8,128)(2,1)S(1)}, u32[]{:S(2)}, u32[]{:S(2)}) collective-permute-start(bf16[64,2048]{1,0:T(8,128)(2,1)S(1)} %get-tuple-element.533), channel_id=1, source_target_pairs={{0,24},{1,25},{2,26},{3,27},{4,28},{5,29},{6,30},{7,31},{8,0},{9,1... | collective-permute-start | bytes 786440 | tf_op jit(solution)/shard_map/ppermute | solution.py:57
  (111 other events, 1123.5 us)
